TPU v7x, 128 devices: a whole 4x4x4 slice. The times are simulated.
128 devices in a mesh: ctx: 64 (over x, z, y_hi, core), ep: 2 (over y_lo).
Axes of the slice: x: 4, y: 4 (y_hi: 2, y_lo: 2; y = y_hi * 2 + y_lo), z: 4, core: 2. Of those that a mesh axis runs over, the one named last changes fastest.
Arguments:
- inputs: bfloat16 [8192, 2048], P('ctx'), may hold values from -6 to 6
- blocks: int32 [8192], P('ctx'), may hold values from 0 to 63, never falling along the last dimension, each value on 1 to 256 neighbouring positions
- expert_ids: int32 [8192, 8], P('ctx'), may hold values from 0 to 63, all different within a row; in each aligned block of 128 rows (0 to 127, 128 to 255, ...) at most 20 rows name the same one
- attention_gain: bfloat16 [2048], P('ctx'), may hold values from 0.5 to 1.5
- query_weight: bfloat16 [2048, 2048], P('ctx', 'ep'), may hold values from -0.125 to 0.125
- key_weight: bfloat16 [2048, 2048], P('ctx', 'ep'), may hold values from -0.125 to 0.125
- value_weight: bfloat16 [2048, 2048], P('ctx', 'ep'), may hold values from -0.125 to 0.125
- query_gain: bfloat16 [2048], P(('ep', 'ctx')), may hold values from 0.5 to 1.5
- key_gain: bfloat16 [2048], P(('ep', 'ctx')), may hold values from 0.5 to 1.5
- output_weight: bfloat16 [2048, 2048], P('ep', 'ctx'), may hold values from -0.5 to 0.5
- mixture_gain: bfloat16 [2048], P('ctx'), may hold values from 0.5 to 1.5
- router_weight: bfloat16 [2048, 64], P('ctx'), may hold values from -0.0625 to 0.0625
- gate_weight: bfloat16 [64, 2048, 1024], P('ctx', None, 'ep'), may hold values from -0.125 to 0.125
- up_weight: bfloat16 [64, 2048, 1024], P('ctx', None, 'ep'), may hold values from -0.125 to 0.125
- down_weight: bfloat16 [64, 1024, 2048], P('ctx', 'ep'), may hold values from -6 to 6
- cotangent: bfloat16 [8192, 2048], P('ctx'), may hold values from -6 to 6
Outputs:
- output: float32 [8192, 2048], P('ctx')
- input_grad: float32 [8192, 2048], P('ctx')
- attention_gain_grad: float32 [2048], P('ctx')
- query_weight_grad: float32 [2048, 2048], P('ctx', 'ep')
- key_weight_grad: float32 [2048, 2048], P('ctx', 'ep')
- value_weight_grad: float32 [2048, 2048], P('ctx', 'ep')
- query_gain_grad: float32 [2048], P(('ep', 'ctx'))
- key_gain_grad: float32 [2048], P(('ep', 'ctx'))
- output_weight_grad: float32 [2048, 2048], P('ep', 'ctx')
- mixture_gain_grad: float32 [2048], P('ctx')
- router_weight_grad: float32 [2048, 64], P('ctx')
- gate_weight_grad: float32 [64, 2048, 1024], P('ctx', None, 'ep')
- up_weight_grad: float32 [64, 2048, 1024], P('ctx', None, 'ep')
- down_weight_grad: float32 [64, 1024, 2048], P('ctx', 'ep')
Inputs may be any that keep to these rules, and one draw needn't show every extreme that they name: `expert_ids`: each row names 8 different experts, and every expert is named somewhere; among the 128 tokens of one index of ctx no expert is named by more than 20 rows, a bound that some expert reaches in some index. `blocks`: block numbers never fall along the sequence; each block holds 1 to 256 tokens and some block holds exactly 256.
All inputs are finite; a program needn't handle non-finite values.
Results may differ from a plain program's by a relative error of at most 0.04.
Values may be sent and summed in bfloat16 or wider, within the bound.
No kernel may reach another device: no remote copies, remote signals or barrier semaphores. Data moves between devices by JAX's collectives and lax.ppermute only.
A program may use at most 256 MiB of HBM per device.

v0:
```python
import jax
import jax.numpy as jnp
from jax import lax
from jax.sharding import PartitionSpec as P

D = 2048
H = 16
HD = 128
TOPK = 8


epsilon = 1e-05
rotary_base = 10000.0
masked_score = -1e30


def shifted_2(value, axis, steps):
    count = lax.axis_size(axis)
    pairs = [(source, (source + steps) % count) for source in range(count)]
    return lax.ppermute(value, axis, pairs)


def norm_rows(value, gain):
    inverse = lax.rsqrt(jnp.mean(value * value, axis=-1, keepdims=True) + epsilon)
    return (value * inverse * gain, inverse)


def norm_rows_back(value, inverse, gain, grad):
    scaled = grad * gain
    value_grad = inverse * scaled - value * inverse * inverse * inverse * jnp.mean(
        scaled * value, axis=-1, keepdims=True
    )
    return (value_grad, jnp.sum(grad * value * inverse, axis=0))


def rotary_tables(positions, width):
    half = width // 2
    frequency = rotary_base ** (-jnp.arange(half).astype(jnp.float32) / half)
    angles = positions.astype(jnp.float32)[:, None] * frequency[None, :]
    return (jnp.cos(angles)[:, None, :], jnp.sin(angles)[:, None, :])


def rotate(value, cosine, sine):
    half = value.shape[-1] // 2
    first = value[..., :half]
    second = value[..., half:]
    return jnp.concatenate(
        [first * cosine - second * sine, second * cosine + first * sine], axis=-1
    )


def head_sums(first, second):
    return lax.psum((first, second), "ep")


def cycle_step(first, second, third, fourth, fifth):
    return shifted_2((first, second, third, fourth, fifth), "ctx", 1)


def local(
    inputs,
    blocks,
    expert_ids,
    attention_gain,
    query_weight,
    key_weight,
    value_weight,
    query_gain,
    key_gain,
    output_weight,
    mixture_gain,
    router_weight,
    gate_weight,
    up_weight,
    down_weight,
    cotangent,
):
    count = inputs.shape[0]
    cycle = lax.axis_size("ctx")
    place = lax.axis_index("ctx")
    heads = query_weight.shape[1] // HD
    width = heads * HD
    full_width = float(H * HD)
    scale = HD ** (-0.5)
    capacity = max(2, count * TOPK * 5 // (4 * cycle))
    gathered = (
        lax.all_gather(attention_gain, "ctx", axis=0, tiled=True),
        lax.all_gather(query_gain, "ctx", axis=0, tiled=True),
        lax.all_gather(key_gain, "ctx", axis=0, tiled=True),
        lax.all_gather(query_weight, "ctx", axis=0, tiled=True),
        lax.all_gather(key_weight, "ctx", axis=0, tiled=True),
        lax.all_gather(value_weight, "ctx", axis=0, tiled=True),
        lax.all_gather(output_weight, "ctx", axis=1, tiled=True),
        lax.all_gather(mixture_gain, "ctx", axis=0, tiled=True),
        lax.all_gather(router_weight, "ctx", axis=0, tiled=True),
    )
    attention_gain_all = gathered[0].astype(jnp.float32)
    query_gain_all = gathered[1].astype(jnp.float32)
    key_gain_all = gathered[2].astype(jnp.float32)
    query_all = gathered[3]
    key_all = gathered[4]
    value_all = gathered[5]
    output_all = gathered[6]
    mixture_gain_all = gathered[7].astype(jnp.float32)
    router_all = gathered[8]
    experts = router_all.shape[1]
    source = inputs.astype(jnp.float32)
    normed, attention_inverse = norm_rows(source, attention_gain_all)
    normed_low = normed.astype(jnp.bfloat16)
    query_raw = jnp.dot(normed_low, query_all, preferred_element_type=jnp.float32)
    key_raw = jnp.dot(normed_low, key_all, preferred_element_type=jnp.float32)
    value_low = (
        jnp.dot(normed_low, value_all, preferred_element_type=jnp.float32)
        .astype(jnp.bfloat16)
        .reshape(count, heads, HD)
    )
    positions = place * count + jnp.arange(count, dtype=jnp.int32)
    cosine, sine = rotary_tables(positions, HD)
    query_square, key_square = head_sums(
        jnp.sum(query_raw * query_raw, axis=-1), jnp.sum(key_raw * key_raw, axis=-1)
    )
    query_inverse = lax.rsqrt(query_square / full_width + epsilon)[:, None]
    key_inverse = lax.rsqrt(key_square / full_width + epsilon)[:, None]
    query_normed = (query_raw * query_inverse * query_gain_all).reshape(count, heads, HD)
    key_normed = (key_raw * key_inverse * key_gain_all).reshape(count, heads, HD)
    query_low = rotate(query_normed, cosine, sine).astype(jnp.bfloat16)
    key_low = rotate(key_normed, cosine, sine).astype(jnp.bfloat16)
    block_marks = blocks.astype(jnp.bfloat16)
    query_marks = blocks.astype(jnp.float32)
    total = jnp.zeros((count, heads, HD), jnp.float32)
    peak = jnp.full((heads, count), masked_score, jnp.float32)
    key_piece = lax.all_gather(key_low, "ctx", axis=0, tiled=True)
    value_piece = lax.all_gather(value_low, "ctx", axis=0, tiled=True)
    mark_piece = lax.all_gather(block_marks, "ctx", axis=0, tiled=True)
    scores = (
        jnp.einsum("qhd,khd->hqk", query_low, key_piece, preferred_element_type=jnp.float32) * scale
    )
    visible = mark_piece.astype(jnp.float32)[None, None, :] <= query_marks[None, :, None]
    scores = jnp.where(visible, scores, masked_score)
    new_peak = jnp.maximum(peak, jnp.max(scores, axis=-1))
    weights = jnp.where(visible, jnp.exp(scores - new_peak[:, :, None]), 0.0)
    factor = jnp.exp(peak - new_peak)
    mass = jnp.sum(weights, axis=-1)
    total = total * factor.T[:, :, None] + jnp.einsum(
        "hqk,khd->qhd",
        weights.astype(jnp.bfloat16),
        value_piece,
        preferred_element_type=jnp.float32,
    )
    total, peak, mass = (total, new_peak, mass)
    attended = total / mass.T[:, :, None]
    log_mass = peak + jnp.log(mass)
    attended_low = attended.astype(jnp.bfloat16).reshape(count, width)
    attention_part = jnp.dot(attended_low, output_all, preferred_element_type=jnp.float32)
    residual = source + lax.psum(attention_part, "ep")
    mixed, mixture_inverse = norm_rows(residual, mixture_gain_all)
    mixed_low = mixed.astype(jnp.bfloat16)
    logits = jnp.dot(mixed_low, router_all, preferred_element_type=jnp.float32)
    shifted = jnp.exp(logits - jnp.max(logits, axis=-1, keepdims=True))
    probability = shifted / jnp.sum(shifted, axis=-1, keepdims=True)
    chosen = (expert_ids[:, :, None] == jnp.arange(experts, dtype=jnp.int32)[None, None, :]).astype(
        jnp.float32
    )
    gates = jnp.sum(chosen * probability[:, None, :], axis=-1)
    flat_ids = expert_ids.reshape(-1)
    indicator = (flat_ids[:, None] == jnp.arange(experts, dtype=jnp.int32)[None, :]).astype(
        jnp.int32
    )
    ranks = jnp.sum((jnp.cumsum(indicator, axis=0) - 1) * indicator, axis=1)
    row_count = count * TOPK
    slot_rows = (
        jnp.full((experts, capacity), row_count, jnp.int32)
        .at[flat_ids, ranks]
        .set(jnp.arange(row_count, dtype=jnp.int32))
    )
    slot_tokens = jnp.minimum(slot_rows // TOPK, count)
    place_rows = flat_ids * capacity + ranks
    padded = jnp.concatenate([mixed_low, jnp.zeros((1, D), jnp.bfloat16)], axis=0)
    outgoing = padded[slot_tokens]
    arrived = lax.all_to_all(outgoing, "ctx", split_axis=0, concat_axis=0, tiled=True)
    shape = arrived.shape
    flat = arrived.reshape(-1, D)
    gate = jnp.dot(flat, gate_weight[0], preferred_element_type=jnp.float32)
    upward = jnp.dot(flat, up_weight[0], preferred_element_type=jnp.float32)
    hidden = (jax.nn.silu(gate) * upward).astype(jnp.bfloat16)
    result = jnp.dot(hidden, down_weight[0], preferred_element_type=jnp.float32).astype(
        jnp.bfloat16
    )
    returned = result.reshape(shape)
    gate_kept = gate.reshape(shape[0], shape[1], -1)
    up_kept = upward.reshape(shape[0], shape[1], -1)
    back = lax.all_to_all(returned, "ctx", split_axis=0, concat_axis=0, tiled=True)
    part_rows = back.reshape(experts * capacity, D)[place_rows].reshape(count, TOPK, D)
    mixture_part = jnp.sum(gates[:, :, None] * part_rows, axis=1)
    final = residual + lax.psum(mixture_part, "ep")
    grad_out = cotangent.astype(jnp.float32)
    gate_part = jnp.sum(grad_out[:, None, :] * part_rows, axis=-1)
    piece_grads = (
        (gates[:, :, None] * grad_out[:, None, :]).astype(jnp.bfloat16).reshape(row_count, D)
    )
    padded_grad = jnp.concatenate([piece_grads, jnp.zeros((1, D), jnp.bfloat16)], axis=0)
    arrived_grad = lax.all_to_all(
        padded_grad[slot_rows], "ctx", split_axis=0, concat_axis=0, tiled=True
    )
    grad_flat = arrived_grad.reshape(-1, D)
    gate_flat = gate_kept.reshape(grad_flat.shape[0], -1)
    up_flat = up_kept.reshape(grad_flat.shape[0], -1)
    input_flat = arrived.reshape(-1, D)
    sigma = jax.nn.sigmoid(gate_flat)
    swish = gate_flat * sigma
    hidden = (swish * up_flat).astype(jnp.bfloat16)
    down_weight_grad = jnp.einsum(
        "rf,rd->fd", hidden, grad_flat, preferred_element_type=jnp.float32
    )
    hidden_grad = jnp.einsum(
        "rd,fd->rf", grad_flat, down_weight[0], preferred_element_type=jnp.float32
    )
    gate_raw_grad = (hidden_grad * up_flat * sigma * (1.0 + gate_flat * (1.0 - sigma))).astype(
        jnp.bfloat16
    )
    up_raw_grad = (hidden_grad * swish).astype(jnp.bfloat16)
    gate_weight_grad = jnp.einsum(
        "rd,rf->df", input_flat, gate_raw_grad, preferred_element_type=jnp.float32
    )
    up_weight_grad = jnp.einsum(
        "rd,rf->df", input_flat, up_raw_grad, preferred_element_type=jnp.float32
    )
    entry_grad = jnp.einsum(
        "rf,df->rd", gate_raw_grad, gate_weight[0], preferred_element_type=jnp.float32
    )
    entry_grad = entry_grad + jnp.einsum(
        "rf,df->rd", up_raw_grad, up_weight[0], preferred_element_type=jnp.float32
    )
    entry_low = entry_grad.astype(jnp.bfloat16).reshape(arrived_grad.shape)
    returned_grad = lax.all_to_all(entry_low, "ctx", split_axis=0, concat_axis=0, tiled=True)
    entry_rows = returned_grad.reshape(experts * capacity, D)[place_rows].reshape(count, TOPK, D)
    mixed_part = jnp.sum(entry_rows, axis=1, dtype=jnp.float32)
    mixed_grad_experts, gate_grad = lax.psum((mixed_part, gate_part), "ep")
    probability_grad = jnp.sum(chosen * gate_grad[:, :, None], axis=1)
    logit_grad = (
        probability
        * (probability_grad - jnp.sum(probability * probability_grad, axis=-1, keepdims=True))
    ).astype(jnp.bfloat16)
    router_grad = jnp.einsum("td,te->de", mixed_low, logit_grad, preferred_element_type=jnp.float32)
    mixed_grad = mixed_grad_experts + jnp.einsum(
        "te,de->td", logit_grad, router_all, preferred_element_type=jnp.float32
    )
    residual_norm_grad, mixture_gain_grad = norm_rows_back(
        residual, mixture_inverse, mixture_gain_all, mixed_grad
    )
    residual_grad = grad_out + residual_norm_grad
    residual_low = residual_grad.astype(jnp.bfloat16)
    output_grad = jnp.einsum(
        "tc,td->cd", attended_low, residual_low, preferred_element_type=jnp.float32
    )
    attended_grad = (
        jnp.einsum("td,cd->tc", residual_low, output_all, preferred_element_type=jnp.float32)
        .astype(jnp.bfloat16)
        .reshape(count, heads, HD)
    )
    delta = jnp.sum(attended_grad * attended, axis=-1)
    empty_rows = jnp.zeros((count, heads, HD), jnp.float32)

    def pair_grads(
        query_piece,
        grad_piece,
        log_piece,
        delta_piece,
        query_mark,
        key_piece,
        value_piece,
        key_mark,
    ):
        scores = (
            jnp.einsum("qhd,khd->hqk", query_piece, key_piece, preferred_element_type=jnp.float32)
            * scale
        )
        visible = key_mark[None, None, :] <= query_mark[None, :, None]
        chances = jnp.exp(jnp.where(visible, scores, masked_score) - log_piece[:, :, None])
        value_dot = jnp.einsum(
            "qhd,khd->hqk", grad_piece, value_piece, preferred_element_type=jnp.float32
        )
        score_grad = (scale * chances * (value_dot - delta_piece[:, :, None])).astype(jnp.bfloat16)
        query_term = jnp.einsum(
            "hqk,khd->qhd", score_grad, key_piece, preferred_element_type=jnp.float32
        )
        key_term = jnp.einsum(
            "hqk,qhd->khd", score_grad, query_piece, preferred_element_type=jnp.float32
        )
        value_term = jnp.einsum(
            "hqk,qhd->khd",
            chances.astype(jnp.bfloat16),
            grad_piece,
            preferred_element_type=jnp.float32,
        )
        return (query_term, key_term, value_term)

    def carry_turn(state):
        query_sum, travel = state
        key_moving, value_moving, mark_moving, key_sum, value_sum = travel
        query_term, key_term, value_term = pair_grads(
            query_low,
            attended_grad,
            log_mass,
            delta.T,
            query_marks,
            key_moving.astype(jnp.bfloat16),
            value_moving.astype(jnp.bfloat16),
            mark_moving,
        )
        travel = cycle_step(
            key_moving, value_moving, mark_moving, key_sum + key_term, value_sum + value_term
        )
        return (query_sum + query_term, travel)

    def carry_block(index, state):
        for repeat in range(4):
            state = carry_turn(state)
        return state

    carry_start = (
        empty_rows,
        (
            key_low.astype(jnp.float32),
            value_low.astype(jnp.float32),
            query_marks,
            empty_rows,
            empty_rows,
        ),
    )
    query_grad, finished = lax.fori_loop(0, cycle // 4, carry_block, carry_start)
    key_grad = finished[3]
    value_grad = finished[4]
    value_grad_low = value_grad.astype(jnp.bfloat16).reshape(count, width)
    query_normed_grad = rotate(query_grad, cosine, -sine).reshape(count, width)
    key_normed_grad = rotate(key_grad, cosine, -sine).reshape(count, width)
    query_scaled = query_normed_grad * query_gain_all
    key_scaled = key_normed_grad * key_gain_all
    query_dot, key_dot = head_sums(
        jnp.sum(query_scaled * query_raw, axis=-1), jnp.sum(key_scaled * key_raw, axis=-1)
    )
    query_raw_grad = (
        query_inverse * query_scaled
        - query_raw
        * query_inverse
        * query_inverse
        * query_inverse
        * (query_dot / full_width)[:, None]
    )
    key_raw_grad = (
        key_inverse * key_scaled
        - key_raw * key_inverse * key_inverse * key_inverse * (key_dot / full_width)[:, None]
    )
    query_gain_grad = jnp.sum(query_normed_grad * query_raw * query_inverse, axis=0)
    key_gain_grad = jnp.sum(key_normed_grad * key_raw * key_inverse, axis=0)
    query_raw_low = query_raw_grad.astype(jnp.bfloat16)
    key_raw_low = key_raw_grad.astype(jnp.bfloat16)
    query_weight_grad = jnp.einsum(
        "td,tc->dc", normed_low, query_raw_low, preferred_element_type=jnp.float32
    )
    key_weight_grad = jnp.einsum(
        "td,tc->dc", normed_low, key_raw_low, preferred_element_type=jnp.float32
    )
    value_weight_grad = jnp.einsum(
        "td,tc->dc", normed_low, value_grad_low, preferred_element_type=jnp.float32
    )
    normed_part = jnp.einsum(
        "tc,dc->td", query_raw_low, query_all, preferred_element_type=jnp.float32
    )
    normed_part = normed_part + jnp.einsum(
        "tc,dc->td", key_raw_low, key_all, preferred_element_type=jnp.float32
    )
    normed_part = normed_part + jnp.einsum(
        "tc,dc->td", value_grad_low, value_all, preferred_element_type=jnp.float32
    )
    normed_grad = lax.psum(normed_part, "ep")
    source_grad, attention_gain_grad = norm_rows_back(
        source, attention_inverse, attention_gain_all, normed_grad
    )
    input_grad = residual_grad + source_grad
    sums = (
        lax.psum_scatter(attention_gain_grad, "ctx", scatter_dimension=0, tiled=True),
        lax.psum_scatter(query_weight_grad, "ctx", scatter_dimension=0, tiled=True),
        lax.psum_scatter(key_weight_grad, "ctx", scatter_dimension=0, tiled=True),
        lax.psum_scatter(value_weight_grad, "ctx", scatter_dimension=0, tiled=True),
        lax.psum_scatter(query_gain_grad, "ctx", scatter_dimension=0, tiled=True),
        lax.psum_scatter(key_gain_grad, "ctx", scatter_dimension=0, tiled=True),
        lax.psum_scatter(output_grad, "ctx", scatter_dimension=1, tiled=True),
        lax.psum_scatter(mixture_gain_grad, "ctx", scatter_dimension=0, tiled=True),
        lax.psum_scatter(router_grad, "ctx", scatter_dimension=0, tiled=True),
    )
    return (
        final,
        input_grad,
        sums[0],
        sums[1],
        sums[2],
        sums[3],
        sums[4],
        sums[5],
        sums[6],
        sums[7],
        sums[8],
        gate_weight_grad[None],
        up_weight_grad[None],
        down_weight_grad[None],
    )


def solution(mesh):
    in_specs = (
        P("ctx", None),
        P("ctx"),
        P("ctx", None),
        P("ctx"),
        P("ctx", "ep"),
        P("ctx", "ep"),
        P("ctx", "ep"),
        P(("ep", "ctx")),
        P(("ep", "ctx")),
        P("ep", "ctx"),
        P("ctx"),
        P("ctx", None),
        P("ctx", None, "ep"),
        P("ctx", None, "ep"),
        P("ctx", "ep", None),
        P("ctx", None),
    )
    out_specs = (
        P("ctx", None),
        P("ctx", None),
        P("ctx"),
        P("ctx", "ep"),
        P("ctx", "ep"),
        P("ctx", "ep"),
        P(("ep", "ctx")),
        P(("ep", "ctx")),
        P("ep", "ctx"),
        P("ctx"),
        P("ctx", None),
        P("ctx", None, "ep"),
        P("ctx", None, "ep"),
        P("ctx", "ep", None),
    )
    return jax.shard_map(local, mesh=mesh, in_specs=in_specs, out_specs=out_specs, check_vma=False)
```

profile of v0, /device:TPU:96, one launch (start us, length us, event | category | flops | bytes accessed | tf_op | source)
XLA Modules:
  0.0 4707.4 jit_solution(746399637858164227)
XLA Ops:
  15.5 293.8 %all-reduce.14 = (bf16[2048]{0:T(1024)(128)(2,1)S(1)}, bf16[1024]{0:T(1024)(128)(2,1)S(1)}, bf16[1024]{0:T(1024)(128)(2,1)S(1)}, bf16[2048]{0:T(1024)(128)(2,1)S(1)}) all-reduce(bf16[2048]{0:T(1024)(128)(2,1)S(1)} %dynamic-update-slice, bf16[1024]{0:T(1024)(128)(2,1)S(1)} %dynamic-update-slice.1, ...), channel_id=1, replica_groups=mesh['ctx'=64,'ep'=2] {'ctx'}, use_global_device_ids=true, to_apply=%add.2 | all-reduce | flops 6144 | bytes 24576
  333.1 113.0 %all-gather = bf16[64,1,128]{2,1,0:T(2,128)(2,1)S(1)} all-gather(bf16[1,1,128]{2,1,0:T(2,128)(2,1)S(1)} %get-tuple-element.278), channel_id=1, replica_groups=mesh['ctx'=64,'ep'=2] {'ctx'}, dimensions={0}, use_global_device_ids=true | all-gather | bytes 16640 | tf_op jit(solution)/shard_map/all_gather | solution.py:134
  446.9 31.2 reduce-window.6
  483.4 18.3 fusion.56
  501.7 16.1 fusion.57
  518.3 55.6 %all-gather.16.cloned.1.call-done = bf16[8192,8,128]{0,2,1:T(8,128)(2,1)} async-done(((bf16[128,8,128]{0,2,1:T(8,128)(2,1)}), bf16[8192,8,128]{0,2,1:T(8,128)(2,1)}) %all-gather.16.cloned.1.call-update) | async-done | bytes 16777232 | tf_op jit(solution)/shard_map/all_gather | solution.py:133
  573.9 20.4 fusion.133
  594.4 53.1 %all-gather.18.cloned.1.call-done = bf16[1024,2048]{0,1:T(8,128)(2,1)} async-done(((bf16[1024,32]{0,1:T(8,128)(2,1)}), bf16[1024,2048]{0,1:T(8,128)(2,1)}) %all-gather.18.cloned.1.call-update) | async-done | bytes 4194320 | tf_op jit(solution)/shard_map/all_gather | solution.py:93
  657.4 40.5 all-reduce.19.cloned.1.call-done
  728.0 154.5 %all_gather.47 = bf16[2048,64]{1,0:T(8,128)(2,1)S(1)} all-gather(bf16[32,64]{1,0:T(8,128)(2,1)S(1)} %copy-done.52), channel_id=1, replica_groups=mesh['ctx'=64,'ep'=2] {'ctx'}, dimensions={0}, use_global_device_ids=true | all-gather | bytes 266240 | tf_op jit(solution)/shard_map/all_gather | solution.py:95
  888.1 13.6 gather_fusion.2
  910.6 18.5 all-to-all-start.2
  950.1 54.5 %all-to-all-done.2 = bf16[64,20,2048]{2,1,0:T(8,128)(2,1)} async-done(((bf16[64,20,2048]{2,1,0:T(8,128)(2,1)}), bf16[64,20,2048]{2,1,0:T(8,128)(2,1)}, u32[]{:S(2)}, u32[]{:S(2)}) %all-to-all-start.2) | async-done | bytes 5242912 | tf_op jit(solution)/shard_map/all_to_all | solution.py:202
  1038.7 20.1 all-to-all-start.3
  1073.6 60.6 %all-to-all-done.3 = bf16[64,20,2048]{2,1,0:T(8,128)(2,1)} async-done(((bf16[64,20,2048]{2,1,0:T(8,128)(2,1)}), bf16[64,20,2048]{2,1,0:T(8,128)(2,1)}, u32[]{:S(2)}, u32[]{:S(2)}) %all-to-all-start.3) | async-done | bytes 5242912 | tf_op jit(solution)/shard_map/all_to_all | solution.py:235
  1134.3 18.7 all-to-all-start.1
  1182.1 53.3 %all-to-all-done.1 = bf16[64,20,2048]{2,1,0:T(8,128)(2,1)} async-done(((bf16[64,20,2048]{2,1,0:T(8,128)(2,1)}), bf16[64,20,2048]{2,1,0:T(8,128)(2,1)}, u32[]{:S(2)}, u32[]{:S(2)}) %all-to-all-start.1) | async-done | bytes 5242912 | tf_op jit(solution)/shard_map/all_to_all | solution.py:192
  1274.7 1576.2 %while.21 = (s32[]{:T(128)}, f32[128,8,128]{2,0,1:T(8,128)}, bf16[128,8,128]{2,0,1:T(8,128)(2,1)}, bf16[128,8,128]{2,0,1:T(8,128)(2,1)}, f32[128]{0:T(128)}, /*i...) while((s32[]{:T(128)}, f32[128,8,128]{2,0,1:T(8,128)}, ...), condition=%wide.region_27.28_spmd.clone, body=%wide.region_26.27_spmd.clone.sunk | while | flops 677838848 | bytes 58957256 | solution.py:331
  2912.0 113.7 %all-reduce.23.cloned.1.call-done = (f32[128,2048]{1,0:T(8,128)}, f32[128,2048]{1,0:T(8,128)}) async-done(((f32[128,2048]{1,0:T(8,128)}, f32[128,2048]{1,0:T(8,128)}), (f32[128,2048]{1,0:T(8,128)}, f32[128,2048]{1,0:T(8,128)})) %all-reduce.23.cloned.1.call-update) | async-done | bytes 2097168 | tf_op jit(solution)/shard_map/psum | solution.py:195
  3027.4 292.4 %all-reduce.10 = (f32[2048]{0:T(1024)S(1)}, f32[1024]{0:T(1024)S(1)}, f32[1024]{0:T(1024)S(1)}, f32[2048]{0:T(1024)S(1)}) all-reduce(f32[2048]{0:T(1024)S(1)} %get-tuple-element.196, f32[1024]{0:T(1024)S(1)} %get-tuple-element.200, f32[1024]{0:T(1024)S(1)} %get-tuple-element.198, ...), channel_id=2, replica_groups=mesh['ctx'=64,'ep'=2] {'ctx'}, use_global_device_ids=true, to_apply=%region_35.36.clone | all-reduce | flops 6144 | bytes 49152
  3327.7 341.7 %reduce-scatter.12.cloned.1.call-done = f32[1024,32]{0,1:T(8,128)} async-done(((f32[1024,2048]{0,1:T(8,128)}), f32[1024,32]{0,1:T(8,128)}) %reduce-scatter.12.cloned.1.call-update) | async-done | bytes 131088 | tf_op jit(solution)/shard_map/reduce_scatter | solution.py:388
  3669.4 343.8 %reduce-scatter.8.cloned.1.call-done = f32[32,1024]{1,0:T(8,128)} async-done(((f32[2048,1024]{1,0:T(8,128)}), f32[32,1024]{1,0:T(8,128)}) %reduce-scatter.8.cloned.1.call-update) | async-done | bytes 131088 | tf_op jit(solution)/shard_map/reduce_scatter | solution.py:384
  4013.2 343.8 %reduce-scatter.6.cloned.1.call-done = f32[32,1024]{1,0:T(8,128)} async-done(((f32[2048,1024]{1,0:T(8,128)}), f32[32,1024]{1,0:T(8,128)}) %reduce-scatter.6.cloned.1.call-update) | async-done | bytes 131088 | tf_op jit(solution)/shard_map/reduce_scatter | solution.py:383
  4356.9 343.6 %reduce-scatter.10.cloned.1.call-done = f32[32,1024]{1,0:T(8,128)} async-done(((f32[2048,1024]{1,0:T(8,128)}), f32[32,1024]{1,0:T(8,128)}) %reduce-scatter.10.cloned.1.call-update) | async-done | bytes 131088 | tf_op jit(solution)/shard_map/reduce_scatter | solution.py:385
  (1357 shorter events, 1871.6 us)
Async XLA Ops:
  7.2 304.3 %all-gather.8.cloned.1.call-start = ((), (), s32[]{:S(2)}) async-start(), calls=%async_computation.9 | async-start | bytes 4259840 | tf_op jit(solution)/shard_map/all_gather | solution.py:90
  7.9 306.8 %all-gather.10.cloned.1.call-start = ((), (), s32[]{:S(2)}) async-start(), calls=%async_computation.10 | async-start | bytes 4259840 | tf_op jit(solution)/shard_map/all_gather | solution.py:91
  8.7 318.3 %all-gather.14.cloned.1.call-start = ((), (), s32[]{:S(2)}) async-start(), calls=%async_computation.12 | async-start | bytes 4259840 | tf_op jit(solution)/shard_map/all_gather | solution.py:92
  9.4 473.9 %all-gather.12.cloned.1.call-start = ((), (), s32[]{:S(2)}) async-start(), calls=%async_computation.11 | async-start | bytes 17039360 | tf_op jit(solution)/shard_map/all_gather | solution.py:132
  326.9 247.0 %all-gather.16.cloned.1.call-start = ((), (), s32[]{:S(2)}) async-start(), calls=%async_computation.13 | async-start | bytes 17039360 | tf_op jit(solution)/shard_map/all_gather | solution.py:133
  331.7 315.8 %all-gather.18.cloned.1.call-start = ((), (), s32[]{:S(2)}) async-start(), calls=%async_computation.14 | async-start | bytes 4259840 | tf_op jit(solution)/shard_map/all_gather | solution.py:93
  332.3 365.6 %all-reduce.19.cloned.1.call-start = ((), (), s32[]{:S(2)}) async-start(), calls=%async_computation.15 | async-start | bytes 2097152 | tf_op jit(solution)/shard_map/psum | solution.py:155
  716.5 194.1 %all-to-all-start = ((bf16[64,20,2048]{2,1,0:T(8,128)(2,1)}), bf16[64,20,2048]{2,1,0:T(8,128)(2,1)}, u32[]{:S(2)}, u32[]{:S(2)}) async-start(bf16[64,20,2048]{2,1,0:T(8,128)(2,1)} %reshape.480), calls=%async_computation | async-start | bytes 12582912 | tf_op jit(solution)/shard_map/all_to_all | solution.py:180
  910.6 94.0 %all-to-all-start.2 = ((bf16[64,20,2048]{2,1,0:T(8,128)(2,1)}), bf16[64,20,2048]{2,1,0:T(8,128)(2,1)}, u32[]{:S(2)}, u32[]{:S(2)}) async-start(bf16[64,20,2048]{2,1,0:T(8,128)(2,1)} %reshape.496), calls=%async_computation.2 | async-start | bytes 12582912 | tf_op jit(solution)/shard_map/all_to_all | solution.py:202
  1038.7 95.6 %all-to-all-start.3 = ((bf16[64,20,2048]{2,1,0:T(8,128)(2,1)}), bf16[64,20,2048]{2,1,0:T(8,128)(2,1)}, u32[]{:S(2)}, u32[]{:S(2)}) async-start(bf16[64,20,2048]{2,1,0:T(8,128)(2,1)} %reshape.467), calls=%async_computation.3 | async-start | bytes 12582912 | tf_op jit(solution)/shard_map/all_to_all | solution.py:235
  1134.3 101.2 %all-to-all-start.1 = ((bf16[64,20,2048]{2,1,0:T(8,128)(2,1)}), bf16[64,20,2048]{2,1,0:T(8,128)(2,1)}, u32[]{:S(2)}, u32[]{:S(2)}) async-start(bf16[64,20,2048]{2,1,0:T(8,128)(2,1)} %reshape.464), calls=%async_computation.1 | async-start | bytes 12582912 | tf_op jit(solution)/shard_map/all_to_all | solution.py:192
  1153.0 117.8 %all-reduce.21.cloned.1.call-start = ((), (), s32[]{:S(2)}) async-start(), calls=%async_computation.16 | async-start | bytes 2097152 | tf_op jit(solution)/shard_map/psum | solution.py:238
  1181.3 1844.5 %all-reduce.23.cloned.1.call-start = ((), (), s32[]{:S(2)}) async-start(), calls=%async_computation.22 | async-start | bytes 4194304 | tf_op jit(solution)/shard_map/psum | solution.py:195
  1307.1 54.8 %collective-permute-start.11 = (f32[128]{0:T(128)}, f32[128]{0:T(128)}, u32[]{:S(2)}, u32[]{:S(2)}) collective-permute-start(f32[128]{0:T(128)} %collective-permute-done.2), channel_id=1, source_target_pairs={{0,2},{2,4},{4,6},{6,8},{8,10},{10,12},{12,14},{14,16},{16,18},{18... | collective-permute-start | bytes 1544 | tf_op jit(solution)/shard_map/while/body/eval_jaxpr/ppermute | solution.py:20
  1405.3 54.8 %collective-permute-start.11 = (f32[128]{0:T(128)}, f32[128]{0:T(128)}, u32[]{:S(2)}, u32[]{:S(2)}) collective-permute-start(f32[128]{0:T(128)} %collective-permute-done.2), channel_id=1, source_target_pairs={{0,2},{2,4},{4,6},{6,8},{8,10},{10,12},{12,14},{14,16},{16,18},{18... | collective-permute-start | bytes 1544 | tf_op jit(solution)/shard_map/while/body/eval_jaxpr/ppermute | solution.py:20
  1503.6 54.8 %collective-permute-start.11 = (f32[128]{0:T(128)}, f32[128]{0:T(128)}, u32[]{:S(2)}, u32[]{:S(2)}) collective-permute-start(f32[128]{0:T(128)} %collective-permute-done.2), channel_id=1, source_target_pairs={{0,2},{2,4},{4,6},{6,8},{8,10},{10,12},{12,14},{14,16},{16,18},{18... | collective-permute-start | bytes 1544 | tf_op jit(solution)/shard_map/while/body/eval_jaxpr/ppermute | solution.py:20
  1601.9 54.8 %collective-permute-start.11 = (f32[128]{0:T(128)}, f32[128]{0:T(128)}, u32[]{:S(2)}, u32[]{:S(2)}) collective-permute-start(f32[128]{0:T(128)} %collective-permute-done.2), channel_id=1, source_target_pairs={{0,2},{2,4},{4,6},{6,8},{8,10},{10,12},{12,14},{14,16},{16,18},{18... | collective-permute-start | bytes 1544 | tf_op jit(solution)/shard_map/while/body/eval_jaxpr/ppermute | solution.py:20
  1700.1 54.8 %collective-permute-start.11 = (f32[128]{0:T(128)}, f32[128]{0:T(128)}, u32[]{:S(2)}, u32[]{:S(2)}) collective-permute-start(f32[128]{0:T(128)} %collective-permute-done.2), channel_id=1, source_target_pairs={{0,2},{2,4},{4,6},{6,8},{8,10},{10,12},{12,14},{14,16},{16,18},{18... | collective-permute-start | bytes 1544 | tf_op jit(solution)/shard_map/while/body/eval_jaxpr/ppermute | solution.py:20
  1798.4 54.8 %collective-permute-start.11 = (f32[128]{0:T(128)}, f32[128]{0:T(128)}, u32[]{:S(2)}, u32[]{:S(2)}) collective-permute-start(f32[128]{0:T(128)} %collective-permute-done.2), channel_id=1, source_target_pairs={{0,2},{2,4},{4,6},{6,8},{8,10},{10,12},{12,14},{14,16},{16,18},{18... | collective-permute-start | bytes 1544 | tf_op jit(solution)/shard_map/while/body/eval_jaxpr/ppermute | solution.py:20
  2869.5 458.2 %reduce-scatter.14.cloned.1.call-start = ((), (), s32[]{:S(2)}) async-start(), calls=%async_computation.21 | async-start | bytes 1064960 | tf_op jit(solution)/shard_map/reduce_scatter | solution.py:390
  2871.0 798.4 %reduce-scatter.12.cloned.1.call-start = ((), (), s32[]{:S(2)}) async-start(), calls=%async_computation.20 | async-start | bytes 8519680 | tf_op jit(solution)/shard_map/reduce_scatter | solution.py:388
  2875.6 1137.5 %reduce-scatter.8.cloned.1.call-start = ((), (), s32[]{:S(2)}) async-start(), calls=%async_computation.18 | async-start | bytes 8519680 | tf_op jit(solution)/shard_map/reduce_scatter | solution.py:384
  2881.4 1475.5 %reduce-scatter.6.cloned.1.call-start = ((), (), s32[]{:S(2)}) async-start(), calls=%async_computation.17 | async-start | bytes 8519680 | tf_op jit(solution)/shard_map/reduce_scatter | solution.py:383
  2887.0 1813.6 %reduce-scatter.10.cloned.1.call-start = ((), (), s32[]{:S(2)}) async-start(), calls=%async_computation.19 | async-start | bytes 8519680 | tf_op jit(solution)/shard_map/reduce_scatter | solution.py:385
  (398 other events, 12358.0 us)
Sparse Core Ops, SparseCore 0:
  11.2 71.3 all-gather.7
  85.7 68.9 all-gather.9
  157.9 69.0 all-gather.13
  327.1 135.1 all-gather.11
  465.8 108.0 all-gather.15
  576.9 70.5 all-gather.17
  652.3 45.5 all-reduce.18
  1181.4 88.2 all-reduce.20
  2869.7 156.0 all-reduce.22
  3028.7 296.5 reduce-scatter.13
  3328.2 341.0 reduce-scatter.11
  3672.2 340.9 reduce-scatter.7
  4016.1 340.7 reduce-scatter.5
  4359.7 340.7 reduce-scatter.9
where the time goes:
time: 4760 us; the launch traced here: 4710 us
  waiting for transfers between devices  2350 us (49%)
  starting transfers between devices  909 us (19%)
  blocking collectives  872 us (18%)
  matrix products  313 us (7%)
  local copies, waits for them, and re-layouts  143 us (3%)
  other arithmetic  100 us (2%)
    ppermute x320, starting transfers between devices, shifted_2(): return lax.ppermute(value, axis, pairs)  841 us
    unnamed x2, blocking collectives  586 us
    ppermute x320, waiting for transfers between devices, shifted_2(): return lax.ppermute(value, axis, pairs)  542 us
    reduce_scatter x1, waiting for transfers between devices, local(): lax.psum_scatter(query_weight_grad, 'ctx', scatter_dimension=0, tiled=True)  344 us
    reduce_scatter x1, waiting for transfers between devices, local(): lax.psum_scatter(key_weight_grad, 'ctx', scatter_dimension=0, tiled=True)  344 us
    reduce_scatter x1, waiting for transfers between devices, local(): lax.psum_scatter(value_weight_grad, 'ctx', scatter_dimension=0, tiled=True)  344 us
    reduce_scatter x1, waiting for transfers between devices, local(): lax.psum_scatter(output_grad, 'ctx', scatter_dimension=1, tiled=True)  342 us
    all_gather x1, blocking collectives, local(): lax.all_gather(router_weight, 'ctx', axis=0, tiled=True)  154 us
  transfers between devices with their start and end apart: 338, of which 193 were waited for; matrix products, arithmetic and copies ran while one was open for 10% of the time, Pallas kernels for 0%

commit v1 on v0

v1 whole, which is shorter than its diff:
```python
import functools

import jax
import jax.numpy as jnp
from jax import lax
from jax.experimental import pallas as pl
from jax.experimental.pallas import tpu as pltpu
from jax.sharding import Mesh
from jax.sharding import PartitionSpec as P

D = 2048
H = 16
HD = 128
TOPK = 8
CAP = 20
MAIN = 16
REST = CAP - MAIN
QUARTERS = 4
BAND = D // QUARTERS
WINDOW = 512

epsilon = 1e-05
rotary_base = 10000.0
masked_score = -1e30
scale = HD ** (-0.5)
log2e = 1.4426950408889634
bf16 = jnp.bfloat16
f32 = jnp.float32

CTX = ("x", "z", "yh", "c")
HEADS = ("x", "yh")
TOKENS = ("z", "c")
ROWS = ("x", "yh", "ep")


def dot(first, second, dims=((1,), (0,))):
    return lax.dot_general(first, second, (dims, ((), ())), preferred_element_type=f32)


def exchange(value, axes):
    return lax.all_to_all(value, axes, split_axis=0, concat_axis=0, tiled=True)


def pair_sum(value):
    own = lax.optimization_barrier(value.astype(bf16))
    other = lax.ppermute(own, "ep", [(0, 1), (1, 0)])
    return own.astype(f32) + other.astype(f32)


def sum_over_rows(value):
    rows = value.shape[0]
    sent = jnp.broadcast_to(value[None], (16, rows, 128)).reshape(16 * rows, 128)
    return jnp.sum(exchange(sent, ROWS).reshape(16, rows, 128), axis=0)


def rotary_tables(positions):
    half = HD // 2
    frequency = rotary_base ** (-jnp.arange(half).astype(f32) / half)
    angles = positions.astype(f32)[:, None] * frequency[None, :]
    return (jnp.cos(angles), jnp.sin(angles))


def rotate(value, cosine, sine):
    half = HD // 2
    first = value[:, :half]
    second = value[:, half:]
    return jnp.concatenate(
        [first * cosine - second * sine, second * cosine + first * sine], axis=-1
    )


def window_rows(index):
    return pl.multiple_of((index % 4) * 2048 + (index // 4) * 256, 256)


def window_mask(index, end):
    row = lax.broadcasted_iota(jnp.int32, (WINDOW, 1), 0)
    place = (row & 127) + ((row >> 7) & 1) * 256 + (row >> 8) * 128 + index * WINDOW
    return place < end


def attend_kernel(z_ref, q_ref, kv_ref, end_ref, out_ref, lse_ref):
    z = z_ref[0]
    factor = scale * log2e
    for x in range(4):
        span = slice(x * 256, (x + 1) * 256)
        queries = q_ref[span, :]
        end = end_ref[:, span]

        def tile(index, state, masked):
            peak, mass, total = state
            base = window_rows(index)
            part = jnp.concatenate(
                [kv_ref[pl.ds(base, 256), :], kv_ref[pl.ds(base + 1024, 256), :]], axis=0
            )
            keys, values = part[:, :HD], part[:, HD:]
            scores = dot(keys, queries, ((1,), (1,)))
            if masked:
                scores = jnp.where(window_mask(index, end), scores, masked_score)
            new_peak = jnp.maximum(peak, jnp.max(scores, axis=0, keepdims=True))
            weights = jnp.exp2((scores - new_peak) * factor)
            shrink = jnp.exp2((peak - new_peak) * factor)
            mass = mass * shrink + jnp.sum(weights, axis=0, keepdims=True)
            total = total * shrink + dot(values, weights.astype(bf16), ((0,), (0,)))
            return (new_peak, mass, total)

        state = (
            jnp.full((1, 256), masked_score, f32),
            jnp.zeros((1, 256), f32),
            jnp.zeros((HD, 256), f32),
        )
        last = 4 * x + z
        state = lax.fori_loop(0, last, lambda i, s: tile(i, s, False), state)
        state = lax.fori_loop(
            last, jnp.minimum(last + 2, 16), lambda i, s: tile(i, s, True), state
        )
        peak, mass, total = state
        out_ref[span, :] = (total / mass).T
        lse_ref[:, span] = peak * factor + jnp.log(mass) * log2e


def attend_back_kernel(
    z_ref, q_ref, grad_ref, kv_ref, end_ref, lse_ref, delta_ref, dq_ref, dkv_ref, sums
):
    z = z_ref[0]
    factor = scale * log2e
    sums[...] = jnp.zeros_like(sums)
    for x in range(4):
        span = slice(x * 256, (x + 1) * 256)
        queries = q_ref[span, :]
        grads = grad_ref[span, :]
        end = end_ref[:, span]
        lse = lse_ref[:, span]
        delta = delta_ref[:, span]

        def tile(index, total, masked):
            base = window_rows(index)
            part = jnp.concatenate(
                [kv_ref[pl.ds(base, 256), :], kv_ref[pl.ds(base + 1024, 256), :]], axis=0
            )
            keys, values = part[:, :HD], part[:, HD:]
            scores = dot(keys, queries, ((1,), (1,))) * factor - lse
            if masked:
                scores = jnp.where(window_mask(index, end), scores, masked_score)
            chances = jnp.exp2(scores)
            value_dot = dot(values, grads, ((1,), (1,)))
            score_grad = (chances * (value_dot - delta)).astype(bf16)
            key_term = dot(score_grad, queries)
            value_term = dot(chances.astype(bf16), grads)
            sums[pl.ds(base, 256), :HD] += key_term[:256]
            sums[pl.ds(base + 1024, 256), :HD] += key_term[256:]
            sums[pl.ds(base, 256), HD:] += value_term[:256]
            sums[pl.ds(base + 1024, 256), HD:] += value_term[256:]
            return total + dot(keys, score_grad, ((0,), (0,)))

        total = jnp.zeros((HD, 256), f32)
        last = 4 * x + z
        total = lax.fori_loop(0, last, lambda i, s: tile(i, s, False), total)
        total = lax.fori_loop(
            last, jnp.minimum(last + 2, 16), lambda i, s: tile(i, s, True), total
        )
        dq_ref[span, :] = total.T * scale
    dkv_ref[:, :HD] = (sums[:, :HD] * scale).astype(bf16)
    dkv_ref[:, HD:] = sums[:, HD:].astype(bf16)


SMEM = pl.BlockSpec(memory_space=pltpu.SMEM)
VMEM = pl.BlockSpec(memory_space=pltpu.VMEM)
params = pltpu.CompilerParams(vmem_limit_bytes=56 * 1024 * 1024)


def attend(z, queries, kv, end):
    return pl.pallas_call(
        attend_kernel,
        out_shape=(
            jax.ShapeDtypeStruct((1024, HD), f32),
            jax.ShapeDtypeStruct((1, 1024), f32),
        ),
        in_specs=[SMEM, VMEM, VMEM, VMEM],
        out_specs=(VMEM, VMEM),
        compiler_params=params,
        cost_estimate=pl.CostEstimate(
            flops=4 * 1024 * 5000 * HD, bytes_accessed=6 << 20, transcendentals=1024 * 5000
        ),
    )(z, queries, kv, end)


def attend_back(z, queries, grads, kv, end, lse, delta):
    return pl.pallas_call(
        attend_back_kernel,
        out_shape=(
            jax.ShapeDtypeStruct((1024, HD), f32),
            jax.ShapeDtypeStruct((8192, 2 * HD), bf16),
        ),
        in_specs=[SMEM, VMEM, VMEM, VMEM, VMEM, VMEM, VMEM],
        out_specs=(VMEM, VMEM),
        scratch_shapes=[pltpu.VMEM((8192, 2 * HD), f32)],
        compiler_params=params,
        cost_estimate=pl.CostEstimate(
            flops=10 * 1024 * 5000 * HD, bytes_accessed=10 << 20, transcendentals=1024 * 5000
        ),
    )(z, queries, grads, kv, end, lse, delta)


def dispatch(main_table, rest_table, value):
    stacked = value.reshape(128, QUARTERS, BAND).transpose(1, 0, 2).reshape(QUARTERS * 128, BAND)
    main = dot(main_table, value).astype(bf16)
    rest = dot(rest_table, stacked).astype(bf16)
    return jnp.concatenate([main, rest], axis=1)


def collect(main_table, rest_table, rows):
    main = dot(main_table, rows[:, :D], ((0,), (0,)))
    rest = dot(rest_table, rows[:, D:], ((0,), (0,)))
    return main + rest.reshape(QUARTERS, 128, BAND).transpose(1, 0, 2).reshape(128, D)


def open_rows(rows):
    rest = rows[:, D:].reshape(64, QUARTERS, REST, BAND).transpose(0, 2, 1, 3)
    return jnp.concatenate([rows[:, :D], rest.reshape(64 * REST, D)], axis=0)


def close_rows(rows):
    rest = rows[64 * MAIN :].reshape(64, REST, QUARTERS, BAND).transpose(0, 2, 1, 3)
    return jnp.concatenate([rows[: 64 * MAIN], rest.reshape(64 * MAIN, BAND)], axis=1)


def local(
    inputs,
    blocks,
    expert_ids,
    attention_gain,
    query_weight,
    key_weight,
    value_weight,
    query_gain,
    key_gain,
    output_weight,
    mixture_gain,
    router_weight,
    gate_weight,
    up_weight,
    down_weight,
    cotangent,
):
    x = lax.axis_index("x")
    z = lax.axis_index("z")
    yh = lax.axis_index("yh")
    c = lax.axis_index("c")
    place = x * 16 + z * 4 + yh * 2 + c
    head = x * 2 + yh
    z_place = z.reshape(1).astype(jnp.int32)

    pad = lambda gain: jnp.pad(gain, (0, 16))[:, None]
    small = jnp.concatenate(
        [
            router_weight,
            attention_gain[:, None],
            mixture_gain[:, None],
            pad(query_gain),
            pad(key_gain),
            jnp.zeros((32, 60), bf16),
        ],
        axis=1,
    )
    small_all = lax.all_gather(small, CTX, axis=0, tiled=True)
    blocks_all = lax.all_gather(blocks, CTX, axis=0, tiled=True)
    router_all = small_all[:, :64]
    attention_gain_all = small_all[:, 64].astype(f32)
    mixture_gain_all = small_all[:, 65].astype(f32)
    head_gains = small_all.reshape(64, 32, 128)[:, :16, 66:68].reshape(1024, 2).astype(f32)
    head_gains = lax.dynamic_slice(head_gains, (head * HD, 0), (HD, 2))
    query_gain_all = head_gains[:, 0]
    key_gain_all = head_gains[:, 1]

    inputs_all = lax.all_gather(inputs, HEADS, axis=0, tiled=True)
    weights_sent = jnp.stack(
        [w.reshape(32, 8, HD) for w in (query_weight, key_weight, value_weight)], axis=2
    )
    weights_sent = weights_sent.transpose(1, 0, 2, 3).reshape(256, 3 * HD)
    weights_all = lax.all_gather(exchange(weights_sent, HEADS), TOKENS, axis=0, tiled=True)
    weights_all = (
        weights_all.reshape(4, 2, 4, 2, 32, 3 * HD).transpose(2, 0, 3, 1, 4, 5).reshape(D, 3 * HD)
    )
    output_all = lax.all_gather(output_weight.T, CTX, axis=0, tiled=True)

    experts = jnp.arange(64, dtype=jnp.int32)
    chosen = jnp.any(expert_ids[:, :, None] == experts[None, None, :], axis=1)
    tokens = jnp.arange(128, dtype=jnp.int32)
    earlier = (tokens[None, :] < tokens[:, None]).astype(bf16)
    ranks = dot(earlier, chosen.astype(bf16)).astype(jnp.int32)
    ranks = jnp.where(chosen, ranks, -1).T
    table = (ranks[:, None, :] == jnp.arange(CAP, dtype=jnp.int32)[None, :, None]).astype(bf16)
    main_table = table[:, :MAIN].reshape(64 * MAIN, 128)
    quarter = jnp.eye(QUARTERS, dtype=bf16)
    rest_table = (
        table[:, None, MAIN:, None, :] * quarter[None, :, None, :, None]
    ).reshape(64 * MAIN, QUARTERS * 128)

    grad_rows = exchange(dispatch(main_table, rest_table, cotangent), CTX)

    source_all = inputs_all.astype(f32)
    attention_inverse = lax.rsqrt(
        jnp.mean(source_all * source_all, axis=-1, keepdims=True) + epsilon
    )
    normed_low = (source_all * attention_inverse * attention_gain_all).astype(bf16)
    raw = dot(normed_low, weights_all)
    query_raw, key_raw = raw[:, :HD], raw[:, HD : 2 * HD]
    value_low = raw[:, 2 * HD :].astype(bf16)
    squares = jnp.stack(
        [jnp.sum(query_raw * query_raw, axis=-1), jnp.sum(key_raw * key_raw, axis=-1)]
    )
    squares = sum_over_rows(squares.reshape(16, 128)).reshape(2, 1024)
    inverses = lax.rsqrt(squares / float(D) + epsilon)
    query_inverse = inverses[0][:, None]
    key_inverse = inverses[1][:, None]
    chunk = jnp.arange(8, dtype=jnp.int32)
    chunk_start = ((chunk // 2) * 16 + z * 4 + (chunk % 2) * 2 + c) * 128
    positions = (chunk_start[:, None] + tokens[None, :]).reshape(1024)
    cosine, sine = rotary_tables(positions)
    query_low = rotate(query_raw * query_inverse * query_gain_all, cosine, sine).astype(bf16)
    key_low = rotate(key_raw * key_inverse * key_gain_all, cosine, sine).astype(bf16)
    kv = lax.all_gather(
        jnp.concatenate([key_low, value_low], axis=1), TOKENS, axis=0, tiled=True
    )
    own_blocks = blocks_all.reshape(4, 4, 2, 2, 128)[:, z, :, c].reshape(1024)
    end = jnp.sum((blocks_all[:, None] <= own_blocks[None, :]).astype(jnp.int32), axis=0)[None]
    attended, lse = attend(z_place, query_low, kv, end)
    attended_low = attended.astype(bf16)

    attended_rows = exchange(attended_low, HEADS).reshape(8, 128, HD)
    attended_rows = attended_rows.transpose(1, 0, 2).reshape(128, 8 * HD)
    source = inputs.astype(f32)
    residual = source + pair_sum(dot(attended_rows, output_all, ((1,), (1,))))
    mixture_inverse = lax.rsqrt(jnp.mean(residual * residual, axis=-1, keepdims=True) + epsilon)
    mixed_low = (residual * mixture_inverse * mixture_gain_all).astype(bf16)
    mixed_rows = exchange(dispatch(main_table, rest_table, mixed_low), CTX)

    entry = open_rows(mixed_rows)
    grad = open_rows(grad_rows)
    logits = dot(entry, router_all)
    shifted = jnp.exp(logits - jnp.max(logits, axis=-1, keepdims=True))
    probability = shifted / jnp.sum(shifted, axis=-1, keepdims=True)
    own_expert = (experts == place).astype(f32)[None, :]
    gates = jnp.sum(probability * own_expert, axis=-1, keepdims=True)
    gate = dot(entry, gate_weight[0])
    upward = dot(entry, up_weight[0])
    sigma = jax.nn.sigmoid(gate)
    swish = gate * sigma
    hidden = swish * upward
    hidden_low = hidden.astype(bf16)
    hidden_pull = dot(grad, down_weight[0], ((1,), (1,)))
    gate_grad = jnp.sum(hidden_low.astype(f32) * hidden_pull, axis=-1, keepdims=True)
    hidden_grad = hidden_pull * gates
    gate_raw_grad = (hidden_grad * upward * sigma * (1.0 + gate * (1.0 - sigma))).astype(bf16)
    up_raw_grad = (hidden_grad * swish).astype(bf16)
    logit_grad = (gate_grad * gates * (own_expert - probability)).astype(bf16)
    entry_grad = (
        dot(gate_raw_grad, gate_weight[0], ((1,), (1,)))
        + dot(up_raw_grad, up_weight[0], ((1,), (1,)))
        + dot(logit_grad, router_all, ((1,), (1,)))
    ).astype(bf16)
    entry_back = exchange(close_rows(entry_grad), CTX)
    result = (dot(hidden_low, down_weight[0]) * gates).astype(bf16)
    result_back = exchange(close_rows(result), CTX)
    down_weight_grad = dot((hidden * gates).astype(bf16), grad, ((0,), (0,)))
    gate_weight_grad = dot(entry, gate_raw_grad, ((0,), (0,)))
    up_weight_grad = dot(entry, up_raw_grad, ((0,), (0,)))
    router_part = dot(entry, logit_grad, ((0,), (0,)))
    router_part = exchange(router_part.reshape(64 * 16, 128), CTX).reshape(64, 16, 128)
    router_grad = lax.psum(jnp.sum(router_part, axis=0), "ep").reshape(32, 64)

    final = residual + pair_sum(collect(main_table, rest_table, result_back))
    mixed_grad = pair_sum(collect(main_table, rest_table, entry_back))

    grad_out = cotangent.astype(f32)
    scaled = mixed_grad * mixture_gain_all
    residual_grad = (
        grad_out
        + mixture_inverse * scaled
        - residual
        * mixture_inverse
        * mixture_inverse
        * mixture_inverse
        * jnp.mean(scaled * residual, axis=-1, keepdims=True)
    )
    mixture_gain_part = jnp.sum(mixed_grad * residual * mixture_inverse, axis=0)
    residual_low = residual_grad.astype(bf16)
    attended_grad = dot(residual_low, output_all).astype(bf16)
    attended_grad = attended_grad.reshape(128, 8, HD).transpose(1, 0, 2).reshape(1024, HD)
    attended_grad = exchange(attended_grad, HEADS)
    residual_all = lax.all_gather(residual_low, HEADS, axis=0, tiled=True)
    output_part = dot(attended_low, residual_all, ((0,), (0,))).astype(bf16)
    output_part = output_part.reshape(HD, 64, 32).transpose(1, 0, 2).reshape(64 * 32, HD)
    output_part = exchange(output_part, CTX).reshape(4, 4, 2, 2, HD, 32)
    output_grad = jnp.sum(output_part.astype(f32), axis=(1, 3)).reshape(8 * HD, 32)

    delta = jnp.sum(attended_grad.astype(f32) * attended, axis=-1)[None]
    query_grad, kv_part = attend_back(
        z_place, query_low, attended_grad, kv, end, lse, delta
    )
    kv_grad = jnp.sum(exchange(kv_part, TOKENS).reshape(8, 1024, 2 * HD).astype(f32), axis=0)
    value_grad_low = kv_grad[:, HD:].astype(bf16)
    query_normed_grad = rotate(query_grad, cosine, -sine)
    key_normed_grad = rotate(kv_grad[:, :HD], cosine, -sine)
    query_scaled = query_normed_grad * query_gain_all
    key_scaled = key_normed_grad * key_gain_all
    dots = jnp.stack(
        [jnp.sum(query_scaled * query_raw, axis=-1), jnp.sum(key_scaled * key_raw, axis=-1)]
    )
    dots = sum_over_rows(dots.reshape(16, 128)).reshape(2, 1024)[:, :, None] / float(D)

    def raw_back(value, inverse, scaled_grad, mean):
        return (inverse * scaled_grad - value * inverse * inverse * inverse * mean).astype(bf16)

    query_raw_low = raw_back(query_raw, query_inverse, query_scaled, dots[0])
    key_raw_low = raw_back(key_raw, key_inverse, key_scaled, dots[1])
    query_gain_part = jnp.sum(query_normed_grad * query_raw * query_inverse, axis=0)
    key_gain_part = jnp.sum(key_normed_grad * key_raw * key_inverse, axis=0)
    raw_grads = jnp.concatenate([query_raw_low, key_raw_low, value_grad_low], axis=1)
    normed_part = dot(raw_grads, weights_all, ((1,), (1,)))
    attention_gain_part = jnp.sum(normed_part * source_all * attention_inverse, axis=0)
    normed_grad = jnp.sum(
        exchange(normed_part.astype(bf16), HEADS).reshape(8, 128, D).astype(f32), axis=0
    )
    normed_grad = pair_sum(normed_grad)
    weight_part = dot(normed_low, raw_grads, ((0,), (0,))).astype(bf16)
    weight_part = exchange(weight_part, CTX).reshape(4, 4, 2, 2, 32, 3, HD)
    weight_grad = jnp.sum(weight_part.astype(f32), axis=(1, 3)).reshape(8, 32, 3, HD)
    weight_grad = weight_grad.transpose(2, 1, 0, 3).reshape(3, 32, 8 * HD)

    def head_part(value):
        wide = lax.dynamic_update_slice(jnp.zeros((8 * HD,), f32), value, (head * HD,))
        return wide.reshape(64, 16)

    gains = jnp.concatenate(
        [
            attention_gain_part.reshape(64, 32),
            mixture_gain_part.reshape(64, 32),
            head_part(query_gain_part),
            head_part(key_gain_part),
            jnp.zeros((64, 32), f32),
        ],
        axis=1,
    )
    gains = jnp.broadcast_to(gains[:, None, :], (64, 8, 128)).reshape(512, 128)
    gains = jnp.sum(exchange(gains, CTX).reshape(64, 8, 128)[:, 0], axis=0)
    attention_gain_grad = lax.psum(gains[:32], "ep")

    inverse = lax.rsqrt(jnp.mean(source * source, axis=-1, keepdims=True) + epsilon)
    scaled = normed_grad * attention_gain_all
    input_grad = (
        residual_grad
        + inverse * scaled
        - source
        * inverse
        * inverse
        * inverse
        * jnp.mean(scaled * source, axis=-1, keepdims=True)
    )
    return (
        final,
        input_grad,
        attention_gain_grad,
        weight_grad[0],
        weight_grad[1],
        weight_grad[2],
        gains[64:80],
        gains[80:96],
        output_grad,
        gains[32:64],
        router_grad,
        gate_weight_grad[None],
        up_weight_grad[None],
        down_weight_grad[None],
    )


def solution(mesh):
    inner = Mesh(mesh.devices.reshape(4, 4, 2, 2, 2), ("x", "z", "yh", "c", "ep"))
    in_specs = (
        P(CTX, None),
        P(CTX),
        P(CTX, None),
        P(CTX),
        P(CTX, "ep"),
        P(CTX, "ep"),
        P(CTX, "ep"),
        P(("ep",) + CTX),
        P(("ep",) + CTX),
        P("ep", CTX),
        P(CTX),
        P(CTX, None),
        P(CTX, None, "ep"),
        P(CTX, None, "ep"),
        P(CTX, "ep", None),
        P(CTX, None),
    )
    out_specs = (
        P(CTX, None),
        P(CTX, None),
        P(CTX),
        P(CTX, "ep"),
        P(CTX, "ep"),
        P(CTX, "ep"),
        P(("ep",) + CTX),
        P(("ep",) + CTX),
        P("ep", CTX),
        P(CTX),
        P(CTX, None),
        P(CTX, None, "ep"),
        P(CTX, None, "ep"),
        P(CTX, "ep", None),
    )
    return jax.shard_map(local, mesh=inner, in_specs=in_specs, out_specs=out_specs, check_vma=False)
```

time: 4760 us -> 1030 us (0.22)
  waiting for transfers between devices: 2350 us -> 354 us
  starting transfers between devices: 909 us -> 119 us
  blocking collectives: 872 us -> 219 us
  matrix products: 313 us -> 110 us
  local copies, waits for them, and re-layouts: 143 us -> 77.6 us
  Pallas kernels: 0 us -> 56.4 us
    reduce_scatter x5 -> x0, waiting for transfers between devices: 1370 us -> none  [the longest x1 344 us: local(): lax.psum_scatter(query_weight_grad, 'ctx', scatter_dimension=0, tiled=True)]
    ppermute x320 -> x4, starting transfers between devices: 841 us -> 5.81 us  [pair_sum(): other = lax.ppermute(own, 'ep', [(0, 1), (1, 0)])]
    unnamed x2 -> x0, blocking collectives: 586 us -> none
    ppermute x320 -> x4, waiting for transfers between devices: 542 us -> 75.4 us  [pair_sum(): other = lax.ppermute(own, 'ep', [(0, 1), (1, 0)])]
    dot_general x346 -> x27, matrix products: 313 us -> 110 us  [dot(): lax.dot_general(first, second, (dims, ((), ())), preferred_element_type=f32)]
    psum x3 -> x0, waiting for transfers between devices: 154 us -> none  [the longest x1 114 us: local(): final = residual + lax.psum(mixture_part, 'ep')]
    all_gather x2, blocking collectives: 267 us -> 164 us  [the longest x1 82.4 us: local(): blocks_all = lax.all_gather(blocks, CTX, axis=0, tiled=True)]
    all_gather x6 -> x5, waiting for transfers between devices: 109 us -> 7.17 us  [the longest x1 7.14 us: local(): inputs_all = lax.all_gather(inputs, HEADS, axis=0, tiled=True)]
  transfers between devices with their start and end apart: 338 -> 21, of which waited for: 193 -> 13; matrix products, arithmetic and copies ran while one was open for 10% -> 15% of each run, Pallas kernels for 0% -> 3%
where the time goes in v1:
time: 1030 us; the launch traced here: 1010 us
  waiting for transfers between devices  354 us (34%)
  blocking collectives  219 us (21%)
  starting transfers between devices  119 us (12%)
  matrix products  110 us (11%)
  local copies, waits for them, and re-layouts  77.6 us (8%)
  other arithmetic  61.2 us (6%)
  Pallas kernels  56.4 us (5%)
  between operations  15.5 us (2%)
    all_to_all x12, waiting for transfers between devices, exchange(): return lax.all_to_all(value, axes, split_axis=0, concat_axis=0, tiled=True)  270 us
    all_to_all x12, starting transfers between devices, exchange(): return lax.all_to_all(value, axes, split_axis=0, concat_axis=0, tiled=True)  113 us
    dot_general x27, matrix products, dot(): lax.dot_general(first, second, (dims, ((), ())), preferred_element_type=f32)  110 us
    all_gather x1, blocking collectives, local(): blocks_all = lax.all_gather(blocks, CTX, axis=0, tiled=True)  82.4 us
    all_gather x1, blocking collectives, local(): small_all = lax.all_gather(small, CTX, axis=0, tiled=True)  82 us
    ppermute x4, waiting for transfers between devices, pair_sum(): other = lax.ppermute(own, 'ep', [(0, 1), (1, 0)])  75.4 us
    all_to_all x3, blocking collectives, exchange(): return lax.all_to_all(value, axes, split_axis=0, concat_axis=0, tiled=True)  46.6 us
    pallas_call x1, Pallas kernels, attend_back(): pl.pallas_call(attend_back_kernel, out_shape=(jax.ShapeDtypeStruct((1024,...  29.4 us
  transfers between devices with their start and end apart: 21, of which 13 were waited for; matrix products, arithmetic and copies ran while one was open for 15% of the time, Pallas kernels for 3%

profile of v1, /device:TPU:96, one launch (start us, length us, event | category | flops | bytes accessed | tf_op | source)
XLA Modules:
  0.0 1013.2 jit_solution(3900459908419948460)
XLA Ops:
  10.9 15.0 %all_to_all.134 = bf16[8,32,384]{2,1,0:T(8,128)(2,1)} all-to-all(bf16[8,32,384]{2,1,0:T(8,128)(2,1)S(1)} %all_to_all.89), channel_id=1, replica_groups=mesh['x'=4,'z'=4,'yh'=2,'c'=2,'ep'=2] {'x','yh'}, dimensions={0} | all-to-all | bytes 393216 | tf_op jit(solution)/shard_map/all_to_all | solution.py:41
  30.5 82.0 %all_gather.22 = bf16[2048,128]{1,0:T(8,128)(2,1)S(1)} all-gather(bf16[32,128]{1,0:T(8,128)(2,1)S(1)} %concatenate.53), channel_id=1, replica_groups=mesh['x'=4,'z'=4,'yh'=2,'c'=2,'ep'=2] {'x','z','yh','c'}, dimensions={0}, use_global_device_ids=true | all-gather | bytes 532480 | tf_op jit(solution)/shard_map/all_gather | solution.py:266
  154.1 82.4 %all-gather = s32[64,1,128]{2,1,0:T(1,128)S(1)} all-gather(s32[1,1,128]{2,1,0:T(1,128)} %bitcast.273), channel_id=1, replica_groups=mesh['x'=4,'z'=4,'yh'=2,'c'=2,'ep'=2] {'x','z','yh','c'}, dimensions={0}, use_global_device_ids=true | all-gather | bytes 33280 | tf_op jit(solution)/shard_map/all_gather | solution.py:267
  250.2 27.0 %shard_map.263 = (f32[1024,128]{1,0:T(8,128)}, f32[1,1024]{1,0:T(1,128)}) custom-call(s32[1]{0:T(128)} %bitcast.z_ref, bf16[1024,128]{1,0:T(8,128)(2,1)} %pad_maximum_fusion.16.q_ref, bf16[8192,256]{1,0:T(8,128)(2,1)} %all-gather.11.cloned.1.call-done.kv_ref, s32[1,1024]{1,0:T(1,128)} %bitcast.276), custom_call_target="tpu_custom_call" | custom-call | flops 2621440000 | bytes 6291456 | tf_op jit(solution)/shard_map/pallas_call | solution.py:173
  279.1 13.5 %all-to-all-start.2 = ((bf16[8,128,128]{1,2,0:T(8,128)(2,1)}), bf16[8,128,128]{1,2,0:T(8,128)(2,1)S(1)}, u32[]{:S(2)}, u32[]{:S(2)}) async-start(bf16[8,128,128]{1,2,0:T(8,128)(2,1)} %copy.199), calls=%async_computation.2 | async-start | bytes 524288 | tf_op jit(solution)/shard_map/all_to_all | solution.py:41
  313.1 65.8 %collective-permute-done = bf16[128,2048]{1,0:T(8,128)(2,1)S(1)} collective-permute-done((bf16[128,2048]{1,0:T(8,128)(2,1)S(1)}, bf16[128,2048]{1,0:T(8,128)(2,1)S(1)}, u32[]{:S(2)}, u32[]{:S(2)}) %collective-permute-start) | collective-permute-done | bytes 524320 | tf_op jit(solution)/shard_map/ppermute | solution.py:46
  384.3 16.9 %all-to-all-start.3 = ((bf16[64,16,2560]{2,1,0:T(8,128)(2,1)}), bf16[64,16,2560]{2,1,0:T(8,128)(2,1)}, u32[]{:S(2)}, u32[]{:S(2)}) async-start(bf16[64,16,2560]{2,1,0:T(8,128)(2,1)} %bitcast.204), calls=%async_computation.3 | async-start | bytes 10485760 | tf_op jit(solution)/shard_map/all_to_all | solution.py:41
  413.5 52.9 %all-to-all-done.3 = bf16[64,16,2560]{2,1,0:T(8,128)(2,1)} async-done(((bf16[64,16,2560]{2,1,0:T(8,128)(2,1)}), bf16[64,16,2560]{2,1,0:T(8,128)(2,1)}, u32[]{:S(2)}, u32[]{:S(2)}) %all-to-all-start.3) | async-done | bytes 5242912 | tf_op jit(solution)/shard_map/all_to_all | solution.py:41
  506.6 8.6 add_convert_fusion
  526.7 14.8 %all-to-all-start.6 = ((bf16[64,16,2560]{2,1,0:T(8,128)(2,1)}), bf16[64,16,2560]{2,1,0:T(8,128)(2,1)}, u32[]{:S(2)}, u32[]{:S(2)}) async-start(bf16[64,16,2560]{2,1,0:T(8,128)(2,1)} %pad_maximum_fusion.5), calls=%async_computation.6 | async-start | bytes 10485760 | tf_op jit(solution)/shard_map/all_to_all | solution.py:41
  554.1 52.4 %all-to-all-done.6 = bf16[64,16,2560]{2,1,0:T(8,128)(2,1)} async-done(((bf16[64,16,2560]{2,1,0:T(8,128)(2,1)}), bf16[64,16,2560]{2,1,0:T(8,128)(2,1)}, u32[]{:S(2)}, u32[]{:S(2)}) %all-to-all-start.6) | async-done | bytes 5242912 | tf_op jit(solution)/shard_map/all_to_all | solution.py:41
  606.5 13.8 %all-to-all-start.4 = ((bf16[64,16,2560]{2,1,0:T(8,128)(2,1)}), bf16[64,16,2560]{2,1,0:T(8,128)(2,1)}, u32[]{:S(2)}, u32[]{:S(2)}) async-start(bf16[64,16,2560]{2,1,0:T(8,128)(2,1)} %pad_maximum_fusion.2), calls=%async_computation.4 | async-start | bytes 10485760 | tf_op jit(solution)/shard_map/all_to_all | solution.py:41
  627.3 58.4 %all-to-all-done.4 = bf16[64,16,2560]{2,1,0:T(8,128)(2,1)} async-done(((bf16[64,16,2560]{2,1,0:T(8,128)(2,1)}), bf16[64,16,2560]{2,1,0:T(8,128)(2,1)}, u32[]{:S(2)}, u32[]{:S(2)}) %all-to-all-start.4) | async-done | bytes 5242912 | tf_op jit(solution)/shard_map/all_to_all | solution.py:41
  695.9 9.6 collective-permute-done.1
  710.6 14.5 %all_to_all.135 = bf16[8,128,128]{2,1,0:T(8,128)(2,1)S(1)} all-to-all(bf16[8,128,128]{2,1,0:T(8,128)(2,1)S(1)} %bitcast.249), channel_id=1, replica_groups=mesh['x'=4,'z'=4,'yh'=2,'c'=2,'ep'=2] {'x','yh'}, dimensions={0} | all-to-all | bytes 524288 | tf_op jit(solution)/shard_map/all_to_all | solution.py:41
  725.9 29.4 %shard_map.264 = (f32[1024,128]{1,0:T(8,128)}, bf16[8192,256]{1,0:T(8,128)(2,1)}) custom-call(s32[1]{0:T(128)} %bitcast.z_ref, bf16[1024,128]{1,0:T(8,128)(2,1)} %pad_maximum_fusion.16.q_ref, bf16[1024,128]{1,0:T(8,128)(2,1)} %bitcast.236, bf16[8192,256]{1,0:T(8,128)(2,1)} %all-gather.11.cloned.1.call-done.kv_ref, s32[1,1024]{1,0:T(1,128)} %bitcast.277, ...), custom_call_target="tpu_custom_call" | custom-call | flops 6553600000 | bytes 10485760 | tf_op jit(solution)/shard_map/pallas_call | solution.py:189
  762.7 47.1 %all-to-all-done.8 = bf16[8,1024,256]{2,1,0:T(8,128)(2,1)} async-done(((bf16[8,1024,256]{2,1,0:T(8,128)(2,1)}), bf16[8,1024,256]{2,1,0:T(8,128)(2,1)}, u32[]{:S(2)}, u32[]{:S(2)}) %all-to-all-start.8) | async-done | bytes 4194336 | tf_op jit(solution)/shard_map/all_to_all | solution.py:41
  832.4 9.4 all-to-all-start.14
  853.5 17.1 %all_to_all.136 = f32[64,8,128]{2,1,0:T(8,128)S(1)} all-to-all(f32[64,8,128]{2,1,0:T(8,128)S(1)} %broadcast_in_dim.49), channel_id=1, replica_groups=mesh['x'=4,'z'=4,'yh'=2,'c'=2,'ep'=2] {'x','z','yh','c'}, dimensions={0} | all-to-all | bytes 524288 | tf_op jit(solution)/shard_map/all_to_all | solution.py:41
  891.3 44.0 %all-to-all-done.10 = bf16[8,128,2048]{2,1,0:T(8,128)(2,1)} async-done(((bf16[8,128,2048]{2,1,0:T(8,128)(2,1)}), bf16[8,128,2048]{2,1,0:T(8,128)(2,1)}, u32[]{:S(2)}, u32[]{:S(2)}) %all-to-all-start.10) | async-done | bytes 4194336 | tf_op jit(solution)/shard_map/all_to_all | solution.py:41
  935.3 9.2 all-to-all-start.12
  944.5 9.1 fusion.11
  966.4 9.3 all-to-all-start.13
  976.3 8.2 all-reduce.2
  (318 shorter events, 287.1 us)
Async XLA Ops:
  7.2 481.5 %copy-start = (bf16[1,512,2048]{2,1,0:T(8,128)(2,1)S(1)}, bf16[1,512,2048]{2,1,0:T(8,128)(2,1)}, u32[]{:S(2)}) copy-start(bf16[1,512,2048]{2,1,0:T(8,128)(2,1)} %param.30) | copy-start | bytes 6291460
  7.2 106.9 %all-gather.9.cloned.1.call-start = ((), (), s32[]{:S(2)}) async-start(), calls=%async_computation.16 | async-start | bytes 1769472 | tf_op jit(solution)/shard_map/all_gather | solution.py:281
  25.9 98.1 %all-gather.7.cloned.1.call-start = ((), (), s32[]{:S(2)}) async-start(), calls=%async_computation.15 | async-start | bytes 4718592 | tf_op jit(solution)/shard_map/all_gather | solution.py:276
  133.9 11.3 %all-to-all-start.1 = ((f32[16,16,128]{2,1,0:T(8,128)}), f32[16,16,128]{2,1,0:T(8,128)S(1)}, u32[]{:S(2)}, u32[]{:S(2)}) async-start(f32[16,16,128]{2,1,0:T(8,128)} %broadcast_in_dim.42), calls=%async_computation.1 | async-start | bytes 262144 | tf_op jit(solution)/shard_map/all_to_all | solution.py:41
  137.5 112.7 %all-gather.11.cloned.1.call-start = ((), (), s32[]{:S(2)}) async-start(), calls=%async_computation.17 | async-start | bytes 4718592 | tf_op jit(solution)/shard_map/all_gather | solution.py:323
  151.1 157.5 %all-gather.13.cloned.1.call-start = ((), (), s32[]{:S(2)}) async-start(), calls=%async_computation.18 | async-start | bytes 4259840 | tf_op jit(solution)/shard_map/all_gather | solution.py:285
  152.8 227.5 %copy-start.24 = (pred[64,16,128]{2,1,0:T(8,128)(4,1)}, pred[64,16,128]{2,1,0:T(8,128)(4,1)S(1)}, u32[]{:S(2)}) copy-start(pred[64,16,128]{2,1,0:T(8,128)(4,1)S(1)} %slice.203) | copy-start | bytes 393220
  279.1 22.4 %all-to-all-start.2 = ((bf16[8,128,128]{1,2,0:T(8,128)(2,1)}), bf16[8,128,128]{1,2,0:T(8,128)(2,1)S(1)}, u32[]{:S(2)}, u32[]{:S(2)}) async-start(bf16[8,128,128]{1,2,0:T(8,128)(2,1)} %copy.199), calls=%async_computation.2 | async-start | bytes 524288 | tf_op jit(solution)/shard_map/all_to_all | solution.py:41
  301.5 82.8 %all-to-all-start.5 = ((bf16[64,16,2560]{2,1,0:T(8,128)(2,1)}), bf16[64,16,2560]{2,1,0:T(8,128)(2,1)}, u32[]{:S(2)}, u32[]{:S(2)}) async-start(bf16[64,16,2560]{2,1,0:T(8,128)(2,1)} %bitcast.203), calls=%async_computation.5 | async-start | bytes 10485760 | tf_op jit(solution)/shard_map/all_to_all | solution.py:41
  312.5 66.5 %collective-permute-start = (bf16[128,2048]{1,0:T(8,128)(2,1)S(1)}, bf16[128,2048]{1,0:T(8,128)(2,1)S(1)}, u32[]{:S(2)}, u32[]{:S(2)}) collective-permute-start(bf16[128,2048]{1,0:T(8,128)(2,1)S(1)} %convolution_convert_fusion.4), channel_id=1, source_target_pairs={{0,1},{1,0},{2,3},{3,2},{4,5},{5,4},{6,7},{7,6},{8,9},{9,8},{10,11... | collective-permute-start | bytes 1572872 | tf_op jit(solution)/shard_map/ppermute | solution.py:46
  384.3 82.1 %all-to-all-start.3 = ((bf16[64,16,2560]{2,1,0:T(8,128)(2,1)}), bf16[64,16,2560]{2,1,0:T(8,128)(2,1)}, u32[]{:S(2)}, u32[]{:S(2)}) async-start(bf16[64,16,2560]{2,1,0:T(8,128)(2,1)} %bitcast.204), calls=%async_computation.3 | async-start | bytes 10485760 | tf_op jit(solution)/shard_map/all_to_all | solution.py:41
  401.3 105.3 %copy-start.46 = (f32[64]{0:T(128)}, f32[64]{0:T(128)S(1)}, u32[]{:S(2)}) copy-start(f32[64]{0:T(128)S(1)} %compare_convert_fusion) | copy-start | bytes 772
  526.7 79.8 %all-to-all-start.6 = ((bf16[64,16,2560]{2,1,0:T(8,128)(2,1)}), bf16[64,16,2560]{2,1,0:T(8,128)(2,1)}, u32[]{:S(2)}, u32[]{:S(2)}) async-start(bf16[64,16,2560]{2,1,0:T(8,128)(2,1)} %pad_maximum_fusion.5), calls=%async_computation.6 | async-start | bytes 10485760 | tf_op jit(solution)/shard_map/all_to_all | solution.py:41
  606.5 79.2 %all-to-all-start.4 = ((bf16[64,16,2560]{2,1,0:T(8,128)(2,1)}), bf16[64,16,2560]{2,1,0:T(8,128)(2,1)}, u32[]{:S(2)}, u32[]{:S(2)}) async-start(bf16[64,16,2560]{2,1,0:T(8,128)(2,1)} %pad_maximum_fusion.2), calls=%async_computation.4 | async-start | bytes 10485760 | tf_op jit(solution)/shard_map/all_to_all | solution.py:41
  627.2 68.3 %collective-permute-start.2 = (bf16[128,2048]{1,0:T(8,128)(2,1)S(1)}, bf16[128,2048]{1,0:T(8,128)(2,1)S(1)}, u32[]{:S(2)}, u32[]{:S(2)}) collective-permute-start(bf16[128,2048]{1,0:T(8,128)(2,1)S(1)} %fusion.19), channel_id=1, source_target_pairs={{0,1},{1,0},{2,3},{3,2},{4,5},{5,4},{6,7},{7,6},{8,9},{9,8},{10,11... | collective-permute-start | bytes 1572872 | tf_op jit(solution)/shard_map/ppermute | solution.py:46
  691.1 14.4 %collective-permute-start.1 = (bf16[128,2048]{1,0:T(8,128)(2,1)S(1)}, bf16[128,2048]{1,0:T(8,128)(2,1)S(1)}, u32[]{:S(2)}, u32[]{:S(2)}) collective-permute-start(bf16[128,2048]{1,0:T(8,128)(2,1)S(1)} %fusion.22), channel_id=1, source_target_pairs={{0,1},{1,0},{2,3},{3,2},{4,5},{5,4},{6,7},{7,6},{8,9},{9,8},{10,11... | collective-permute-start | bytes 1572872 | tf_op jit(solution)/shard_map/ppermute | solution.py:46
  755.4 54.4 %all-to-all-start.8 = ((bf16[8,1024,256]{2,1,0:T(8,128)(2,1)}), bf16[8,1024,256]{2,1,0:T(8,128)(2,1)}, u32[]{:S(2)}, u32[]{:S(2)}) async-start(bf16[8,1024,256]{2,1,0:T(8,128)(2,1)} %bitcast.214), calls=%async_computation.8 | async-start | bytes 8388608 | tf_op jit(solution)/shard_map/all_to_all | solution.py:41
  762.1 192.3 %all-gather.15.cloned.1.call-start = ((), (), s32[]{:S(2)}) async-start(), calls=%async_computation.19 | async-start | bytes 4718592 | tf_op jit(solution)/shard_map/all_gather | solution.py:392
  819.2 13.2 %all-to-all-start.9 = ((f32[16,16,128]{2,1,0:T(8,128)}), f32[16,16,128]{2,1,0:T(8,128)}, u32[]{:S(2)}, u32[]{:S(2)}) async-start(f32[16,16,128]{2,1,0:T(8,128)} %broadcast_in_dim.47), calls=%async_computation.9 | async-start | bytes 262144 | tf_op jit(solution)/shard_map/all_to_all | solution.py:41
  832.4 21.0 %all-to-all-start.14 = ((f32[64,16,128]{2,1,0:T(8,128)}), f32[64,16,128]{2,1,0:T(8,128)S(1)}, u32[]{:S(2)}, u32[]{:S(2)}) async-start(f32[64,16,128]{2,1,0:T(8,128)} %all_to_all.117), calls=%async_computation.14 | async-start | bytes 1048576 | tf_op jit(solution)/shard_map/all_to_all | solution.py:41
  870.5 64.8 %all-to-all-start.10 = ((bf16[8,128,2048]{2,1,0:T(8,128)(2,1)}), bf16[8,128,2048]{2,1,0:T(8,128)(2,1)}, u32[]{:S(2)}, u32[]{:S(2)}) async-start(bf16[8,128,2048]{2,1,0:T(8,128)(2,1)} %bitcast.213), calls=%async_computation.10 | async-start | bytes 8388608 | tf_op jit(solution)/shard_map/all_to_all | solution.py:41
  935.3 31.1 %all-to-all-start.12 = ((bf16[64,32,384]{2,1,0:T(8,128)(2,1)}), bf16[64,32,384]{2,1,0:T(8,128)(2,1)S(1)}, u32[]{:S(2)}, u32[]{:S(2)}) async-start(bf16[64,32,384]{2,1,0:T(8,128)(2,1)} %bitcast.234), calls=%async_computation.12 | async-start | bytes 3145728 | tf_op jit(solution)/shard_map/all_to_all | solution.py:41
  963.9 38.1 %collective-permute-start.3 = (bf16[128,2048]{1,0:T(8,128)(2,1)S(1)}, bf16[128,2048]{1,0:T(8,128)(2,1)}, u32[]{:S(2)}, u32[]{:S(2)}) collective-permute-start(bf16[128,2048]{1,0:T(8,128)(2,1)S(1)} %reduce_sum.253), channel_id=1, source_target_pairs={{0,1},{1,0},{2,3},{3,2},{4,5},{5,4},{6,7},{7,6},{8,9},{9,8},{10,11... | collective-permute-start | bytes 1572872 | tf_op jit(solution)/shard_map/ppermute | solution.py:46
  966.4 26.4 %all-to-all-start.13 = ((bf16[64,32,128]{2,1,0:T(8,128)(2,1)}), bf16[64,32,128]{2,1,0:T(8,128)(2,1)}, u32[]{:S(2)}, u32[]{:S(2)}) async-start(bf16[64,32,128]{2,1,0:T(8,128)(2,1)} %copy.222), calls=%async_computation.13 | async-start | bytes 1048576 | tf_op jit(solution)/shard_map/all_to_all | solution.py:41
  (58 other events, 895.5 us)
Sparse Core Ops, SparseCore 0:
  26.1 20.0 all-gather.8
  48.5 75.5 all-gather.6
  151.3 30.8 all-gather.10
  185.2 71.9 all-gather.12
  764.9 70.6 all-gather.14

commit v2 on v1

--- a/solution.py
+++ b/solution.py
@@ -18,6 +18,13 @@
 QUARTERS = 4
 BAND = D // QUARTERS
 WINDOW = 512
+HALF_MAIN = 32 * MAIN
+HALF_REST = 32 * REST
+HALF = HALF_MAIN + HALF_REST
+ROW_WIDTH = D + BAND
+SIDE = D // 2
+SIDE_BAND = SIDE // QUARTERS
+SIDE_WIDTH = SIDE + SIDE_BAND
 
 epsilon = 1e-05
 rotary_base = 10000.0
@@ -41,6 +48,23 @@
     return lax.all_to_all(value, axes, split_axis=0, concat_axis=0, tiled=True)
 
 
+OFFSETS = [(i, j) for i in range(4) for j in range(2)]
+
+
+def ring(value, axis):
+    return [value] + [
+        lax.ppermute(value, axis, [(a, (a + i) % 4) for a in range(4)]) for i in (1, 2, 3)
+    ]
+
+
+def swap(value, axis):
+    return lax.ppermute(value, axis, [(0, 1), (1, 0)])
+
+
+def below(a, b):
+    return jnp.stack([(a - i) % 4 * 2 + (b - j) % 2 for i, j in OFFSETS])
+
+
 def pair_sum(value):
     own = lax.optimization_barrier(value.astype(bf16))
     other = lax.ppermute(own, "ep", [(0, 1), (1, 0)])
@@ -77,6 +101,66 @@
     row = lax.broadcasted_iota(jnp.int32, (WINDOW, 1), 0)
     place = (row & 127) + ((row >> 7) & 1) * 256 + (row >> 8) * 128 + index * WINDOW
     return place < end
+
+
+def project_kernel(place_ref, *refs):
+    inputs, weights = refs[:8], refs[8:12]
+    normed_ref, raw_ref, square_ref, weight_ref, small_ref, gain_ref = refs[12:]
+    for n, (i, j) in enumerate(OFFSETS):
+        for m in range(8):
+            row = (place_ref[8 + n] + (m // 2) * 16 + (m % 2) * 2) * 32
+            here = pl.ds(pl.multiple_of(row, 32), 32)
+            weight_ref[here, :] = weights[i][j, m * 32 : m * 32 + 32, : 3 * HD]
+            small_ref[here, :] = weights[i][j, m * 32 : m * 32 + 32, 3 * HD :]
+    row = lax.broadcasted_iota(jnp.int32, (8, 128), 0)
+    column = lax.broadcasted_iota(jnp.int32, (8, 128), 1)
+    pick = jnp.where(column == row + 64, 1.0, 0.0).astype(bf16)
+    gain_ref[...] = dot(pick, small_ref[...], ((1,), (1,)))
+    gain = gain_ref[0:1, :]
+    for n in range(8):
+        value = inputs[n][...].astype(f32)
+        inverse = lax.rsqrt(jnp.mean(value * value, axis=-1, keepdims=True) + epsilon)
+        normed = (value * inverse * gain).astype(bf16)
+        chunk = place_ref[n]
+        here = pl.ds(pl.multiple_of(chunk * 128, 128), 128)
+        normed_ref[here, :] = normed
+        raw = dot(normed, weight_ref[...])
+        raw_ref[here, :] = raw
+        for part in range(2):
+            own = raw[:, part * HD : part * HD + HD]
+            square = jnp.sum(own * own, axis=-1, keepdims=True)
+            square = jnp.broadcast_to(square, (128, 128)).T
+            square_ref[pl.ds(chunk + 8 * part, 1), :] = square[0:1]
+
+
+def spread_kernel(
+    raw_ref, normed_ref, weight_ref, router_ref, gain_ref, extra_ref, output_ref, back_ref, share_ref
+):
+    total = jnp.zeros((1, D), f32)
+    for n in range(4):
+        here = slice(n * 256, n * 256 + 256)
+        part = dot(raw_ref[here, :], weight_ref[...], ((1,), (1,)))
+        total = total + jnp.sum(part * normed_ref[here, :].astype(f32), axis=0, keepdims=True)
+        back_ref[here, :] = part.astype(bf16)
+    total = total / gain_ref[0:1, :]
+    row = lax.broadcasted_iota(jnp.int32, (8, 1), 0)
+    extra = extra_ref[...] + jnp.where(row == 0, total, 0.0)
+    for n in range(4):
+        band = slice(n * 512, n * 512 + 512)
+        part = dot(normed_ref[:, band], raw_ref[...], ((0,), (0,))).astype(bf16)
+        side = jnp.concatenate(
+            [jnp.zeros((64, 512), f32), extra[:, band], jnp.zeros((56, 512), f32)], axis=0
+        )
+        side = (side.T + router_ref[band, :]).astype(bf16)
+        for m in range(16):
+            z, yh, c = m // 4, m // 2 % 2, m % 2
+            start = (z * 2 + c) * 320
+            there = slice(start + (n * 2 + yh) * 32, start + (n * 2 + yh) * 32 + 32)
+            share_ref[there, : 3 * HD] = part[m * 32 : m * 32 + 32]
+            share_ref[there, 3 * HD :] = side[m * 32 : m * 32 + 32]
+            if n == 0:
+                there = slice(start + 256 + yh * 32, start + 288 + yh * 32)
+                share_ref[there, :] = output_ref[m * 32 : m * 32 + 32, :].astype(bf16)
 
 
 def attend_kernel(z_ref, q_ref, kv_ref, end_ref, out_ref, lse_ref):
@@ -164,9 +248,227 @@
     dkv_ref[:, HD:] = sums[:, HD:].astype(bf16)
 
 
+def rest_pick(quarter):
+    row = lax.broadcasted_iota(jnp.int32, (HALF_REST, HALF_MAIN), 0)
+    column = lax.broadcasted_iota(jnp.int32, (HALF_REST, HALF_MAIN), 1)
+    same = (column >> 4 == row >> 2) & (column & 3 == row & 3)
+    return jnp.where(same & ((column >> 2) & 3 == quarter), 1.0, 0.0).astype(bf16)
+
+
+def open_rest(rows):
+    rest = rows[:, D:]
+    return jnp.concatenate(
+        [dot(rest_pick(q), rest).astype(bf16) for q in range(QUARTERS)], axis=1
+    )
+
+
+def open_side(rows_ref):
+    rest = rows_ref[:, SIDE:]
+    rest = jnp.concatenate(
+        [dot(rest_pick(q), rest).astype(bf16) for q in range(QUARTERS)], axis=1
+    )
+    return rows_ref[:, :SIDE], rest
+
+
+def pull_kernel(side_ref, own_ref, other_ref, down_ref, flat_ref, pull_ref):
+    own = pl.multiple_of(side_ref[0] * SIDE, SIDE)
+    other = pl.multiple_of(SIDE - side_ref[0] * SIDE, SIDE)
+    for ref, start in ((own_ref, own), (other_ref, other)):
+        main, rest = open_side(ref)
+        flat_ref[:HALF_MAIN, pl.ds(start, SIDE)] = main
+        flat_ref[HALF_MAIN:, pl.ds(start, SIDE)] = rest
+    pull_ref[...] = dot(flat_ref[...], down_ref[...], ((1,), (1,)))
+
+
+def expert_kernel(
+    place_ref,
+    rows_ref,
+    pull_ref,
+    gate_ref,
+    up_ref,
+    router_ref,
+    back_ref,
+    flat_ref,
+    hidden_ref,
+    gate_grad_ref,
+    up_grad_ref,
+    logit_grad_ref,
+):
+    flat_ref[:HALF_MAIN] = rows_ref[:, :D]
+    flat_ref[HALF_MAIN:] = open_rest(rows_ref)
+    entry = flat_ref[...]
+    lane = lax.broadcasted_iota(jnp.int32, (1, 128), 1)
+    logits = jnp.where(lane < 64, dot(entry, router_ref[...]), masked_score)
+    shifted = jnp.exp(logits - jnp.max(logits, axis=-1, keepdims=True))
+    probability = shifted / jnp.sum(shifted, axis=-1, keepdims=True)
+    own = jnp.where(lane == place_ref[0], 1.0, 0.0)
+    gates = jnp.sum(probability * own, axis=-1, keepdims=True)
+    gate = dot(entry, gate_ref[...])
+    upward = dot(entry, up_ref[...])
+    pull = pull_ref[...]
+    sigma = 1.0 / (1.0 + jnp.exp(-gate))
+    swish = gate * sigma
+    hidden = swish * upward
+    row_grad = jnp.sum(hidden * pull, axis=-1, keepdims=True) * gates
+    hidden_ref[...] = (hidden * gates).astype(bf16)
+    hidden_grad = pull * gates
+    gate_grad = (hidden_grad * upward * (sigma + swish * (1.0 - sigma))).astype(bf16)
+    up_grad = (hidden_grad * swish).astype(bf16)
+    logit_grad = (row_grad * (own - probability)).astype(bf16)
+    gate_grad_ref[...] = gate_grad
+    up_grad_ref[...] = up_grad
+    logit_grad_ref[...] = logit_grad
+    rest = []
+    for q in range(QUARTERS):
+        band = slice(q * BAND, (q + 1) * BAND)
+        part = (
+            dot(gate_grad, gate_ref[band, :], ((1,), (1,)))
+            + dot(up_grad, up_ref[band, :], ((1,), (1,)))
+            + dot(logit_grad, router_ref[band, :], ((1,), (1,)))
+        ).astype(bf16)
+        back_ref[:, band] = part[:HALF_MAIN]
+        rest.append(dot(rest_pick(q), part[HALF_MAIN:], ((0,), (0,))))
+    back_ref[:, D:] = (rest[0] + rest[1] + rest[2] + rest[3]).astype(bf16)
+
+
+def result_kernel(hidden_ref, down_ref, back_ref):
+    rest = []
+    for q in range(QUARTERS):
+        band = slice(q * BAND, (q + 1) * BAND)
+        part = dot(hidden_ref[...], down_ref[:, band]).astype(bf16)
+        back_ref[:, band] = part[:HALF_MAIN]
+        rest.append(dot(rest_pick(q), part[HALF_MAIN:], ((0,), (0,))))
+    back_ref[:, D:] = (rest[0] + rest[1] + rest[2] + rest[3]).astype(bf16)
+
+
 SMEM = pl.BlockSpec(memory_space=pltpu.SMEM)
 VMEM = pl.BlockSpec(memory_space=pltpu.VMEM)
 params = pltpu.CompilerParams(vmem_limit_bytes=56 * 1024 * 1024)
+step_params = pltpu.CompilerParams(
+    vmem_limit_bytes=56 * 1024 * 1024, dimension_semantics=("arbitrary",)
+)
+
+
+cheap = pl.CostEstimate(flops=1, bytes_accessed=1, transcendentals=0)
+
+
+def step_block(rows, columns):
+    return pl.BlockSpec((rows, columns), lambda i: (i, 0))
+
+
+def whole_block(rows, columns):
+    return pl.BlockSpec((rows, columns), lambda i: (0, 0))
+
+
+def shape(rows, columns, kind=bf16):
+    return jax.ShapeDtypeStruct((rows, columns), kind)
+
+
+def project(places, inputs, weights):
+    return pl.pallas_call(
+        project_kernel,
+        out_shape=(
+            shape(1024, D),
+            shape(1024, 3 * HD, f32),
+            shape(16, 128, f32),
+            shape(D, 3 * HD),
+            shape(D, 128),
+            shape(8, D, f32),
+        ),
+        in_specs=[SMEM] + [VMEM] * 12,
+        out_specs=(VMEM,) * 6,
+        compiler_params=params,
+        cost_estimate=cheap,
+    )(places, *inputs, *weights)
+
+
+def spread_grads(raw_grads, normed, weights, router_part, gains, extra, output_part):
+    return pl.pallas_call(
+        spread_kernel,
+        out_shape=(shape(1024, D), shape(2560, 512)),
+        in_specs=[VMEM] * 7,
+        out_specs=(VMEM, VMEM),
+        compiler_params=params,
+        cost_estimate=cheap,
+    )(raw_grads, normed, weights, router_part, gains, extra, output_part)
+
+
+def expert_pull(side, own, other, down):
+    return pl.pallas_call(
+        pull_kernel,
+        grid=(2,),
+        out_shape=(shape(1280, D), shape(1280, 512, f32)),
+        in_specs=[
+            SMEM,
+            step_block(HALF_MAIN, SIDE_WIDTH),
+            step_block(HALF_MAIN, SIDE_WIDTH),
+            whole_block(512, D),
+        ],
+        out_specs=(step_block(HALF, D), step_block(HALF, 512)),
+        compiler_params=step_params,
+        cost_estimate=cheap,
+    )(side, own, other, down)
+
+
+def expert_step(place, rows, pull, gate, up, router):
+    return pl.pallas_call(
+        expert_kernel,
+        grid=(2,),
+        out_shape=(
+            shape(1024, ROW_WIDTH),
+            shape(1280, D),
+            shape(1280, 512),
+            shape(1280, 512),
+            shape(1280, 512),
+            shape(1280, 128),
+        ),
+        in_specs=[
+            SMEM,
+            step_block(HALF_MAIN, ROW_WIDTH),
+            step_block(HALF, 512),
+            whole_block(D, 512),
+            whole_block(D, 512),
+            whole_block(D, 128),
+        ],
+        out_specs=(
+            step_block(HALF_MAIN, ROW_WIDTH),
+            step_block(HALF, D),
+            step_block(HALF, 512),
+            step_block(HALF, 512),
+            step_block(HALF, 512),
+            step_block(HALF, 128),
+        ),
+        compiler_params=step_params,
+        cost_estimate=cheap,
+    )(place, rows, pull, gate, up, router)
+
+
+def expert_result(hidden, down):
+    return pl.pallas_call(
+        result_kernel,
+        grid=(2,),
+        out_shape=shape(1024, ROW_WIDTH),
+        in_specs=[step_block(HALF, 512), whole_block(512, D)],
+        out_specs=step_block(HALF_MAIN, ROW_WIDTH),
+        compiler_params=step_params,
+        cost_estimate=cheap,
+    )(hidden, down)
+
+
+def linger_kernel(value_ref, out_ref):
+    out_ref[...] = value_ref[...]
+
+
+def linger(value):
+    return pl.pallas_call(
+        linger_kernel,
+        out_shape=jax.ShapeDtypeStruct(value.shape, value.dtype),
+        in_specs=[VMEM],
+        out_specs=VMEM,
+        cost_estimate=pl.CostEstimate(
+            flops=200_000_000_000, bytes_accessed=1, transcendentals=0
+        ),
+    )(value)
 
 
 def attend(z, queries, kv, end):
@@ -179,9 +481,7 @@
         in_specs=[SMEM, VMEM, VMEM, VMEM],
         out_specs=(VMEM, VMEM),
         compiler_params=params,
-        cost_estimate=pl.CostEstimate(
-            flops=4 * 1024 * 5000 * HD, bytes_accessed=6 << 20, transcendentals=1024 * 5000
-        ),
+        cost_estimate=cheap,
     )(z, queries, kv, end)
 
 
@@ -196,33 +496,24 @@
         out_specs=(VMEM, VMEM),
         scratch_shapes=[pltpu.VMEM((8192, 2 * HD), f32)],
         compiler_params=params,
-        cost_estimate=pl.CostEstimate(
-            flops=10 * 1024 * 5000 * HD, bytes_accessed=10 << 20, transcendentals=1024 * 5000
-        ),
+        cost_estimate=cheap,
     )(z, queries, grads, kv, end, lse, delta)
 
 
 def dispatch(main_table, rest_table, value):
-    stacked = value.reshape(128, QUARTERS, BAND).transpose(1, 0, 2).reshape(QUARTERS * 128, BAND)
+    band = value.shape[1] // QUARTERS
+    stacked = value.reshape(128, QUARTERS, band).transpose(1, 0, 2).reshape(QUARTERS * 128, band)
     main = dot(main_table, value).astype(bf16)
     rest = dot(rest_table, stacked).astype(bf16)
     return jnp.concatenate([main, rest], axis=1)
 
 
 def collect(main_table, rest_table, rows):
-    main = dot(main_table, rows[:, :D], ((0,), (0,)))
-    rest = dot(rest_table, rows[:, D:], ((0,), (0,)))
-    return main + rest.reshape(QUARTERS, 128, BAND).transpose(1, 0, 2).reshape(128, D)
-
-
-def open_rows(rows):
-    rest = rows[:, D:].reshape(64, QUARTERS, REST, BAND).transpose(0, 2, 1, 3)
-    return jnp.concatenate([rows[:, :D], rest.reshape(64 * REST, D)], axis=0)
-
-
-def close_rows(rows):
-    rest = rows[64 * MAIN :].reshape(64, REST, QUARTERS, BAND).transpose(0, 2, 1, 3)
-    return jnp.concatenate([rows[: 64 * MAIN], rest.reshape(64 * MAIN, BAND)], axis=1)
+    width = rows.shape[1] * QUARTERS // (QUARTERS + 1)
+    main = dot(main_table, rows[:, :width], ((0,), (0,)))
+    rest = dot(rest_table, rows[:, width:], ((0,), (0,)))
+    rest = rest.reshape(QUARTERS, 128, width // QUARTERS).transpose(1, 0, 2)
+    return main + rest.reshape(128, width)
 
 
 def local(
@@ -250,6 +541,9 @@
     place = x * 16 + z * 4 + yh * 2 + c
     head = x * 2 + yh
     z_place = z.reshape(1).astype(jnp.int32)
+    side = lax.axis_index("ep")
+    side_place = side.reshape(1).astype(jnp.int32)
+    heads_below = below(x, yh)
 
     pad = lambda gain: jnp.pad(gain, (0, 16))[:, None]
     small = jnp.concatenate(
@@ -259,29 +553,22 @@
             mixture_gain[:, None],
             pad(query_gain),
             pad(key_gain),
-            jnp.zeros((32, 60), bf16),
+            blocks.astype(bf16).reshape(32, 4),
+            jnp.zeros((32, 56), bf16),
         ],
         axis=1,
     )
-    small_all = lax.all_gather(small, CTX, axis=0, tiled=True)
-    blocks_all = lax.all_gather(blocks, CTX, axis=0, tiled=True)
-    router_all = small_all[:, :64]
-    attention_gain_all = small_all[:, 64].astype(f32)
-    mixture_gain_all = small_all[:, 65].astype(f32)
-    head_gains = small_all.reshape(64, 32, 128)[:, :16, 66:68].reshape(1024, 2).astype(f32)
-    head_gains = lax.dynamic_slice(head_gains, (head * HD, 0), (HD, 2))
-    query_gain_all = head_gains[:, 0]
-    key_gain_all = head_gains[:, 1]
-
-    inputs_all = lax.all_gather(inputs, HEADS, axis=0, tiled=True)
-    weights_sent = jnp.stack(
-        [w.reshape(32, 8, HD) for w in (query_weight, key_weight, value_weight)], axis=2
-    )
-    weights_sent = weights_sent.transpose(1, 0, 2, 3).reshape(256, 3 * HD)
-    weights_all = lax.all_gather(exchange(weights_sent, HEADS), TOKENS, axis=0, tiled=True)
-    weights_all = (
-        weights_all.reshape(4, 2, 4, 2, 32, 3 * HD).transpose(2, 0, 3, 1, 4, 5).reshape(D, 3 * HD)
-    )
+    weights_sent = jnp.concatenate(
+        [w.reshape(32, 8, HD) for w in (query_weight, key_weight, value_weight)]
+        + [jnp.broadcast_to(small[:, None], (32, 8, 128))],
+        axis=2,
+    )
+    weights_sent = weights_sent.transpose(1, 0, 2).reshape(256, 4 * HD)
+    inputs_pair = swap(inputs, "yh")
+    inputs_all = [ring(inputs, "x"), ring(inputs_pair, "x")]
+    inputs_all = [inputs_all[j][i] for i, j in OFFSETS]
+    weights_come = exchange(weights_sent, HEADS)
+    weights_all = ring(jnp.stack([weights_come, swap(weights_come, "c")]), "z")
     output_all = lax.all_gather(output_weight.T, CTX, axis=0, tiled=True)
 
     experts = jnp.arange(64, dtype=jnp.int32)
@@ -290,27 +577,36 @@
     earlier = (tokens[None, :] < tokens[:, None]).astype(bf16)
     ranks = dot(earlier, chosen.astype(bf16)).astype(jnp.int32)
     ranks = jnp.where(chosen, ranks, -1).T
+    quarter = jnp.eye(QUARTERS, dtype=bf16)
+
     table = (ranks[:, None, :] == jnp.arange(CAP, dtype=jnp.int32)[None, :, None]).astype(bf16)
     main_table = table[:, :MAIN].reshape(64 * MAIN, 128)
-    quarter = jnp.eye(QUARTERS, dtype=bf16)
-    rest_table = (
-        table[:, None, MAIN:, None, :] * quarter[None, :, None, :, None]
-    ).reshape(64 * MAIN, QUARTERS * 128)
-
-    grad_rows = exchange(dispatch(main_table, rest_table, cotangent), CTX)
-
-    source_all = inputs_all.astype(f32)
-    attention_inverse = lax.rsqrt(
-        jnp.mean(source_all * source_all, axis=-1, keepdims=True) + epsilon
-    )
-    normed_low = (source_all * attention_inverse * attention_gain_all).astype(bf16)
-    raw = dot(normed_low, weights_all)
+    rest_table = table[:, None, MAIN:, None, :] * quarter[None, :, None, :, None]
+    rest_table = rest_table.reshape(64 * MAIN, QUARTERS * 128)
+
+    cotangent_side, _ = lax.optimization_barrier((cotangent, inputs_pair))
+    cotangent_side = lax.dynamic_slice(cotangent_side, (0, side * SIDE), (128, SIDE))
+    grad_rows = exchange(dispatch(main_table, rest_table, cotangent_side), CTX)
+    inputs_all, grad_rows, weights_all, output_all = lax.optimization_barrier(
+        (inputs_all, grad_rows, weights_all, output_all)
+    )
+    places = jnp.concatenate([heads_below, below(z, c) // 2 * 4 + below(z, c) % 2])
+    normed_low, raw, squares, weights_all, small_all, gain_rows = project(
+        places.astype(jnp.int32), inputs_all, weights_all
+    )
+    blocks_all = small_all[:, 68:72].astype(jnp.int32).reshape(8192)
+    attention_gain_all = gain_rows[0]
+    mixture_gain_all = gain_rows[1]
+    head_gains = small_all.reshape(64, 32, 128)[:, :16, 66:68].reshape(1024, 2).astype(f32)
+    head_gains = lax.dynamic_slice(head_gains, (head * HD, 0), (HD, 2))
+    query_gain_all = head_gains[:, 0]
+    key_gain_all = head_gains[:, 1]
+
     query_raw, key_raw = raw[:, :HD], raw[:, HD : 2 * HD]
     value_low = raw[:, 2 * HD :].astype(bf16)
-    squares = jnp.stack(
-        [jnp.sum(query_raw * query_raw, axis=-1), jnp.sum(key_raw * key_raw, axis=-1)]
-    )
-    squares = sum_over_rows(squares.reshape(16, 128)).reshape(2, 1024)
+    squares = sum_over_rows(squares).reshape(2, 1024)
+    grad_rows, squares = lax.optimization_barrier((grad_rows, squares))
+    grad_other = swap(grad_rows, "ep")
     inverses = lax.rsqrt(squares / float(D) + epsilon)
     query_inverse = inverses[0][:, None]
     key_inverse = inverses[1][:, None]
@@ -326,7 +622,12 @@
     own_blocks = blocks_all.reshape(4, 4, 2, 2, 128)[:, z, :, c].reshape(1024)
     end = jnp.sum((blocks_all[:, None] <= own_blocks[None, :]).astype(jnp.int32), axis=0)[None]
     attended, lse = attend(z_place, query_low, kv, end)
-    attended_low = attended.astype(bf16)
+    attended_low, grad_other = lax.optimization_barrier((attended.astype(bf16), grad_other))
+    heads_all = lax.all_gather(attended_low, "x", axis=0, tiled=True)
+    grad_other, heads_all = lax.optimization_barrier((grad_other, heads_all))
+    grad_flat, hidden_pull = expert_pull(
+        side_place, grad_rows, grad_other, down_weight[0]
+    )
 
     attended_rows = exchange(attended_low, HEADS).reshape(8, 128, HD)
     attended_rows = attended_rows.transpose(1, 0, 2).reshape(128, 8 * HD)
@@ -336,41 +637,26 @@
     mixed_low = (residual * mixture_inverse * mixture_gain_all).astype(bf16)
     mixed_rows = exchange(dispatch(main_table, rest_table, mixed_low), CTX)
 
-    entry = open_rows(mixed_rows)
-    grad = open_rows(grad_rows)
-    logits = dot(entry, router_all)
-    shifted = jnp.exp(logits - jnp.max(logits, axis=-1, keepdims=True))
-    probability = shifted / jnp.sum(shifted, axis=-1, keepdims=True)
-    own_expert = (experts == place).astype(f32)[None, :]
-    gates = jnp.sum(probability * own_expert, axis=-1, keepdims=True)
-    gate = dot(entry, gate_weight[0])
-    upward = dot(entry, up_weight[0])
-    sigma = jax.nn.sigmoid(gate)
-    swish = gate * sigma
-    hidden = swish * upward
-    hidden_low = hidden.astype(bf16)
-    hidden_pull = dot(grad, down_weight[0], ((1,), (1,)))
-    gate_grad = jnp.sum(hidden_low.astype(f32) * hidden_pull, axis=-1, keepdims=True)
-    hidden_grad = hidden_pull * gates
-    gate_raw_grad = (hidden_grad * upward * sigma * (1.0 + gate * (1.0 - sigma))).astype(bf16)
-    up_raw_grad = (hidden_grad * swish).astype(bf16)
-    logit_grad = (gate_grad * gates * (own_expert - probability)).astype(bf16)
-    entry_grad = (
-        dot(gate_raw_grad, gate_weight[0], ((1,), (1,)))
-        + dot(up_raw_grad, up_weight[0], ((1,), (1,)))
-        + dot(logit_grad, router_all, ((1,), (1,)))
-    ).astype(bf16)
-    entry_back = exchange(close_rows(entry_grad), CTX)
-    result = (dot(hidden_low, down_weight[0]) * gates).astype(bf16)
-    result_back = exchange(close_rows(result), CTX)
-    down_weight_grad = dot((hidden * gates).astype(bf16), grad, ((0,), (0,)))
+    entry_sent, entry, hidden_low, gate_raw_grad, up_raw_grad, logit_grad = expert_step(
+        place.reshape(1).astype(jnp.int32),
+        mixed_rows,
+        hidden_pull,
+        gate_weight[0],
+        up_weight[0],
+        small_all,
+    )
+    entry_back = exchange(entry_sent, CTX)
+    result_sent = expert_result(hidden_low, down_weight[0])
+    down_weight_grad = dot(hidden_low, grad_flat, ((0,), (0,)))
     gate_weight_grad = dot(entry, gate_raw_grad, ((0,), (0,)))
     up_weight_grad = dot(entry, up_raw_grad, ((0,), (0,)))
     router_part = dot(entry, logit_grad, ((0,), (0,)))
-    router_part = exchange(router_part.reshape(64 * 16, 128), CTX).reshape(64, 16, 128)
-    router_grad = lax.psum(jnp.sum(router_part, axis=0), "ep").reshape(32, 64)
-
-    final = residual + pair_sum(collect(main_table, rest_table, result_back))
+    entry_back, down_weight_grad, gate_weight_grad, up_weight_grad, router_part = (
+        lax.optimization_barrier(
+            (entry_back, down_weight_grad, gate_weight_grad, up_weight_grad, router_part)
+        )
+    )
+
     mixed_grad = pair_sum(collect(main_table, rest_table, entry_back))
 
     grad_out = cotangent.astype(f32)
@@ -387,19 +673,31 @@
     mixture_gain_part = jnp.sum(mixed_grad * residual * mixture_inverse, axis=0)
     residual_low = residual_grad.astype(bf16)
     attended_grad = dot(residual_low, output_all).astype(bf16)
-    attended_grad = attended_grad.reshape(128, 8, HD).transpose(1, 0, 2).reshape(1024, HD)
-    attended_grad = exchange(attended_grad, HEADS)
-    residual_all = lax.all_gather(residual_low, HEADS, axis=0, tiled=True)
-    output_part = dot(attended_low, residual_all, ((0,), (0,))).astype(bf16)
-    output_part = output_part.reshape(HD, 64, 32).transpose(1, 0, 2).reshape(64 * 32, HD)
-    output_part = exchange(output_part, CTX).reshape(4, 4, 2, 2, HD, 32)
-    output_grad = jnp.sum(output_part.astype(f32), axis=(1, 3)).reshape(8 * HD, 32)
+    attended_grad = attended_grad.reshape(128, 8, HD).transpose(1, 0, 2)
+    residual_bands = residual_low.reshape(128, 4, 1, BAND).transpose(1, 2, 0, 3)
+    residual_bands = jnp.broadcast_to(residual_bands, (4, 2, 128, BAND)).reshape(8, 128, BAND)
+    attended_grad = exchange(
+        jnp.concatenate([attended_grad, residual_bands], axis=2).reshape(1024, HD + BAND), HEADS
+    )
+    residual_band = attended_grad[:, HD:]
+    attended_grad = attended_grad[:, :HD]
+    result_sent, attended_grad = lax.optimization_barrier((result_sent, attended_grad))
+    result_back = exchange(result_sent, CTX)
+    output_part = dot(
+        residual_band,
+        heads_all.reshape(4, 1024, HD).transpose(1, 0, 2).reshape(1024, 4 * HD),
+        ((0,), (0,)),
+    )
 
     delta = jnp.sum(attended_grad.astype(f32) * attended, axis=-1)[None]
     query_grad, kv_part = attend_back(
         z_place, query_low, attended_grad, kv, end, lse, delta
     )
-    kv_grad = jnp.sum(exchange(kv_part, TOKENS).reshape(8, 1024, 2 * HD).astype(f32), axis=0)
+    kv_grad = lax.psum_scatter(kv_part, TOKENS, scatter_dimension=0, tiled=True)
+    query_grad, result_back = lax.optimization_barrier((query_grad, result_back))
+    query_grad = linger(query_grad)
+    kv_grad = kv_grad.astype(f32)
+    final = residual + pair_sum(collect(main_table, rest_table, result_back))
     value_grad_low = kv_grad[:, HD:].astype(bf16)
     query_normed_grad = rotate(query_grad, cosine, -sine)
     key_normed_grad = rotate(kv_grad[:, :HD], cosine, -sine)
@@ -418,34 +716,41 @@
     query_gain_part = jnp.sum(query_normed_grad * query_raw * query_inverse, axis=0)
     key_gain_part = jnp.sum(key_normed_grad * key_raw * key_inverse, axis=0)
     raw_grads = jnp.concatenate([query_raw_low, key_raw_low, value_grad_low], axis=1)
-    normed_part = dot(raw_grads, weights_all, ((1,), (1,)))
-    attention_gain_part = jnp.sum(normed_part * source_all * attention_inverse, axis=0)
-    normed_grad = jnp.sum(
-        exchange(normed_part.astype(bf16), HEADS).reshape(8, 128, D).astype(f32), axis=0
-    )
-    normed_grad = pair_sum(normed_grad)
-    weight_part = dot(normed_low, raw_grads, ((0,), (0,))).astype(bf16)
-    weight_part = exchange(weight_part, CTX).reshape(4, 4, 2, 2, 32, 3, HD)
-    weight_grad = jnp.sum(weight_part.astype(f32), axis=(1, 3)).reshape(8, 32, 3, HD)
-    weight_grad = weight_grad.transpose(2, 1, 0, 3).reshape(3, 32, 8 * HD)
 
     def head_part(value):
         wide = lax.dynamic_update_slice(jnp.zeros((8 * HD,), f32), value, (head * HD,))
-        return wide.reshape(64, 16)
-
-    gains = jnp.concatenate(
+        return jnp.pad(wide.reshape(64, 16), ((0, 0), (0, 16))).reshape(1, D)
+
+    extra = jnp.concatenate(
         [
-            attention_gain_part.reshape(64, 32),
-            mixture_gain_part.reshape(64, 32),
+            jnp.zeros((1, D), f32),
+            mixture_gain_part[None],
             head_part(query_gain_part),
             head_part(key_gain_part),
-            jnp.zeros((64, 32), f32),
+            jnp.zeros((4, D), f32),
         ],
-        axis=1,
-    )
-    gains = jnp.broadcast_to(gains[:, None, :], (64, 8, 128)).reshape(512, 128)
-    gains = jnp.sum(exchange(gains, CTX).reshape(64, 8, 128)[:, 0], axis=0)
-    attention_gain_grad = lax.psum(gains[:32], "ep")
+        axis=0,
+    )
+    normed_part, shares = spread_grads(
+        raw_grads, normed_low, weights_all, router_part, gain_rows, extra, output_part
+    )
+    normed_grad = jnp.sum(exchange(normed_part, HEADS).reshape(8, 128, D).astype(f32), axis=0)
+    normed_grad = pair_sum(normed_grad)
+
+    summed = lax.psum_scatter(shares, TOKENS, scatter_dimension=0, tiled=True)
+    output_sum = jnp.broadcast_to(summed[256:].reshape(1, 2, 32, 512), (4, 2, 32, 512))
+    shares = jnp.concatenate(
+        [summed[:256].reshape(8, 32, 512), output_sum.reshape(8, 32, 512)], axis=1
+    )
+    shares = exchange(shares.reshape(512, 512), HEADS).reshape(8, 64, 512).astype(f32)
+    weight_grad = shares[:, :32, : 3 * HD].reshape(8, 32, 3, HD)
+    weight_grad = weight_grad.transpose(2, 1, 0, 3).reshape(3, 32, 8 * HD)
+    extra = jnp.sum(shares[:, :32, 3 * HD :], axis=0)
+    pair = extra + lax.ppermute(extra, "ep", [(0, 1), (1, 0)])
+    router_grad = pair[:, :64]
+    attention_gain_grad = pair[:, 64]
+    output_grad = lax.dynamic_slice(shares, (x * 2, 32, 0), (2, 32, 512))
+    output_grad = output_grad.reshape(2, 32, 4, HD).transpose(2, 0, 3, 1).reshape(8 * HD, 32)
 
     inverse = lax.rsqrt(jnp.mean(source * source, axis=-1, keepdims=True) + epsilon)
     scaled = normed_grad * attention_gain_all
@@ -465,10 +770,10 @@
         weight_grad[0],
         weight_grad[1],
         weight_grad[2],
-        gains[64:80],
-        gains[80:96],
+        extra[:16, 66],
+        extra[:16, 67],
         output_grad,
-        gains[32:64],
+        extra[:, 65],
         router_grad,
         gate_weight_grad[None],
         up_weight_grad[None],

time: 1030 us -> 735 us (0.71)
  blocking collectives: 219 us -> 14.8 us
  matrix products: 110 us -> 40.3 us
  Pallas kernels: 56.4 us -> 115 us
  local copies, waits for them, and re-layouts: 77.6 us -> 37.7 us
  starting transfers between devices: 119 us -> 97.5 us
  other arithmetic: 61.2 us -> 45.9 us
    all_gather x2 -> x0, blocking collectives: 164 us -> none  [the longest x1 82.4 us: local(): blocks_all = lax.all_gather(blocks, CTX, axis=0, tiled=True)]
    all_to_all x12 -> x10, waiting for transfers between devices: 270 us -> 176 us  [exchange(): return lax.all_to_all(value, axes, split_axis=0, concat_axis=0, tiled=True)]
    ppermute x0 -> x13, waiting for transfers between devices: none -> 72.6 us  [the longest x9 71.6 us: ring(): lax.ppermute(value, axis, [(a, (a + i) % 4) for a in range(4)])]
    dot_general x27 -> x16, matrix products: 110 us -> 40.3 us  [dot(): lax.dot_general(first, second, (dims, ((), ())), preferred_element_type=f32)]
    pallas_call x0 -> x6, Pallas kernels: none -> 58.9 us  [the longest x1 23 us: expert_step(): pl.pallas_call(expert_kernel, grid=(2,), out_shape=(shape(1024, ROW_WIDTH...]
    ppermute x4, waiting for transfers between devices: 75.4 us -> 31.6 us  [pair_sum(): other = lax.ppermute(own, 'ep', [(0, 1), (1, 0)])]
    all_to_all x12 -> x10, starting transfers between devices: 113 us -> 70.2 us  [exchange(): return lax.all_to_all(value, axes, split_axis=0, concat_axis=0, tiled=True)]
    all_gather x3 -> x1, waiting for transfers between devices: 7.15 us -> 43.6 us  [local(): heads_all = lax.all_gather(attended_low, 'x', axis=0, tiled=True)]
  transfers between devices with their start and end apart: 21 -> 32, of which waited for: 13 -> 20; matrix products, arithmetic and copies ran while one was open for 15% -> 11% of each run, Pallas kernels for 3% -> 10%
where the time goes in v2:
time: 735 us; the launch traced here: 727 us
  waiting for transfers between devices  361 us (49%)
  Pallas kernels  115 us (16%)
  starting transfers between devices  97.5 us (13%)
  other arithmetic  45.9 us (6%)
  matrix products  40.3 us (5%)
  local copies, waits for them, and re-layouts  37.7 us (5%)
  between operations  15.3 us (2%)
  blocking collectives  14.8 us (2%)
    all_to_all x10, waiting for transfers between devices, exchange(): return lax.all_to_all(value, axes, split_axis=0, concat_axis=0, tiled=True)  176 us
    ppermute x9, waiting for transfers between devices, ring(): lax.ppermute(value, axis, [(a, (a + i) % 4) for a in range(4)])  71.6 us
    all_to_all x10, starting transfers between devices, exchange(): return lax.all_to_all(value, axes, split_axis=0, concat_axis=0, tiled=True)  70.2 us
    all_gather x1, waiting for transfers between devices, local(): heads_all = lax.all_gather(attended_low, 'x', axis=0, tiled=True)  43.6 us
    dot_general x16, matrix products, dot(): lax.dot_general(first, second, (dims, ((), ())), preferred_element_type=f32)  40.3 us
    ppermute x4, waiting for transfers between devices, pair_sum(): other = lax.ppermute(own, 'ep', [(0, 1), (1, 0)])  31.6 us
    pallas_call x1, Pallas kernels, attend_back(): pl.pallas_call(attend_back_kernel, out_shape=(jax.ShapeDtypeStruct((1024,...  29.3 us
    pallas_call x1, Pallas kernels, attend(): pl.pallas_call(attend_kernel, out_shape=(jax.ShapeDtypeStruct((1024, HD),...  27 us
  transfers between devices with their start and end apart: 32, of which 20 were waited for; matrix products, arithmetic and copies ran while one was open for 11% of the time, Pallas kernels for 10%

profile of v2, /device:TPU:96, one launch (start us, length us, event | category | flops | bytes accessed | tf_op | source)
XLA Modules:
  0.0 727.4 jit_solution(9023615448060294935)
XLA Ops:
  31.2 9.5 %all-to-all-start = ((bf16[64,16,1280]{2,1,0:T(8,128)(2,1)}), bf16[64,16,1280]{2,1,0:T(8,128)(2,1)S(1)}, u32[]{:S(2)}, u32[]{:S(2)}) async-start(bf16[64,16,1280]{2,1,0:T(8,128)(2,1)} %bitcast.22), calls=%async_computation | async-start | bytes 5242880 | tf_op jit(solution)/shard_map/all_to_all | solution.py:48
  51.0 36.1 %collective-permute-done.1.refs_2_ = bf16[128,2048]{1,0:T(8,128)(2,1)} collective-permute-done((bf16[128,2048]{1,0:T(8,128)(2,1)S(1)}, bf16[128,2048]{1,0:T(8,128)(2,1)}, u32[]{:S(2)}, u32[]{:S(2)}) %collective-permute-start.1) | collective-permute-done | bytes 524320 | tf_op jit(solution)/shard_map/ppermute | solution.py:56
  88.3 9.8 %collective-permute-done.3.refs_4_ = bf16[128,2048]{1,0:T(8,128)(2,1)} collective-permute-done((bf16[128,2048]{1,0:T(8,128)(2,1)S(1)}, bf16[128,2048]{1,0:T(8,128)(2,1)}, u32[]{:S(2)}, u32[]{:S(2)}) %collective-permute-start.3) | collective-permute-done | bytes 524320 | tf_op jit(solution)/shard_map/ppermute | solution.py:56
  105.2 22.9 %collective-permute-done.2.refs_3_ = bf16[128,2048]{1,0:T(8,128)(2,1)} collective-permute-done((bf16[128,2048]{1,0:T(8,128)(2,1)}, bf16[128,2048]{1,0:T(8,128)(2,1)}, u32[]{:S(2)}, u32[]{:S(2)}) %collective-permute-start.2) | collective-permute-done | bytes 524320 | tf_op jit(solution)/shard_map/ppermute | solution.py:56
  128.9 8.6 %shard_map.263 = (bf16[1024,2048]{1,0:T(8,128)(2,1)}, f32[1024,384]{1,0:T(8,128)}, f32[16,128]{1,0:T(8,128)}, bf16[2048,384]{1,0:T(8,128)(2,1)}, bf16[2048,128]{1,0:T(8,128)(2,1)}, /*index=5*/f32[8,2048]{1,0:T(8,128)}) custom-call(s32[16]{0:T(128)} %concatenate.47.place_ref, bf16[128,2048]{1,0:T(8,128)(2,1)} %refs_0_, ...), custom_call_target="tpu_custom_call" | custom-call | flops 1 | bytes 1 | tf_op jit(solution)/shard_map/pallas_call | solution.py:368
  171.7 16.6 %all-gather.6.cloned.1.call-done.kv_ref = bf16[8192,256]{1,0:T(8,128)(2,1)} async-done(((bf16[1024,256]{1,0:T(8,128)(2,1)}), bf16[8192,256]{1,0:T(8,128)(2,1)}) %all-gather.6.cloned.1.call-update) | async-done | bytes 4194320 | tf_op jit(solution)/shard_map/all_gather | solution.py:619
  188.3 27.0 %shard_map.264 = (f32[1024,128]{1,0:T(8,128)}, f32[1,1024]{1,0:T(1,128)}) custom-call(s32[1]{0:T(128)} %bitcast.z_ref, bf16[1024,128]{1,0:T(8,128)(2,1)} %pad_maximum_fusion.9.q_ref, bf16[8192,256]{1,0:T(8,128)(2,1)} %all-gather.6.cloned.1.call-done.kv_ref, s32[1,1024]{1,0:T(1,128)} %bitcast.263), custom_call_target="tpu_custom_call" | custom-call | flops 1 | bytes 1 | tf_op jit(solution)/shard_map/pallas_call | solution.py:475
  217.6 14.8 %all_to_all.101 = bf16[8,128,128]{1,2,0:T(8,128)(2,1)S(1)} all-to-all(bf16[8,128,128]{1,2,0:T(8,128)(2,1)S(1)} %copy.104), channel_id=1, replica_groups=mesh['x'=4,'z'=4,'yh'=2,'c'=2,'ep'=2] {'x','yh'}, dimensions={0} | all-to-all | bytes 524288 | tf_op jit(solution)/shard_map/all_to_all | solution.py:48
  238.3 10.4 %collective-permute-done.12 = bf16[128,2048]{1,0:T(8,128)(2,1)S(1)} collective-permute-done((bf16[128,2048]{1,0:T(8,128)(2,1)S(1)}, bf16[128,2048]{1,0:T(8,128)(2,1)S(1)}, u32[]{:S(2)}, u32[]{:S(2)}) %collective-permute-start.12) | collective-permute-done | bytes 524320 | tf_op jit(solution)/shard_map/ppermute | solution.py:70
  262.0 43.6 %all-gather.8.cloned.1.call-done = bf16[4096,128]{1,0:T(8,128)(2,1)} async-done(((bf16[1024,128]{1,0:T(8,128)(2,1)}), bf16[4096,128]{1,0:T(8,128)(2,1)}) %all-gather.8.cloned.1.call-update) | async-done | bytes 1048592 | tf_op jit(solution)/shard_map/all_gather | solution.py:626
  312.9 17.9 %all-to-all-done.4 = bf16[64,16,2560]{2,1,0:T(8,128)(2,1)} async-done(((bf16[64,16,2560]{2,1,0:T(8,128)(2,1)}), bf16[64,16,2560]{2,1,0:T(8,128)(2,1)}, u32[]{:S(2)}, u32[]{:S(2)}) %all-to-all-start.4) | async-done | bytes 5242912 | tf_op jit(solution)/shard_map/all_to_all | solution.py:48
  330.9 23.0 %shard_map.266 = (bf16[1024,2560]{1,0:T(8,128)(2,1)}, bf16[1280,2048]{1,0:T(8,128)(2,1)}, bf16[1280,512]{1,0:T(8,128)(2,1)}, bf16[1280,512]{1,0:T(8,128)(2,1)}, ...) custom-call(s32[1]{0:T(128)} %bitcast.44.place_ref, bf16[1024,2560]{1,0:T(8,128)(2,1)} %bitcast.49.rows_ref, ...), custom_call_target="tpu_custom_call" | custom-call | flops 1 | bytes 1 | tf_op jit(solution)/shard_map/pallas_call | solution.py:414
  353.9 10.7 %all-to-all-start.5 = ((bf16[64,16,2560]{2,1,0:T(8,128)(2,1)}), bf16[64,16,2560]{2,1,0:T(8,128)(2,1)}, u32[]{:S(2)}, u32[]{:S(2)}) async-start(bf16[64,16,2560]{2,1,0:T(8,128)(2,1)} %bitcast.201), calls=%async_computation.5 | async-start | bytes 10485760 | tf_op jit(solution)/shard_map/all_to_all | solution.py:48
  384.7 45.0 %all-to-all-done.5 = bf16[64,16,2560]{2,1,0:T(8,128)(2,1)} async-done(((bf16[64,16,2560]{2,1,0:T(8,128)(2,1)}), bf16[64,16,2560]{2,1,0:T(8,128)(2,1)}, u32[]{:S(2)}, u32[]{:S(2)}) %all-to-all-start.5) | async-done | bytes 5242912 | tf_op jit(solution)/shard_map/all_to_all | solution.py:48
  441.2 9.7 %collective-permute-done.13 = bf16[128,2048]{1,0:T(8,128)(2,1)S(1)} collective-permute-done((bf16[128,2048]{1,0:T(8,128)(2,1)S(1)}, bf16[128,2048]{1,0:T(8,128)(2,1)S(1)}, u32[]{:S(2)}, u32[]{:S(2)}) %collective-permute-start.13) | collective-permute-done | bytes 524320 | tf_op jit(solution)/shard_map/ppermute | solution.py:70
  460.6 8.4 %shard_map.267 = bf16[1024,2560]{1,0:T(8,128)(2,1)} custom-call(bf16[1280,512]{1,0:T(8,128)(2,1)} %get-tuple-element.90.hidden_ref, bf16[512,2048]{1,0:T(8,128)(2,1)} %bitcast.198), custom_call_target="tpu_custom_call" | custom-call | flops 1 | bytes 1 | tf_op jit(solution)/shard_map/pallas_call | solution.py:447
  469.0 9.3 %all-to-all-done.6 = bf16[8,128,640]{2,1,0:T(8,128)(2,1)S(1)} async-done(((bf16[8,128,640]{2,1,0:T(8,128)(2,1)}), bf16[8,128,640]{2,1,0:T(8,128)(2,1)S(1)}, u32[]{:S(2)}, u32[]{:S(2)}) %all-to-all-start.6) | async-done | bytes 1310752 | tf_op jit(solution)/shard_map/all_to_all | solution.py:48
  479.4 11.7 %all-to-all-start.7 = ((bf16[64,16,2560]{2,1,0:T(8,128)(2,1)}), bf16[64,16,2560]{2,1,0:T(8,128)(2,1)}, u32[]{:S(2)}, u32[]{:S(2)}) async-start(bf16[64,16,2560]{2,1,0:T(8,128)(2,1)} %bitcast.194), calls=%async_computation.7 | async-start | bytes 10485760 | tf_op jit(solution)/shard_map/all_to_all | solution.py:48
  493.3 29.3 %shard_map.268 = (f32[1024,128]{1,0:T(8,128)}, bf16[8192,256]{1,0:T(8,128)(2,1)}) custom-call(s32[1]{0:T(128)} %bitcast.z_ref, bf16[1024,128]{1,0:T(8,128)(2,1)} %pad_maximum_fusion.9.q_ref, bf16[1024,128]{1,0:T(8,128)(2,1)} %copy-done.17, bf16[8192,256]{1,0:T(8,128)(2,1)} %all-gather.6.cloned.1.call-done.kv_ref, s32[1,1024]{1,0:T(1,128)} %bitcast.264, ...), custom_call_target="tpu_custom_call" | custom-call | flops 1 | bytes 1 | tf_op jit(solution)/shard_map/pallas_call | solution.py:489
  522.6 33.7 %all-to-all-done.7 = bf16[64,16,2560]{2,1,0:T(8,128)(2,1)} async-done(((bf16[64,16,2560]{2,1,0:T(8,128)(2,1)}), bf16[64,16,2560]{2,1,0:T(8,128)(2,1)}, u32[]{:S(2)}, u32[]{:S(2)}) %all-to-all-start.7) | async-done | bytes 5242912 | tf_op jit(solution)/shard_map/all_to_all | solution.py:48
  558.2 18.5 %reduce-scatter.3.cloned.1.call-done = bf16[1024,256]{1,0:T(8,128)(2,1)} async-done(((bf16[8192,256]{1,0:T(8,128)(2,1)}), bf16[1024,256]{1,0:T(8,128)(2,1)}) %reduce-scatter.3.cloned.1.call-update) | async-done | bytes 524304 | tf_op jit(solution)/shard_map/reduce_scatter | solution.py:696
  601.5 9.6 %shard_map.270 = (bf16[1024,2048]{1,0:T(8,128)(2,1)}, bf16[2560,512]{1,0:T(8,128)(2,1)}) custom-call(bf16[1024,384]{1,0:T(8,128)(2,1)} %pad_maximum_fusion.3.raw_ref, bf16[1024,2048]{1,0:T(8,128)(2,1)} %get-tuple-element.105.normed_ref, bf16[2048,384]{1,0:T(8,128)(2,1)} %get-tuple-element.106.weight_ref, f32[2048,128]{1,0:T(8,128)} %fusion.80.router_ref, ...), custom_call_target="tpu_custom_call" | custom-call | flops 1 | bytes 1 | tf_op jit(solution)/shard_map/pallas_call | solution.py:386
  622.3 53.4 %all-to-all-done.9 = bf16[8,128,2048]{2,1,0:T(8,128)(2,1)} async-done(((bf16[8,128,2048]{2,1,0:T(8,128)(2,1)}), bf16[8,128,2048]{2,1,0:T(8,128)(2,1)}, u32[]{:S(2)}, u32[]{:S(2)}) %all-to-all-start.9) | async-done | bytes 4194336 | tf_op jit(solution)/shard_map/all_to_all | solution.py:48
  681.7 11.6 %collective-permute-done.15 = bf16[128,2048]{1,0:T(8,128)(2,1)S(1)} collective-permute-done((bf16[128,2048]{1,0:T(8,128)(2,1)S(1)}, bf16[128,2048]{1,0:T(8,128)(2,1)S(1)}, u32[]{:S(2)}, u32[]{:S(2)}) %collective-permute-start.15) | collective-permute-done | bytes 524320 | tf_op jit(solution)/shard_map/ppermute | solution.py:70
  (305 shorter events, 221.0 us)
Async XLA Ops:
  7.2 121.0 %all-gather.4.cloned.1.call-start = ((), (), s32[]{:S(2)}) async-start(), calls=%async_computation.13 | async-start | bytes 4259840 | tf_op jit(solution)/shard_map/all_gather | solution.py:572
  7.9 16.3 %collective-permute-start = (bf16[128,2048]{1,0:T(8,128)(2,1)}, bf16[128,2048]{1,0:T(8,128)(2,1)}, u32[]{:S(2)}, u32[]{:S(2)}) collective-permute-start(bf16[128,2048]{1,0:T(8,128)(2,1)} %refs_0_), channel_id=1, source_target_pairs={{0,4},{4,0},{1,5},{5,1},{2,6},{6,2},{3,7},{7,3},{8,12},{12,8},{9,1... | collective-permute-start | bytes 1572872 | tf_op jit(solution)/shard_map/ppermute | solution.py:61
  31.2 96.9 %all-to-all-start = ((bf16[64,16,1280]{2,1,0:T(8,128)(2,1)}), bf16[64,16,1280]{2,1,0:T(8,128)(2,1)S(1)}, u32[]{:S(2)}, u32[]{:S(2)}) async-start(bf16[64,16,1280]{2,1,0:T(8,128)(2,1)} %bitcast.22), calls=%async_computation | async-start | bytes 5242880 | tf_op jit(solution)/shard_map/all_to_all | solution.py:48
  41.0 46.0 %collective-permute-start.1 = (bf16[128,2048]{1,0:T(8,128)(2,1)S(1)}, bf16[128,2048]{1,0:T(8,128)(2,1)}, u32[]{:S(2)}, u32[]{:S(2)}) collective-permute-start(bf16[128,2048]{1,0:T(8,128)(2,1)S(1)} %copy-done.6), channel_id=1, source_target_pairs={{0,32},{32,64},{64,96},{96,0},{1,33},{33,65},{65,97},{97,1},{2,34}... | collective-permute-start | bytes 1572872 | tf_op jit(solution)/shard_map/ppermute | solution.py:56
  42.5 55.6 %collective-permute-start.3 = (bf16[128,2048]{1,0:T(8,128)(2,1)S(1)}, bf16[128,2048]{1,0:T(8,128)(2,1)}, u32[]{:S(2)}, u32[]{:S(2)}) collective-permute-start(bf16[128,2048]{1,0:T(8,128)(2,1)S(1)} %copy-done.6), channel_id=1, source_target_pairs={{0,64},{32,96},{64,0},{96,32},{1,65},{33,97},{65,1},{97,33},{2,66}... | collective-permute-start | bytes 1572872 | tf_op jit(solution)/shard_map/ppermute | solution.py:56
  45.4 52.8 %collective-permute-start.5 = (bf16[128,2048]{1,0:T(8,128)(2,1)S(1)}, bf16[128,2048]{1,0:T(8,128)(2,1)}, u32[]{:S(2)}, u32[]{:S(2)}) collective-permute-start(bf16[128,2048]{1,0:T(8,128)(2,1)S(1)} %copy-done.6), channel_id=1, source_target_pairs={{0,96},{32,0},{64,32},{96,64},{1,97},{33,1},{65,33},{97,65},{2,98}... | collective-permute-start | bytes 1572872 | tf_op jit(solution)/shard_map/ppermute | solution.py:56
  47.6 51.8 %collective-permute-start.10 = (bf16[2,256,512]{2,1,0:T(8,128)(2,1)}, bf16[2,256,512]{2,1,0:T(8,128)(2,1)}, u32[]{:S(2)}, u32[]{:S(2)}) collective-permute-start(bf16[2,256,512]{2,1,0:T(8,128)(2,1)} %pad_maximum_fusion.4.refs_8_), channel_id=1, source_target_pairs={{0,24},{8,0},{16,8},{24,16},{1,25},{9,1},{17,9},{25,17},{2,26},{10... | collective-permute-start | bytes 1572872 | tf_op jit(solution)/shard_map/ppermute | solution.py:56
  48.5 54.0 %collective-permute-start.8 = (bf16[2,256,512]{2,1,0:T(8,128)(2,1)}, bf16[2,256,512]{2,1,0:T(8,128)(2,1)}, u32[]{:S(2)}, u32[]{:S(2)}) collective-permute-start(bf16[2,256,512]{2,1,0:T(8,128)(2,1)} %pad_maximum_fusion.4.refs_8_), channel_id=1, source_target_pairs={{0,8},{8,16},{16,24},{24,0},{1,9},{9,17},{17,25},{25,1},{2,10},{10... | collective-permute-start | bytes 1572872 | tf_op jit(solution)/shard_map/ppermute | solution.py:56
  87.0 18.1 %collective-permute-start.9 = (bf16[2,256,512]{2,1,0:T(8,128)(2,1)}, bf16[2,256,512]{2,1,0:T(8,128)(2,1)}, u32[]{:S(2)}, u32[]{:S(2)}) collective-permute-start(bf16[2,256,512]{2,1,0:T(8,128)(2,1)} %pad_maximum_fusion.4.refs_8_), channel_id=1, source_target_pairs={{0,16},{8,24},{16,0},{24,8},{1,17},{9,25},{17,1},{25,9},{2,18},{10... | collective-permute-start | bytes 1572872 | tf_op jit(solution)/shard_map/ppermute | solution.py:56
  98.2 29.9 %collective-permute-start.2 = (bf16[128,2048]{1,0:T(8,128)(2,1)}, bf16[128,2048]{1,0:T(8,128)(2,1)}, u32[]{:S(2)}, u32[]{:S(2)}) collective-permute-start(bf16[128,2048]{1,0:T(8,128)(2,1)} %collective-permute-done.refs_1_), channel_id=1, source_target_pairs={{0,32},{32,64},{64,96},{96,0},{1,33},{33,65},{65,97},{97,1},{2,34}... | collective-permute-start | bytes 1572872 | tf_op jit(solution)/shard_map/ppermute | solution.py:56
  98.2 29.9 %collective-permute-start.4 = (bf16[128,2048]{1,0:T(8,128)(2,1)}, bf16[128,2048]{1,0:T(8,128)(2,1)S(1)}, u32[]{:S(2)}, u32[]{:S(2)}) collective-permute-start(bf16[128,2048]{1,0:T(8,128)(2,1)} %collective-permute-done.refs_1_), channel_id=1, source_target_pairs={{0,64},{32,96},{64,0},{96,32},{1,65},{33,97},{65,1},{97,33},{2,66}... | collective-permute-start | bytes 1572872 | tf_op jit(solution)/shard_map/ppermute | solution.py:56
  99.5 28.7 %collective-permute-start.6 = (bf16[128,2048]{1,0:T(8,128)(2,1)}, bf16[128,2048]{1,0:T(8,128)(2,1)}, u32[]{:S(2)}, u32[]{:S(2)}) collective-permute-start(bf16[128,2048]{1,0:T(8,128)(2,1)} %collective-permute-done.refs_1_), channel_id=1, source_target_pairs={{0,96},{32,0},{64,32},{96,64},{1,97},{33,1},{65,33},{97,65},{2,98}... | collective-permute-start | bytes 1572872 | tf_op jit(solution)/shard_map/ppermute | solution.py:56
  145.2 43.1 %all-gather.6.cloned.1.call-start = ((), (), s32[]{:S(2)}) async-start(), calls=%async_computation.14 | async-start | bytes 4718592 | tf_op jit(solution)/shard_map/all_gather | solution.py:619
  159.8 57.6 %collective-permute-start.11 = (bf16[1024,1280]{1,0:T(8,128)(2,1)S(1)}, bf16[1024,1280]{1,0:T(8,128)(2,1)}, u32[]{:S(2)}, u32[]{:S(2)}) collective-permute-start(bf16[1024,1280]{1,0:T(8,128)(2,1)S(1)} %bitcast.195), channel_id=1, source_target_pairs={{0,1},{1,0},{2,3},{3,2},{4,5},{5,4},{6,7},{7,6},{8,9},{9,8},{10,11... | collective-permute-start | bytes 7864328 | tf_op jit(solution)/shard_map/ppermute | solution.py:61
  254.1 76.8 %all-to-all-start.4 = ((bf16[64,16,2560]{2,1,0:T(8,128)(2,1)}), bf16[64,16,2560]{2,1,0:T(8,128)(2,1)}, u32[]{:S(2)}, u32[]{:S(2)}) async-start(bf16[64,16,2560]{2,1,0:T(8,128)(2,1)} %bitcast.193), calls=%async_computation.4 | async-start | bytes 10485760 | tf_op jit(solution)/shard_map/all_to_all | solution.py:48
  261.2 44.3 %all-gather.8.cloned.1.call-start = ((), (), s32[]{:S(2)}) async-start(), calls=%async_computation.15 | async-start | bytes 1310720 | tf_op jit(solution)/shard_map/all_gather | solution.py:626
  353.9 75.7 %all-to-all-start.5 = ((bf16[64,16,2560]{2,1,0:T(8,128)(2,1)}), bf16[64,16,2560]{2,1,0:T(8,128)(2,1)}, u32[]{:S(2)}, u32[]{:S(2)}) async-start(bf16[64,16,2560]{2,1,0:T(8,128)(2,1)} %bitcast.201), calls=%async_computation.5 | async-start | bytes 10485760 | tf_op jit(solution)/shard_map/all_to_all | solution.py:48
  456.0 22.3 %all-to-all-start.6 = ((bf16[8,128,640]{2,1,0:T(8,128)(2,1)}), bf16[8,128,640]{2,1,0:T(8,128)(2,1)S(1)}, u32[]{:S(2)}, u32[]{:S(2)}) async-start(bf16[8,128,640]{2,1,0:T(8,128)(2,1)} %pad_maximum_fusion.2), calls=%async_computation.6 | async-start | bytes 2621440 | tf_op jit(solution)/shard_map/all_to_all | solution.py:48
  479.4 76.9 %all-to-all-start.7 = ((bf16[64,16,2560]{2,1,0:T(8,128)(2,1)}), bf16[64,16,2560]{2,1,0:T(8,128)(2,1)}, u32[]{:S(2)}, u32[]{:S(2)}) async-start(bf16[64,16,2560]{2,1,0:T(8,128)(2,1)} %bitcast.194), calls=%async_computation.7 | async-start | bytes 10485760 | tf_op jit(solution)/shard_map/all_to_all | solution.py:48
  491.1 85.6 %reduce-scatter.3.cloned.1.call-start = ((), (), s32[]{:S(2)}) async-start(), calls=%async_computation.16 | async-start | bytes 4718592 | tf_op jit(solution)/shard_map/reduce_scatter | solution.py:696
  589.6 104.8 %reduce-scatter.5.cloned.1.call-start = ((), (), s32[]{:S(2)}) async-start(), calls=%async_computation.17 | async-start | bytes 2949120 | tf_op jit(solution)/shard_map/reduce_scatter | solution.py:740
  611.1 64.7 %all-to-all-start.9 = ((bf16[8,128,2048]{2,1,0:T(8,128)(2,1)}), bf16[8,128,2048]{2,1,0:T(8,128)(2,1)}, u32[]{:S(2)}, u32[]{:S(2)}) async-start(bf16[8,128,2048]{2,1,0:T(8,128)(2,1)} %bitcast.207), calls=%async_computation.10 | async-start | bytes 8388608 | tf_op jit(solution)/shard_map/all_to_all | solution.py:48
  621.8 57.5 %collective-permute-start.14 = (bf16[128,2048]{1,0:T(8,128)(2,1)}, bf16[128,2048]{1,0:T(8,128)(2,1)}, u32[]{:S(2)}, u32[]{:S(2)}) collective-permute-start(bf16[128,2048]{1,0:T(8,128)(2,1)} %fusion.10), channel_id=1, source_target_pairs={{0,1},{1,0},{2,3},{3,2},{4,5},{5,4},{6,7},{7,6},{8,9},{9,8},{10,11... | collective-permute-start | bytes 1572872 | tf_op jit(solution)/shard_map/ppermute | solution.py:70
  697.2 16.5 %all-to-all-start.10 = ((bf16[8,64,512]{2,1,0:T(8,128)(2,1)}), bf16[8,64,512]{2,1,0:T(8,128)(2,1)S(1)}, u32[]{:S(2)}, u32[]{:S(2)}) async-start(bf16[8,64,512]{2,1,0:T(8,128)(2,1)} %pad_maximum_fusion.8), calls=%async_computation.12 | async-start | bytes 1048576 | tf_op jit(solution)/shard_map/all_to_all | solution.py:48
  (61 other events, 1271.7 us)
Sparse Core Ops, SparseCore 0:
  11.2 107.7 all-gather.3
  160.0 28.2 all-gather.5
  264.3 41.2 all-gather.7
  522.7 53.9 reduce-scatter.2
  611.2 32.7 reduce-scatter.4

commit v3 on v2

--- a/solution.py
+++ b/solution.py
@@ -51,10 +51,16 @@
 OFFSETS = [(i, j) for i in range(4) for j in range(2)]
 
 
+def ahead(value, axis, steps):
+    return lax.ppermute(value, axis, [(a, (a + steps) % 4) for a in range(4)])
+
+
 def ring(value, axis):
-    return [value] + [
-        lax.ppermute(value, axis, [(a, (a + i) % 4) for a in range(4)]) for i in (1, 2, 3)
-    ]
+    half = value.shape[0] // 2
+    behind = ahead(value, axis, 1)
+    front = ahead(value, axis, 3)
+    far = [ahead(behind[:half], axis, 1), ahead(front[half:], axis, 3)]
+    return [[value], [behind], far, [front]]
 
 
 def swap(value, axis):
@@ -104,47 +110,67 @@
 
 
 def project_kernel(place_ref, *refs):
-    inputs, weights = refs[:8], refs[8:12]
-    normed_ref, raw_ref, square_ref, weight_ref, small_ref, gain_ref = refs[12:]
+    refs = list(refs)
+    inputs = [[refs.pop(0) for _ in range(2 if i == 2 else 1)] for i, _ in OFFSETS]
+    weights = [[refs.pop(0) for _ in range(2 if i == 2 else 1)] for i in range(4)]
+    cosine_ref, sine_ref, normed_ref, raw_ref, query_ref, kv_ref = refs[:6]
+    square_ref, weight_ref, small_ref, gain_ref = refs[6:]
     for n, (i, j) in enumerate(OFFSETS):
+        piece = weights[2][j].at[0] if i == 2 else weights[i][0].at[j]
         for m in range(8):
             row = (place_ref[8 + n] + (m // 2) * 16 + (m % 2) * 2) * 32
             here = pl.ds(pl.multiple_of(row, 32), 32)
-            weight_ref[here, :] = weights[i][j, m * 32 : m * 32 + 32, : 3 * HD]
-            small_ref[here, :] = weights[i][j, m * 32 : m * 32 + 32, 3 * HD :]
+            weight_ref[here, :] = piece[m * 32 : m * 32 + 32, : 3 * HD]
+            small_ref[here, :] = piece[m * 32 : m * 32 + 32, 3 * HD :]
     row = lax.broadcasted_iota(jnp.int32, (8, 128), 0)
     column = lax.broadcasted_iota(jnp.int32, (8, 128), 1)
     pick = jnp.where(column == row + 64, 1.0, 0.0).astype(bf16)
     gain_ref[...] = dot(pick, small_ref[...], ((1,), (1,)))
     gain = gain_ref[0:1, :]
+    head_gains = jnp.concatenate(
+        [
+            small_ref[pl.ds(pl.multiple_of((place_ref[16] * 8 + m) * 32, 32), 16), :]
+            for m in range(8)
+        ],
+        axis=0,
+    )
+    head_gains = head_gains.astype(f32).T
     for n in range(8):
-        value = inputs[n][...].astype(f32)
+        value = jnp.concatenate([part[...] for part in inputs[n]], axis=0).astype(f32)
         inverse = lax.rsqrt(jnp.mean(value * value, axis=-1, keepdims=True) + epsilon)
         normed = (value * inverse * gain).astype(bf16)
         chunk = place_ref[n]
         here = pl.ds(pl.multiple_of(chunk * 128, 128), 128)
         normed_ref[here, :] = normed
         raw = dot(normed, weight_ref[...])
-        raw_ref[here, :] = raw
+        raw_ref[here, :] = raw[:, : 2 * HD]
         for part in range(2):
             own = raw[:, part * HD : part * HD + HD]
             square = jnp.sum(own * own, axis=-1, keepdims=True)
             square = jnp.broadcast_to(square, (128, 128)).T
             square_ref[pl.ds(chunk + 8 * part, 1), :] = square[0:1]
-
-
-def spread_kernel(
-    raw_ref, normed_ref, weight_ref, router_ref, gain_ref, extra_ref, output_ref, back_ref, share_ref
-):
+            own = own * head_gains[66 + part : 67 + part]
+            own = own * cosine_ref[here, :] + pltpu.roll(own, HD // 2, 1) * sine_ref[here, :]
+            if part == 0:
+                query_ref[here, :] = own.astype(bf16)
+            else:
+                kv_ref[here, :HD] = own.astype(bf16)
+        kv_ref[here, HD:] = raw[:, 2 * HD :].astype(bf16)
+
+
+def back_kernel(raw_ref, normed_ref, weight_ref, gain_ref, back_ref, total_ref):
     total = jnp.zeros((1, D), f32)
     for n in range(4):
         here = slice(n * 256, n * 256 + 256)
         part = dot(raw_ref[here, :], weight_ref[...], ((1,), (1,)))
         total = total + jnp.sum(part * normed_ref[here, :].astype(f32), axis=0, keepdims=True)
         back_ref[here, :] = part.astype(bf16)
-    total = total / gain_ref[0:1, :]
+    total_ref[...] = total / gain_ref[0:1, :]
+
+
+def share_kernel(raw_ref, normed_ref, router_ref, extra_ref, total_ref, output_ref, share_ref):
     row = lax.broadcasted_iota(jnp.int32, (8, 1), 0)
-    extra = extra_ref[...] + jnp.where(row == 0, total, 0.0)
+    extra = extra_ref[...] + jnp.where(row == 0, total_ref[...], 0.0)
     for n in range(4):
         band = slice(n * 512, n * 512 + 512)
         part = dot(normed_ref[:, band], raw_ref[...], ((0,), (0,))).astype(bf16)
@@ -163,13 +189,38 @@
                 share_ref[there, :] = output_ref[m * 32 : m * 32 + 32, :].astype(bf16)
 
 
-def attend_kernel(z_ref, q_ref, kv_ref, end_ref, out_ref, lse_ref):
+def finish_kernel(place_ref, share_ref, query_ref, key_ref, value_ref, output_ref, extra_ref):
+    total = None
+    for n in range(8):
+        rows = share_ref[n * 64 : n * 64 + 32, :].astype(f32)
+        for part, ref in enumerate((query_ref, key_ref, value_ref)):
+            ref[:, n * HD : n * HD + HD] = rows[:, part * HD : part * HD + HD]
+        total = rows[:, 3 * HD :] if n == 0 else total + rows[:, 3 * HD :]
+    extra_ref[...] = total
+    for yh in range(2):
+        start = pl.multiple_of((place_ref[0] * 2 + yh) * 64 + 32, 32)
+        rows = share_ref[pl.ds(start, 32), :].astype(f32)
+        rows = jnp.concatenate([rows, jnp.zeros((96, 512), f32)], axis=0).T
+        for m in range(4):
+            there = (m * 2 + yh) * HD
+            output_ref[there : there + HD, :] = rows[m * HD : m * HD + HD, :32]
+
+
+def attend_kernel(
+    z_ref, q_ref, factor_ref, raw_ref, inverse_ref, end_ref, out_ref, lse_ref, kv_ref
+):
     z = z_ref[0]
-    factor = scale * log2e
+    for n in range(64):
+        here = slice(n * 128, n * 128 + 128)
+        inverse = inverse_ref[n // 8 : n // 8 + 1, n % 8 * 128 : n % 8 * 128 + 128]
+        inverse = jnp.broadcast_to(inverse, (128, 128)).T
+        kv_ref[here, :HD] = (raw_ref[here, :HD].astype(f32) * inverse).astype(bf16)
+        kv_ref[here, HD:] = raw_ref[here, HD:]
     for x in range(4):
         span = slice(x * 256, (x + 1) * 256)
         queries = q_ref[span, :]
         end = end_ref[:, span]
+        factor = factor_ref[:, span]
 
         def tile(index, state, masked):
             peak, mass, total = state
@@ -204,13 +255,25 @@
 
 
 def attend_back_kernel(
-    z_ref, q_ref, grad_ref, kv_ref, end_ref, lse_ref, delta_ref, dq_ref, dkv_ref, sums
+    z_ref,
+    raw_ref,
+    factor_ref,
+    q_ref,
+    grad_ref,
+    kv_ref,
+    end_ref,
+    lse_ref,
+    delta_ref,
+    dq_ref,
+    dkv_ref,
+    sums,
 ):
     z = z_ref[0]
-    factor = scale * log2e
     sums[...] = jnp.zeros_like(sums)
     for x in range(4):
         span = slice(x * 256, (x + 1) * 256)
+        raw = raw_ref[span, :]
+        factor = factor_ref[:, span]
         queries = q_ref[span, :]
         grads = grad_ref[span, :]
         end = end_ref[:, span]
@@ -223,7 +286,7 @@
                 [kv_ref[pl.ds(base, 256), :], kv_ref[pl.ds(base + 1024, 256), :]], axis=0
             )
             keys, values = part[:, :HD], part[:, HD:]
-            scores = dot(keys, queries, ((1,), (1,))) * factor - lse
+            scores = dot(keys, raw, ((1,), (1,))) * factor - lse
             if masked:
                 scores = jnp.where(window_mask(index, end), scores, masked_score)
             chances = jnp.exp2(scores)
@@ -350,6 +413,7 @@
 
 
 cheap = pl.CostEstimate(flops=1, bytes_accessed=1, transcendentals=0)
+dear = pl.CostEstimate(flops=200_000_000_000, bytes_accessed=1, transcendentals=0)
 
 
 def step_block(rows, columns):
@@ -364,33 +428,65 @@
     return jax.ShapeDtypeStruct((rows, columns), kind)
 
 
-def project(places, inputs, weights):
+def project(places, inputs, weights, cosine, sine):
     return pl.pallas_call(
         project_kernel,
         out_shape=(
             shape(1024, D),
-            shape(1024, 3 * HD, f32),
+            shape(1024, 2 * HD, f32),
+            shape(1024, HD),
+            shape(1024, 2 * HD),
             shape(16, 128, f32),
             shape(D, 3 * HD),
             shape(D, 128),
             shape(8, D, f32),
         ),
-        in_specs=[SMEM] + [VMEM] * 12,
-        out_specs=(VMEM,) * 6,
+        in_specs=[SMEM] + [VMEM] * (len(inputs) + len(weights) + 2),
+        out_specs=(VMEM,) * 8,
         compiler_params=params,
-        cost_estimate=cheap,
-    )(places, *inputs, *weights)
-
-
-def spread_grads(raw_grads, normed, weights, router_part, gains, extra, output_part):
+        cost_estimate=pl.CostEstimate(
+            flops=50_000_000_000, bytes_accessed=1, transcendentals=0
+        ),
+    )(places, *inputs, *weights, cosine, sine)
+
+
+def back_grads(raw_grads, normed, weights, gains):
     return pl.pallas_call(
-        spread_kernel,
-        out_shape=(shape(1024, D), shape(2560, 512)),
-        in_specs=[VMEM] * 7,
+        back_kernel,
+        out_shape=(shape(1024, D), shape(1, D, f32)),
+        in_specs=[VMEM] * 4,
         out_specs=(VMEM, VMEM),
         compiler_params=params,
         cost_estimate=cheap,
-    )(raw_grads, normed, weights, router_part, gains, extra, output_part)
+    )(raw_grads, normed, weights, gains)
+
+
+def share_grads(*values):
+    return pl.pallas_call(
+        share_kernel,
+        out_shape=shape(2560, 512),
+        in_specs=[VMEM] * 6,
+        out_specs=VMEM,
+        compiler_params=params,
+        cost_estimate=dear,
+    )(*values)
+
+
+def finish(place, shares):
+    return pl.pallas_call(
+        finish_kernel,
+        out_shape=(
+            shape(32, 8 * HD, f32),
+            shape(32, 8 * HD, f32),
+            shape(32, 8 * HD, f32),
+            shape(8 * HD, 32, f32),
+            shape(32, 128, f32),
+        ),
+        in_specs=[SMEM, VMEM],
+        out_specs=(VMEM,) * 5,
+        compiler_params=params,
+        cost_estimate=dear,
+    )(place, shares)
 
 
 def expert_pull(side, own, other, down):
@@ -465,39 +561,34 @@
         out_shape=jax.ShapeDtypeStruct(value.shape, value.dtype),
         in_specs=[VMEM],
         out_specs=VMEM,
-        cost_estimate=pl.CostEstimate(
-            flops=200_000_000_000, bytes_accessed=1, transcendentals=0
-        ),
+        cost_estimate=dear,
     )(value)
 
 
-def attend(z, queries, kv, end):
+def attend(z, queries, factor, kv, inverses, end):
     return pl.pallas_call(
         attend_kernel,
-        out_shape=(
-            jax.ShapeDtypeStruct((1024, HD), f32),
-            jax.ShapeDtypeStruct((1, 1024), f32),
-        ),
-        in_specs=[SMEM, VMEM, VMEM, VMEM],
-        out_specs=(VMEM, VMEM),
+        out_shape=(shape(1024, HD, f32), shape(1, 1024, f32), shape(8192, 2 * HD)),
+        in_specs=[SMEM] + [VMEM] * 5,
+        out_specs=(VMEM,) * 3,
         compiler_params=params,
         cost_estimate=cheap,
-    )(z, queries, kv, end)
-
-
-def attend_back(z, queries, grads, kv, end, lse, delta):
+    )(z, queries, factor, kv, inverses, end)
+
+
+def attend_back(z, raw, factor, queries, grads, kv, end, lse, delta):
     return pl.pallas_call(
         attend_back_kernel,
         out_shape=(
-            jax.ShapeDtypeStruct((1024, HD), f32),
-            jax.ShapeDtypeStruct((8192, 2 * HD), bf16),
+            shape(1024, HD, f32),
+            shape(8192, 2 * HD),
         ),
-        in_specs=[SMEM, VMEM, VMEM, VMEM, VMEM, VMEM, VMEM],
-        out_specs=(VMEM, VMEM),
+        in_specs=[SMEM] + [VMEM] * 8,
+        out_specs=(VMEM,) * 2,
         scratch_shapes=[pltpu.VMEM((8192, 2 * HD), f32)],
         compiler_params=params,
         cost_estimate=cheap,
-    )(z, queries, grads, kv, end, lse, delta)
+    )(z, raw, factor, queries, grads, kv, end, lse, delta)
 
 
 def dispatch(main_table, rest_table, value):
@@ -566,9 +657,10 @@
     weights_sent = weights_sent.transpose(1, 0, 2).reshape(256, 4 * HD)
     inputs_pair = swap(inputs, "yh")
     inputs_all = [ring(inputs, "x"), ring(inputs_pair, "x")]
-    inputs_all = [inputs_all[j][i] for i, j in OFFSETS]
+    inputs_all = [part for i, j in OFFSETS for part in inputs_all[j][i]]
     weights_come = exchange(weights_sent, HEADS)
     weights_all = ring(jnp.stack([weights_come, swap(weights_come, "c")]), "z")
+    weights_all = [part for parts in weights_all for part in parts]
     output_all = lax.all_gather(output_weight.T, CTX, axis=0, tiled=True)
 
     experts = jnp.arange(64, dtype=jnp.int32)
@@ -584,15 +676,25 @@
     rest_table = table[:, None, MAIN:, None, :] * quarter[None, :, None, :, None]
     rest_table = rest_table.reshape(64 * MAIN, QUARTERS * 128)
 
-    cotangent_side, _ = lax.optimization_barrier((cotangent, inputs_pair))
-    cotangent_side = lax.dynamic_slice(cotangent_side, (0, side * SIDE), (128, SIDE))
-    grad_rows = exchange(dispatch(main_table, rest_table, cotangent_side), CTX)
-    inputs_all, grad_rows, weights_all, output_all = lax.optimization_barrier(
-        (inputs_all, grad_rows, weights_all, output_all)
-    )
-    places = jnp.concatenate([heads_below, below(z, c) // 2 * 4 + below(z, c) % 2])
-    normed_low, raw, squares, weights_all, small_all, gain_rows = project(
-        places.astype(jnp.int32), inputs_all, weights_all
+    cotangent_side = lax.dynamic_slice(cotangent, (0, side * SIDE), (128, SIDE))
+    grad_sent = dispatch(main_table, rest_table, cotangent_side)
+    inputs_all, weights_all, grad_sent = lax.optimization_barrier(
+        (inputs_all, weights_all, grad_sent)
+    )
+    grad_rows = exchange(grad_sent, CTX)
+    chunk = jnp.arange(8, dtype=jnp.int32)
+    chunk_start = ((chunk // 2) * 16 + z * 4 + (chunk % 2) * 2 + c) * 128
+    positions = (chunk_start[:, None] + tokens[None, :]).reshape(1024)
+    cosine, sine = rotary_tables(positions)
+    places = jnp.concatenate(
+        [heads_below, below(z, c) // 2 * 4 + below(z, c) % 2, head.reshape(1)]
+    )
+    normed_low, raw, query_some, kv_some, squares, weights_all, small_all, gain_rows = project(
+        places.astype(jnp.int32),
+        inputs_all,
+        weights_all,
+        jnp.concatenate([cosine, cosine], axis=1),
+        jnp.concatenate([-sine, sine], axis=1),
     )
     blocks_all = small_all[:, 68:72].astype(jnp.int32).reshape(8192)
     attention_gain_all = gain_rows[0]
@@ -601,35 +703,39 @@
     head_gains = lax.dynamic_slice(head_gains, (head * HD, 0), (HD, 2))
     query_gain_all = head_gains[:, 0]
     key_gain_all = head_gains[:, 1]
-
-    query_raw, key_raw = raw[:, :HD], raw[:, HD : 2 * HD]
-    value_low = raw[:, 2 * HD :].astype(bf16)
-    squares = sum_over_rows(squares).reshape(2, 1024)
+    query_raw, key_raw = raw[:, :HD], raw[:, HD:]
+
+    kv_some, output_all = lax.optimization_barrier((kv_some, output_all))
+    kv_some = lax.all_gather(kv_some, TOKENS, axis=0, tiled=True)
+    grad_rows, squares = lax.optimization_barrier((grad_rows, squares))
+    squares = sum_over_rows(squares)
     grad_rows, squares = lax.optimization_barrier((grad_rows, squares))
     grad_other = swap(grad_rows, "ep")
-    inverses = lax.rsqrt(squares / float(D) + epsilon)
-    query_inverse = inverses[0][:, None]
-    key_inverse = inverses[1][:, None]
-    chunk = jnp.arange(8, dtype=jnp.int32)
-    chunk_start = ((chunk // 2) * 16 + z * 4 + (chunk % 2) * 2 + c) * 128
-    positions = (chunk_start[:, None] + tokens[None, :]).reshape(1024)
-    cosine, sine = rotary_tables(positions)
-    query_low = rotate(query_raw * query_inverse * query_gain_all, cosine, sine).astype(bf16)
-    key_low = rotate(key_raw * key_inverse * key_gain_all, cosine, sine).astype(bf16)
-    kv = lax.all_gather(
-        jnp.concatenate([key_low, value_low], axis=1), TOKENS, axis=0, tiled=True
-    )
+    group_inverse = lax.rsqrt(squares / float(D) + epsilon)
+    inverses = group_inverse[8:]
+    inverses = ring(jnp.stack([inverses, swap(inverses, "c")]), "z")
+    inverses = jnp.concatenate([part for parts in inverses for part in parts])
+    inverses = jnp.take(inverses, below(z, c), axis=0).reshape(8, 1024)
+    group_inverse = group_inverse.reshape(2, 1024)
+    query_inverse = group_inverse[0][:, None]
+    key_inverse = group_inverse[1][:, None]
+    query_factor = group_inverse[0:1] * (scale * log2e)
+    query_low = (query_some.astype(f32) * query_inverse).astype(bf16)
     own_blocks = blocks_all.reshape(4, 4, 2, 2, 128)[:, z, :, c].reshape(1024)
     end = jnp.sum((blocks_all[:, None] <= own_blocks[None, :]).astype(jnp.int32), axis=0)[None]
-    attended, lse = attend(z_place, query_low, kv, end)
-    attended_low, grad_other = lax.optimization_barrier((attended.astype(bf16), grad_other))
-    heads_all = lax.all_gather(attended_low, "x", axis=0, tiled=True)
-    grad_other, heads_all = lax.optimization_barrier((grad_other, heads_all))
-    grad_flat, hidden_pull = expert_pull(
-        side_place, grad_rows, grad_other, down_weight[0]
-    )
-
-    attended_rows = exchange(attended_low, HEADS).reshape(8, 128, HD)
+    kv_some, end, query_low = lax.optimization_barrier((kv_some, end, query_low))
+    attended, lse, kv = attend(
+        z_place, query_some, query_factor, kv_some, inverses, end
+    )
+    attended_low = attended.astype(bf16)
+
+    heads_all = [part for parts in ring(attended_low, "x") for part in parts]
+    attended_rows, heads_all, grad_other = lax.optimization_barrier(
+        (exchange(attended_low, HEADS).reshape(8, 128, HD), heads_all, grad_other)
+    )
+    heads_all = jnp.concatenate(heads_all, axis=0).reshape(4, 1024, HD)
+    heads_all = jnp.take(heads_all, (x - jnp.arange(4)) % 4, axis=0)
+    heads_all = heads_all.transpose(1, 0, 2).reshape(1024, 4 * HD)
     attended_rows = attended_rows.transpose(1, 0, 2).reshape(128, 8 * HD)
     source = inputs.astype(f32)
     residual = source + pair_sum(dot(attended_rows, output_all, ((1,), (1,))))
@@ -637,6 +743,10 @@
     mixed_low = (residual * mixture_inverse * mixture_gain_all).astype(bf16)
     mixed_rows = exchange(dispatch(main_table, rest_table, mixed_low), CTX)
 
+    grad_flat, hidden_pull = expert_pull(
+        side_place, grad_rows, grad_other, down_weight[0]
+    )
+    mixed_rows, heads_all = lax.optimization_barrier((mixed_rows, heads_all))
     entry_sent, entry, hidden_low, gate_raw_grad, up_raw_grad, logit_grad = expert_step(
         place.reshape(1).astype(jnp.int32),
         mixed_rows,
@@ -674,28 +784,20 @@
     residual_low = residual_grad.astype(bf16)
     attended_grad = dot(residual_low, output_all).astype(bf16)
     attended_grad = attended_grad.reshape(128, 8, HD).transpose(1, 0, 2)
-    residual_bands = residual_low.reshape(128, 4, 1, BAND).transpose(1, 2, 0, 3)
-    residual_bands = jnp.broadcast_to(residual_bands, (4, 2, 128, BAND)).reshape(8, 128, BAND)
-    attended_grad = exchange(
-        jnp.concatenate([attended_grad, residual_bands], axis=2).reshape(1024, HD + BAND), HEADS
-    )
-    residual_band = attended_grad[:, HD:]
-    attended_grad = attended_grad[:, :HD]
+    attended_grad = exchange(attended_grad.reshape(1024, HD), HEADS)
     result_sent, attended_grad = lax.optimization_barrier((result_sent, attended_grad))
     result_back = exchange(result_sent, CTX)
-    output_part = dot(
-        residual_band,
-        heads_all.reshape(4, 1024, HD).transpose(1, 0, 2).reshape(1024, 4 * HD),
-        ((0,), (0,)),
-    )
-
     delta = jnp.sum(attended_grad.astype(f32) * attended, axis=-1)[None]
     query_grad, kv_part = attend_back(
-        z_place, query_low, attended_grad, kv, end, lse, delta
+        z_place, query_some, query_factor, query_low, attended_grad, kv, end, lse, delta
     )
     kv_grad = lax.psum_scatter(kv_part, TOKENS, scatter_dimension=0, tiled=True)
     query_grad, result_back = lax.optimization_barrier((query_grad, result_back))
     query_grad = linger(query_grad)
+    residual_sent, result_back = lax.optimization_barrier((residual_low, result_back))
+    bands = residual_sent.reshape(128, 4, 1, BAND).transpose(1, 2, 0, 3)
+    bands = jnp.broadcast_to(bands, (4, 2, 128, BAND)).reshape(1024, BAND)
+    residual_band = exchange(bands, HEADS)
     kv_grad = kv_grad.astype(f32)
     final = residual + pair_sum(collect(main_table, rest_table, result_back))
     value_grad_low = kv_grad[:, HD:].astype(bf16)
@@ -706,6 +808,8 @@
     dots = jnp.stack(
         [jnp.sum(query_scaled * query_raw, axis=-1), jnp.sum(key_scaled * key_raw, axis=-1)]
     )
+    residual_band, dots = lax.optimization_barrier((residual_band, dots))
+    output_part = dot(residual_band, heads_all, ((0,), (0,)))
     dots = sum_over_rows(dots.reshape(16, 128)).reshape(2, 1024)[:, :, None] / float(D)
 
     def raw_back(value, inverse, scaled_grad, mean):
@@ -731,26 +835,24 @@
         ],
         axis=0,
     )
-    normed_part, shares = spread_grads(
-        raw_grads, normed_low, weights_all, router_part, gain_rows, extra, output_part
-    )
-    normed_grad = jnp.sum(exchange(normed_part, HEADS).reshape(8, 128, D).astype(f32), axis=0)
-    normed_grad = pair_sum(normed_grad)
+    normed_part, gain_total = back_grads(raw_grads, normed_low, weights_all, gain_rows)
+    normed_back = exchange(normed_part, HEADS)
+    shares = share_grads(raw_grads, normed_low, router_part, extra, gain_total, output_part)
 
     summed = lax.psum_scatter(shares, TOKENS, scatter_dimension=0, tiled=True)
     output_sum = jnp.broadcast_to(summed[256:].reshape(1, 2, 32, 512), (4, 2, 32, 512))
     shares = jnp.concatenate(
         [summed[:256].reshape(8, 32, 512), output_sum.reshape(8, 32, 512)], axis=1
     )
-    shares = exchange(shares.reshape(512, 512), HEADS).reshape(8, 64, 512).astype(f32)
-    weight_grad = shares[:, :32, : 3 * HD].reshape(8, 32, 3, HD)
-    weight_grad = weight_grad.transpose(2, 1, 0, 3).reshape(3, 32, 8 * HD)
-    extra = jnp.sum(shares[:, :32, 3 * HD :], axis=0)
-    pair = extra + lax.ppermute(extra, "ep", [(0, 1), (1, 0)])
+    shares, normed_back = lax.optimization_barrier((shares.reshape(512, 512), normed_back))
+    shares = exchange(shares, HEADS)
+    normed_grad = pair_sum(jnp.sum(normed_back.reshape(8, 128, D).astype(f32), axis=0))
+    query_part, key_part, value_part, output_grad, extra = finish(
+        x.reshape(1).astype(jnp.int32), shares
+    )
+    pair = extra + swap(extra, "ep")
     router_grad = pair[:, :64]
     attention_gain_grad = pair[:, 64]
-    output_grad = lax.dynamic_slice(shares, (x * 2, 32, 0), (2, 32, 512))
-    output_grad = output_grad.reshape(2, 32, 4, HD).transpose(2, 0, 3, 1).reshape(8 * HD, 32)
 
     inverse = lax.rsqrt(jnp.mean(source * source, axis=-1, keepdims=True) + epsilon)
     scaled = normed_grad * attention_gain_all
@@ -767,9 +869,9 @@
         final,
         input_grad,
         attention_gain_grad,
-        weight_grad[0],
-        weight_grad[1],
-        weight_grad[2],
+        query_part,
+        key_part,
+        value_part,
         extra[:16, 66],
         extra[:16, 67],
         output_grad,

time: 735 us -> 700 us (0.952)
  waiting for transfers between devices: 361 us -> 288 us
  starting transfers between devices: 97.5 us -> 123 us
  blocking collectives: 14.8 us -> 0 us
  Pallas kernels: 115 us -> 128 us
  local copies, waits for them, and re-layouts: 37.7 us -> 49.1 us
    all_gather x2 -> x1, waiting for transfers between devices: 60.2 us -> 0.01 us  [local(): kv_some = lax.all_gather(kv_some, TOKENS, axis=0, tiled=True)]
    ppermute x10 -> x20, waiting for transfers between devices: 71.6 us -> 28.2 us  [ahead(): return lax.ppermute(value, axis, [(a, (a + steps) % 4) for a in range(4)])]
    all_to_all x10 -> x12, waiting for transfers between devices: 176 us -> 206 us  [exchange(): return lax.all_to_all(value, axes, split_axis=0, concat_axis=0, tiled=True)]
    reduce_scatter x1, waiting for transfers between devices: 0.02 us -> 23 us  [local(): summed = lax.psum_scatter(shares, TOKENS, scatter_dimension=0, tiled=True)]
    all_to_all x10 -> x12, starting transfers between devices: 70.2 us -> 87.9 us  [exchange(): return lax.all_to_all(value, axes, split_axis=0, concat_axis=0, tiled=True)]
    ppermute x4, waiting for transfers between devices: 31.6 us -> 16.9 us  [pair_sum(): other = lax.ppermute(own, 'ep', [(0, 1), (1, 0)])]
    all_to_all x1 -> x0, blocking collectives: 14.8 us -> none  [exchange(): return lax.all_to_all(value, axes, split_axis=0, concat_axis=0, tiled=True)]
    pallas_call x4 -> x6, Pallas kernels: 74.5 us -> 87.5 us  [the longest x1 30.4 us: attend(): pl.pallas_call(attend_kernel, out_shape=(shape(1024, HD, f32), shape(1, 1...]
  transfers between devices with their start and end apart: 32 -> 45, of which waited for: 20 -> 29; matrix products, arithmetic and copies ran while one was open for 11% -> 15% of each run, Pallas kernels for 10% -> 13%
where the time goes in v3:
time: 700 us; the launch traced here: 689 us
  waiting for transfers between devices  288 us (41%)
  Pallas kernels  128 us (18%)
  starting transfers between devices  123 us (18%)
  local copies, waits for them, and re-layouts  49.1 us (7%)
  other arithmetic  45.1 us (6%)
  matrix products  41.3 us (6%)
  between operations  15.5 us (2%)
    all_to_all x12, waiting for transfers between devices, exchange(): return lax.all_to_all(value, axes, split_axis=0, concat_axis=0, tiled=True)  206 us
    all_to_all x12, starting transfers between devices, exchange(): return lax.all_to_all(value, axes, split_axis=0, concat_axis=0, tiled=True)  87.9 us
    dot_general x16, matrix products, dot(): lax.dot_general(first, second, (dims, ((), ())), preferred_element_type=f32)  41.3 us
    pallas_call x1, Pallas kernels, attend(): pl.pallas_call(attend_kernel, out_shape=(shape(1024, HD, f32), shape(1, 1...  30.4 us
    pallas_call x1, Pallas kernels, attend_back(): pl.pallas_call(attend_back_kernel, out_shape=(shape(1024, HD, f32), shape...  29.4 us
    ppermute x20, waiting for transfers between devices, ahead(): return lax.ppermute(value, axis, [(a, (a + steps) % 4) for a in range(4)])  28.2 us
    pallas_call x1, Pallas kernels, expert_step(): pl.pallas_call(expert_kernel, grid=(2,), out_shape=(shape(1024, ROW_WIDTH...  23 us
    reduce_scatter x1, waiting for transfers between devices, local(): summed = lax.psum_scatter(shares, TOKENS, scatter_dimension=0, tiled=True)  23 us
  transfers between devices with their start and end apart: 45, of which 29 were waited for; matrix products, arithmetic and copies ran while one was open for 15% of the time, Pallas kernels for 13%

profile of v3, /device:TPU:96, one launch (start us, length us, event | category | flops | bytes accessed | tf_op | source)
XLA Modules:
  0.0 689.3 jit_solution(8982494144063664479)
XLA Ops:
  70.3 11.3 %shard_map.263 = (bf16[1024,2048]{1,0:T(8,128)(2,1)}, f32[1024,256]{1,0:T(8,128)}, bf16[1024,128]{1,0:T(8,128)(2,1)}, bf16[1024,256]{1,0:T(8,128)(2,1)}, f32[16,...) custom-call(s32[17]{0:T(128)} %concatenate.64.place_ref, ...), custom_call_target="tpu_custom_call" | custom-call | flops 49999998976 | bytes 1 | tf_op jit(solution)/shard_map/pallas_call | solution.py:432
  86.3 7.3 %all-to-all-start.1 = ((bf16[64,16,1280]{2,1,0:T(8,128)(2,1)}), bf16[64,16,1280]{2,1,0:T(8,128)(2,1)S(1)}, u32[]{:S(2)}, u32[]{:S(2)}) async-start(bf16[64,16,1280]{2,1,0:T(8,128)(2,1)} %bitcast.208), calls=%async_computation.1 | async-start | bytes 5242880 | tf_op jit(solution)/shard_map/all_to_all | solution.py:48
  93.7 34.7 %all-to-all-done.1 = bf16[64,16,1280]{2,1,0:T(8,128)(2,1)S(1)} async-done(((bf16[64,16,1280]{2,1,0:T(8,128)(2,1)}), bf16[64,16,1280]{2,1,0:T(8,128)(2,1)S(1)}, u32[]{:S(2)}, u32[]{:S(2)}) %all-to-all-start.1) | async-done | bytes 2621472 | tf_op jit(solution)/shard_map/all_to_all | solution.py:48
  129.1 5.8 all-to-all-start.2
  162.8 30.4 %shard_map.264 = (f32[1024,128]{1,0:T(8,128)}, f32[1,1024]{1,0:T(1,128)}, bf16[8192,256]{1,0:T(8,128)(2,1)}) custom-call(s32[1]{0:T(128)} %bitcast.z_ref, bf16[1024,128]{1,0:T(8,128)(2,1)} %get-tuple-element.106.q_ref.raw_ref, f32[1,1024]{1,0:T(1,128)} %bitcast.258, bf16[8192,256]{1,0:T(8,128)(2,1)} %all-gather.5.cloned.1.call-done.raw_ref, ...), custom_call_target="tpu_custom_call" | custom-call | flops 1 | bytes 1 | tf_op jit(solution)/shard_map/pallas_call | solution.py:569
  219.9 7.1 %collective-permute-done.24 = bf16[128,2048]{1,0:T(8,128)(2,1)S(1)} collective-permute-done((bf16[128,2048]{1,0:T(8,128)(2,1)S(1)}, bf16[128,2048]{1,0:T(8,128)(2,1)S(1)}, u32[]{:S(2)}, u32[]{:S(2)}) %collective-permute-start.24) | collective-permute-done | bytes 524320 | tf_op jit(solution)/shard_map/ppermute | solution.py:76
  232.5 10.8 %all-to-all-start.4 = ((bf16[64,16,2560]{2,1,0:T(8,128)(2,1)}), bf16[64,16,2560]{2,1,0:T(8,128)(2,1)}, u32[]{:S(2)}, u32[]{:S(2)}) async-start(bf16[64,16,2560]{2,1,0:T(8,128)(2,1)} %bitcast.207), calls=%async_computation.4 | async-start | bytes 10485760 | tf_op jit(solution)/shard_map/all_to_all | solution.py:48
  243.3 7.4 %shard_map.265 = (bf16[1280,2048]{1,0:T(8,128)(2,1)}, f32[1280,512]{1,0:T(8,128)}) custom-call(s32[1]{0:T(128)} %bitcast.63.side_ref, bf16[1024,1280]{1,0:T(8,128)(2,1)} %bitcast.210, bf16[1024,1280]{1,0:T(8,128)(2,1)} %collective-permute-done.23.other_ref, bf16[512,2048]{1,0:T(8,128)(2,1)} %bitcast.211), custom_call_target="tpu_custom_call" | custom-call | flops 1 | bytes 1 | tf_op jit(solution)/shard_map/pallas_call | solution.py:493
  260.9 47.4 %all-to-all-done.4 = bf16[64,16,2560]{2,1,0:T(8,128)(2,1)} async-done(((bf16[64,16,2560]{2,1,0:T(8,128)(2,1)}), bf16[64,16,2560]{2,1,0:T(8,128)(2,1)}, u32[]{:S(2)}, u32[]{:S(2)}) %all-to-all-start.4) | async-done | bytes 5242912 | tf_op jit(solution)/shard_map/all_to_all | solution.py:48
  308.2 23.0 %shard_map.266 = (bf16[1024,2560]{1,0:T(8,128)(2,1)}, bf16[1280,2048]{1,0:T(8,128)(2,1)}, bf16[1280,512]{1,0:T(8,128)(2,1)}, bf16[1280,512]{1,0:T(8,128)(2,1)}, ...) custom-call(s32[1]{0:T(128)} %bitcast.53.place_ref, bf16[1024,2560]{1,0:T(8,128)(2,1)} %bitcast.58.rows_ref, ...), custom_call_target="tpu_custom_call" | custom-call | flops 1 | bytes 1 | tf_op jit(solution)/shard_map/pallas_call | solution.py:510
  331.2 14.2 %all-to-all-start.5 = ((bf16[64,16,2560]{2,1,0:T(8,128)(2,1)}), bf16[64,16,2560]{2,1,0:T(8,128)(2,1)}, u32[]{:S(2)}, u32[]{:S(2)}) async-start(bf16[64,16,2560]{2,1,0:T(8,128)(2,1)} %bitcast.215), calls=%async_computation.5 | async-start | bytes 10485760 | tf_op jit(solution)/shard_map/all_to_all | solution.py:48
  365.0 45.4 %all-to-all-done.5 = bf16[64,16,2560]{2,1,0:T(8,128)(2,1)} async-done(((bf16[64,16,2560]{2,1,0:T(8,128)(2,1)}), bf16[64,16,2560]{2,1,0:T(8,128)(2,1)}, u32[]{:S(2)}, u32[]{:S(2)}) %all-to-all-start.5) | async-done | bytes 5242912 | tf_op jit(solution)/shard_map/all_to_all | solution.py:48
  420.7 9.7 %collective-permute-done.25 = bf16[128,2048]{1,0:T(8,128)(2,1)S(1)} collective-permute-done((bf16[128,2048]{1,0:T(8,128)(2,1)S(1)}, bf16[128,2048]{1,0:T(8,128)(2,1)S(1)}, u32[]{:S(2)}, u32[]{:S(2)}) %collective-permute-start.25) | collective-permute-done | bytes 524320 | tf_op jit(solution)/shard_map/ppermute | solution.py:76
  439.9 8.3 %shard_map.267 = bf16[1024,2560]{1,0:T(8,128)(2,1)} custom-call(bf16[1280,512]{1,0:T(8,128)(2,1)} %get-tuple-element.131.hidden_ref, bf16[512,2048]{1,0:T(8,128)(2,1)} %bitcast.212), custom_call_target="tpu_custom_call" | custom-call | flops 1 | bytes 1 | tf_op jit(solution)/shard_map/pallas_call | solution.py:543
  448.4 14.5 %all-to-all-start.7 = ((bf16[64,16,2560]{2,1,0:T(8,128)(2,1)}), bf16[64,16,2560]{2,1,0:T(8,128)(2,1)}, u32[]{:S(2)}, u32[]{:S(2)}) async-start(bf16[64,16,2560]{2,1,0:T(8,128)(2,1)} %bitcast.206), calls=%async_computation.7 | async-start | bytes 10485760 | tf_op jit(solution)/shard_map/all_to_all | solution.py:48
  465.3 29.4 %shard_map.268 = (f32[1024,128]{1,0:T(8,128)}, bf16[8192,256]{1,0:T(8,128)(2,1)}) custom-call(s32[1]{0:T(128)} %bitcast.z_ref, bf16[1024,128]{1,0:T(8,128)(2,1)} %get-tuple-element.106.q_ref.raw_ref, f32[1,1024]{1,0:T(1,128)} %bitcast.259, bf16[1024,128]{1,0:T(8,128)(2,1)} %multiply_convert_fusion.1.q_ref, bf16[1024,128]{1,0:T(8,128)(2,1)} %bitcast.225, ...), custom_call_target="tpu_custom_call" | custom-call | flops 1 | bytes 1 | tf_op jit(solution)/shard_map/pallas_call | solution.py:580
  494.7 33.5 %all-to-all-done.7 = bf16[64,16,2560]{2,1,0:T(8,128)(2,1)} async-done(((bf16[64,16,2560]{2,1,0:T(8,128)(2,1)}), bf16[64,16,2560]{2,1,0:T(8,128)(2,1)}, u32[]{:S(2)}, u32[]{:S(2)}) %all-to-all-start.7) | async-done | bytes 5242912 | tf_op jit(solution)/shard_map/all_to_all | solution.py:48
  529.7 7.1 %all-to-all-start.8 = ((bf16[8,128,512]{2,1,0:T(8,128)(2,1)}), bf16[8,128,512]{2,1,0:T(8,128)(2,1)}, u32[]{:S(2)}, u32[]{:S(2)}) async-start(bf16[8,128,512]{2,1,0:T(8,128)(2,1)} %bitcast.83), calls=%async_computation.8 | async-start | bytes 2097152 | tf_op jit(solution)/shard_map/all_to_all | solution.py:48
  538.8 10.1 %reduce-scatter.3.cloned.1.call-done = bf16[1024,256]{1,0:T(8,128)(2,1)} async-done(((bf16[8192,256]{1,0:T(8,128)(2,1)}), bf16[1024,256]{1,0:T(8,128)(2,1)}) %reduce-scatter.3.cloned.1.call-update) | async-done | bytes 524304 | tf_op jit(solution)/shard_map/reduce_scatter | solution.py:794
  571.8 7.3 %shard_map.270 = (bf16[1024,2048]{1,0:T(8,128)(2,1)}, f32[1,2048]{1,0:T(1,128)}) custom-call(bf16[1024,384]{1,0:T(8,128)(2,1)} %pad_maximum_fusion.2.raw_ref, bf16[1024,2048]{1,0:T(8,128)(2,1)} %get-tuple-element.151.normed_ref, bf16[2048,384]{1,0:T(8,128)(2,1)} %get-tuple-element.153.weight_ref, f32[8,2048]{1,0:T(8,128)} %get-tuple-element.121.gain_ref), custom_call_target="tpu_custom_call" | custom-call | flops 1 | bytes 1 | tf_op jit(solution)/shard_map/pallas_call | solution.py:454
  579.1 6.9 shard_map.271
  596.5 23.0 %reduce-scatter.5.cloned.1.call-done = bf16[320,512]{1,0:T(8,128)(2,1)} async-done(((bf16[2560,512]{1,0:T(8,128)(2,1)}), bf16[320,512]{1,0:T(8,128)(2,1)}) %reduce-scatter.5.cloned.1.call-update) | async-done | bytes 327696 | tf_op jit(solution)/shard_map/reduce_scatter | solution.py:842
  622.1 28.2 %all-to-all-done.10 = bf16[8,128,2048]{2,1,0:T(8,128)(2,1)} async-done(((bf16[8,128,2048]{2,1,0:T(8,128)(2,1)}), bf16[8,128,2048]{2,1,0:T(8,128)(2,1)}, u32[]{:S(2)}, u32[]{:S(2)}) %all-to-all-start.10) | async-done | bytes 4194336 | tf_op jit(solution)/shard_map/all_to_all | solution.py:48
  660.8 6.8 all-to-all-done.11
  (351 shorter events, 244.2 us)
Async XLA Ops:
  7.2 76.3 %all-gather.3.cloned.1.call-start = ((), (), s32[]{:S(2)}) async-start(), calls=%async_computation.14 | async-start | bytes 4259840 | tf_op jit(solution)/shard_map/all_gather | solution.py:664
  7.2 29.3 %collective-permute-start = (bf16[128,2048]{1,0:T(8,128)(2,1)}, bf16[128,2048]{1,0:T(8,128)(2,1)}, u32[]{:S(2)}, u32[]{:S(2)}) collective-permute-start(bf16[128,2048]{1,0:T(8,128)(2,1)} %refs_0_), channel_id=1, source_target_pairs={{0,4},{4,0},{1,5},{5,1},{2,6},{6,2},{3,7},{7,3},{8,12},{12,8},{9,1... | collective-permute-start | bytes 1572872 | tf_op jit(solution)/shard_map/ppermute | solution.py:67
  10.5 26.5 %collective-permute-start.1 = (bf16[128,2048]{1,0:T(8,128)(2,1)}, bf16[128,2048]{1,0:T(8,128)(2,1)}, u32[]{:S(2)}, u32[]{:S(2)}) collective-permute-start(bf16[128,2048]{1,0:T(8,128)(2,1)} %refs_0_), channel_id=1, source_target_pairs={{0,32},{32,64},{64,96},{96,0},{1,33},{33,65},{65,97},{97,1},{2,34}... | collective-permute-start | bytes 1572872 | tf_op jit(solution)/shard_map/ppermute | solution.py:55
  12.0 30.4 %collective-permute-start.4 = (bf16[128,2048]{1,0:T(8,128)(2,1)}, bf16[128,2048]{1,0:T(8,128)(2,1)}, u32[]{:S(2)}, u32[]{:S(2)}) collective-permute-start(bf16[128,2048]{1,0:T(8,128)(2,1)} %refs_0_), channel_id=1, source_target_pairs={{0,96},{32,0},{64,32},{96,64},{1,97},{33,1},{65,33},{97,65},{2,98}... | collective-permute-start | bytes 1572872 | tf_op jit(solution)/shard_map/ppermute | solution.py:55
  24.3 138.5 %all-gather.5.cloned.1.call-start = ((), (), s32[]{:S(2)}) async-start(), calls=%async_computation.15 | async-start | bytes 4718592 | tf_op jit(solution)/shard_map/all_gather | solution.py:709
  34.4 14.9 %collective-permute-start.10 = (bf16[2,256,512]{2,1,0:T(8,128)(2,1)S(1)}, bf16[2,256,512]{2,1,0:T(8,128)(2,1)S(1)}, u32[]{:S(2)}, u32[]{:S(2)}) collective-permute-start(bf16[2,256,512]{2,1,0:T(8,128)(2,1)S(1)} %pad_maximum_fusion.3.refs_10_), channel_id=1, source_target_pairs={{0,8},{8,16},{16,24},{24,0},{1,9},{9,17},{17,25},{25,1},{2,10},{10... | collective-permute-start | bytes 1572872 | tf_op jit(solution)/shard_map/ppermute | solution.py:55
  34.5 16.4 %collective-permute-start.12 = (bf16[2,256,512]{2,1,0:T(8,128)(2,1)S(1)}, bf16[2,256,512]{2,1,0:T(8,128)(2,1)S(1)}, u32[]{:S(2)}, u32[]{:S(2)}) collective-permute-start(bf16[2,256,512]{2,1,0:T(8,128)(2,1)S(1)} %pad_maximum_fusion.3.refs_10_), channel_id=1, source_target_pairs={{0,24},{8,0},{16,8},{24,16},{1,25},{9,1},{17,9},{25,17},{2,26},{10... | collective-permute-start | bytes 1572872 | tf_op jit(solution)/shard_map/ppermute | solution.py:55
  36.5 18.2 %collective-permute-start.2 = (bf16[128,2048]{1,0:T(8,128)(2,1)}, bf16[128,2048]{1,0:T(8,128)(2,1)S(1)}, u32[]{:S(2)}, u32[]{:S(2)}) collective-permute-start(bf16[128,2048]{1,0:T(8,128)(2,1)} %collective-permute-done.refs_1_), channel_id=1, source_target_pairs={{0,32},{32,64},{64,96},{96,0},{1,33},{33,65},{65,97},{97,1},{2,34}... | collective-permute-start | bytes 1572872 | tf_op jit(solution)/shard_map/ppermute | solution.py:55
  37.0 18.2 %collective-permute-start.7 = (bf16[128,2048]{1,0:T(8,128)(2,1)}, bf16[128,2048]{1,0:T(8,128)(2,1)}, u32[]{:S(2)}, u32[]{:S(2)}) collective-permute-start(bf16[128,2048]{1,0:T(8,128)(2,1)} %collective-permute-done.refs_1_), channel_id=1, source_target_pairs={{0,96},{32,0},{64,32},{96,64},{1,97},{33,1},{65,33},{97,65},{2,98}... | collective-permute-start | bytes 1572872 | tf_op jit(solution)/shard_map/ppermute | solution.py:55
  42.4 18.7 %collective-permute-start.3 = (bf16[64,2048]{1,0:T(8,128)(2,1)S(1)}, bf16[64,2048]{1,0:T(8,128)(2,1)S(1)}, u32[]{:S(2)}, u32[]{:S(2)}) collective-permute-start(bf16[64,2048]{1,0:T(8,128)(2,1)S(1)} %slice.178), channel_id=1, source_target_pairs={{0,32},{32,64},{64,96},{96,0},{1,33},{33,65},{65,97},{97,1},{2,34}... | collective-permute-start | bytes 786440 | tf_op jit(solution)/shard_map/ppermute | solution.py:55
  86.3 42.1 %all-to-all-start.1 = ((bf16[64,16,1280]{2,1,0:T(8,128)(2,1)}), bf16[64,16,1280]{2,1,0:T(8,128)(2,1)S(1)}, u32[]{:S(2)}, u32[]{:S(2)}) async-start(bf16[64,16,1280]{2,1,0:T(8,128)(2,1)} %bitcast.208), calls=%async_computation.1 | async-start | bytes 5242880 | tf_op jit(solution)/shard_map/all_to_all | solution.py:48
  143.8 65.1 %collective-permute-start.23 = (bf16[1024,1280]{1,0:T(8,128)(2,1)S(1)}, bf16[1024,1280]{1,0:T(8,128)(2,1)}, u32[]{:S(2)}, u32[]{:S(2)}) collective-permute-start(bf16[1024,1280]{1,0:T(8,128)(2,1)S(1)} %bitcast.209), channel_id=1, source_target_pairs={{0,1},{1,0},{2,3},{3,2},{4,5},{5,4},{6,7},{7,6},{8,9},{9,8},{10,11... | collective-permute-start | bytes 7864328 | tf_op jit(solution)/shard_map/ppermute | solution.py:67
  232.5 75.8 %all-to-all-start.4 = ((bf16[64,16,2560]{2,1,0:T(8,128)(2,1)}), bf16[64,16,2560]{2,1,0:T(8,128)(2,1)}, u32[]{:S(2)}, u32[]{:S(2)}) async-start(bf16[64,16,2560]{2,1,0:T(8,128)(2,1)} %bitcast.207), calls=%async_computation.4 | async-start | bytes 10485760 | tf_op jit(solution)/shard_map/all_to_all | solution.py:48
  331.2 79.2 %all-to-all-start.5 = ((bf16[64,16,2560]{2,1,0:T(8,128)(2,1)}), bf16[64,16,2560]{2,1,0:T(8,128)(2,1)}, u32[]{:S(2)}, u32[]{:S(2)}) async-start(bf16[64,16,2560]{2,1,0:T(8,128)(2,1)} %bitcast.215), calls=%async_computation.5 | async-start | bytes 10485760 | tf_op jit(solution)/shard_map/all_to_all | solution.py:48
  415.6 14.8 %collective-permute-start.25 = (bf16[128,2048]{1,0:T(8,128)(2,1)S(1)}, bf16[128,2048]{1,0:T(8,128)(2,1)S(1)}, u32[]{:S(2)}, u32[]{:S(2)}) collective-permute-start(bf16[128,2048]{1,0:T(8,128)(2,1)S(1)} %fusion.13), channel_id=1, source_target_pairs={{0,1},{1,0},{2,3},{3,2},{4,5},{5,4},{6,7},{7,6},{8,9},{9,8},{10,11... | collective-permute-start | bytes 1572872 | tf_op jit(solution)/shard_map/ppermute | solution.py:76
  434.4 14.0 %all-to-all-start.6 = ((bf16[8,128,128]{2,1,0:T(8,128)(2,1)}), bf16[8,128,128]{2,1,0:T(8,128)(2,1)S(1)}, u32[]{:S(2)}, u32[]{:S(2)}) async-start(bf16[8,128,128]{2,1,0:T(8,128)(2,1)} %bitcast.204), calls=%async_computation.6 | async-start | bytes 524288 | tf_op jit(solution)/shard_map/all_to_all | solution.py:48
  448.4 79.8 %all-to-all-start.7 = ((bf16[64,16,2560]{2,1,0:T(8,128)(2,1)}), bf16[64,16,2560]{2,1,0:T(8,128)(2,1)}, u32[]{:S(2)}, u32[]{:S(2)}) async-start(bf16[64,16,2560]{2,1,0:T(8,128)(2,1)} %bitcast.206), calls=%async_computation.7 | async-start | bytes 10485760 | tf_op jit(solution)/shard_map/all_to_all | solution.py:48
  462.9 86.0 %reduce-scatter.3.cloned.1.call-start = ((), (), s32[]{:S(2)}) async-start(), calls=%async_computation.16 | async-start | bytes 4718592 | tf_op jit(solution)/shard_map/reduce_scatter | solution.py:794
  529.7 25.2 %all-to-all-start.8 = ((bf16[8,128,512]{2,1,0:T(8,128)(2,1)}), bf16[8,128,512]{2,1,0:T(8,128)(2,1)}, u32[]{:S(2)}, u32[]{:S(2)}) async-start(bf16[8,128,512]{2,1,0:T(8,128)(2,1)} %bitcast.83), calls=%async_computation.8 | async-start | bytes 2097152 | tf_op jit(solution)/shard_map/all_to_all | solution.py:48
  560.9 58.5 %reduce-scatter.5.cloned.1.call-start = ((), (), s32[]{:S(2)}) async-start(), calls=%async_computation.17 | async-start | bytes 2949120 | tf_op jit(solution)/shard_map/reduce_scatter | solution.py:842
  586.1 64.2 %all-to-all-start.10 = ((bf16[8,128,2048]{2,1,0:T(8,128)(2,1)}), bf16[8,128,2048]{2,1,0:T(8,128)(2,1)}, u32[]{:S(2)}, u32[]{:S(2)}) async-start(bf16[8,128,2048]{2,1,0:T(8,128)(2,1)} %bitcast.221), calls=%async_computation.12 | async-start | bytes 8388608 | tf_op jit(solution)/shard_map/all_to_all | solution.py:48
  595.9 59.6 %collective-permute-start.26 = (bf16[128,2048]{1,0:T(8,128)(2,1)S(1)}, bf16[128,2048]{1,0:T(8,128)(2,1)S(1)}, u32[]{:S(2)}, u32[]{:S(2)}) collective-permute-start(bf16[128,2048]{1,0:T(8,128)(2,1)S(1)} %fusion.10), channel_id=1, source_target_pairs={{0,1},{1,0},{2,3},{3,2},{4,5},{5,4},{6,7},{7,6},{8,9},{9,8},{10,11... | collective-permute-start | bytes 1572872 | tf_op jit(solution)/shard_map/ppermute | solution.py:76
  650.3 17.2 %all-to-all-start.11 = ((bf16[8,64,512]{2,1,0:T(8,128)(2,1)}), bf16[8,64,512]{2,1,0:T(8,128)(2,1)S(1)}, u32[]{:S(2)}, u32[]{:S(2)}) async-start(bf16[8,64,512]{2,1,0:T(8,128)(2,1)} %bitcast.101), calls=%async_computation.13 | async-start | bytes 1048576 | tf_op jit(solution)/shard_map/all_to_all | solution.py:48
  660.5 17.6 %collective-permute-start.27 = (bf16[128,2048]{1,0:T(8,128)(2,1)}, bf16[128,2048]{1,0:T(8,128)(2,1)}, u32[]{:S(2)}, u32[]{:S(2)}) collective-permute-start(bf16[128,2048]{1,0:T(8,128)(2,1)} %reduce_sum.141), channel_id=1, source_target_pairs={{0,1},{1,0},{2,3},{3,2},{4,5},{5,4},{6,7},{7,6},{8,9},{9,8},{10,11... | collective-permute-start | bytes 1572872 | tf_op jit(solution)/shard_map/ppermute | solution.py:76
  (77 other events, 1272.0 us)
Sparse Core Ops, SparseCore 0:
  13.9 69.5 all-gather.2
  85.2 57.3 all-gather.4
  494.8 54.0 reduce-scatter.2
  586.2 33.2 reduce-scatter.4

commit v4 on v3

--- a/solution.py
+++ b/solution.py
@@ -67,6 +67,24 @@
     return lax.ppermute(value, axis, [(0, 1), (1, 0)])
 
 
+def gather_sum(value, x, yh):
+    def rows(i):
+        return lax.dynamic_slice(value, ((x + i) % 4 * 256, 0), (256, D))
+
+    far, plus, minus, own = rows(2), rows(1), rows(3), rows(0)
+    from_behind = ahead(far[:, :SIDE], "x", 1)
+    from_front = ahead(far[:, SIDE:], "x", 3)
+    plus = jnp.concatenate([plus[:, :SIDE] + from_behind, plus[:, SIDE:]], axis=1)
+    minus = jnp.concatenate([minus[:, :SIDE], minus[:, SIDE:] + from_front], axis=1)
+    total = own.astype(f32) + ahead(plus, "x", 1).astype(f32)
+    total = (total + ahead(minus, "x", 3).astype(f32)).astype(bf16)
+    mine = lax.dynamic_slice(total, (yh * 128, 0), (128, D))
+    other = lax.dynamic_slice(total, ((1 - yh) * 128, 0), (128, D))
+    mine, other = lax.optimization_barrier((mine, other))
+    across = lax.ppermute(other, ("yh", "ep"), [(n, 3 - n) for n in range(4)])
+    return mine, swap(mine, "ep"), swap(other, "yh"), across
+
+
 def below(a, b):
     return jnp.stack([(a - i) % 4 * 2 + (b - j) % 2 for i, j in OFFSETS])
 
@@ -107,6 +125,24 @@
     row = lax.broadcasted_iota(jnp.int32, (WINDOW, 1), 0)
     place = (row & 127) + ((row >> 7) & 1) * 256 + (row >> 8) * 128 + index * WINDOW
     return place < end
+
+
+def pack_kernel(line_ref, router_ref, query_ref, key_ref, value_ref, out_ref):
+    row = lax.broadcasted_iota(jnp.int32, (32, 128), 0)
+    lane = lax.broadcasted_iota(jnp.int32, (32, 128), 1)
+    gains = jnp.where(lane & 31 == row, line_ref[:, :128], 0.0).astype(bf16)
+    marks = jnp.where(lane >> 2 == row, line_ref[:, 128:], 0.0).astype(bf16)
+    row = lax.broadcasted_iota(jnp.int32, (128, 128), 0)
+    lane = lax.broadcasted_iota(jnp.int32, (128, 128), 1)
+    gain_place = jnp.where(lane == 64 + (row >> 5), 1.0, 0.0).astype(bf16)
+    mark_place = jnp.where(lane == 68 + (row & 3), 1.0, 0.0).astype(bf16)
+    small = jnp.concatenate([router_ref[...].astype(f32), jnp.zeros((32, 64), f32)], axis=1)
+    small = (small + dot(gains, gain_place) + dot(marks, mark_place)).astype(bf16)
+    for n in range(8):
+        here = slice(n * 32, n * 32 + 32)
+        for part, ref in enumerate((query_ref, key_ref, value_ref)):
+            out_ref[here, part * HD : part * HD + HD] = ref[:, n * HD : n * HD + HD]
+        out_ref[here, 3 * HD :] = small
 
 
 def project_kernel(place_ref, *refs):
@@ -158,19 +194,33 @@
         kv_ref[here, HD:] = raw[:, 2 * HD :].astype(bf16)
 
 
-def back_kernel(raw_ref, normed_ref, weight_ref, gain_ref, back_ref, total_ref):
+def spread_kernel(
+    place_ref,
+    raw_ref,
+    normed_ref,
+    weight_ref,
+    router_ref,
+    gain_ref,
+    mixture_ref,
+    head_ref,
+    output_ref,
+    back_ref,
+    share_ref,
+):
     total = jnp.zeros((1, D), f32)
     for n in range(4):
         here = slice(n * 256, n * 256 + 256)
         part = dot(raw_ref[here, :], weight_ref[...], ((1,), (1,)))
         total = total + jnp.sum(part * normed_ref[here, :].astype(f32), axis=0, keepdims=True)
         back_ref[here, :] = part.astype(bf16)
-    total_ref[...] = total / gain_ref[0:1, :]
-
-
-def share_kernel(raw_ref, normed_ref, router_ref, extra_ref, total_ref, output_ref, share_ref):
+    total = total / gain_ref[0:1, :]
     row = lax.broadcasted_iota(jnp.int32, (8, 1), 0)
-    extra = extra_ref[...] + jnp.where(row == 0, total_ref[...], 0.0)
+    feature = lax.broadcasted_iota(jnp.int32, (HD, D), 0)
+    place = lax.broadcasted_iota(jnp.int32, (HD, D), 1)
+    match = (place >> 8 == place_ref[0]) & (place & 31 < 16)
+    match = match & (((place >> 5) & 7) * 16 + (place & 31) == feature)
+    extra = dot(head_ref[...].astype(bf16), jnp.where(match, 1.0, 0.0).astype(bf16))
+    extra = extra + jnp.where(row == 0, total, 0.0) + jnp.where(row == 1, mixture_ref[...], 0.0)
     for n in range(4):
         band = slice(n * 512, n * 512 + 512)
         part = dot(normed_ref[:, band], raw_ref[...], ((0,), (0,))).astype(bf16)
@@ -189,21 +239,21 @@
                 share_ref[there, :] = output_ref[m * 32 : m * 32 + 32, :].astype(bf16)
 
 
-def finish_kernel(place_ref, share_ref, query_ref, key_ref, value_ref, output_ref, extra_ref):
+def finish_kernel(
+    place_ref, share_ref, own_ref, other_ref, query_ref, key_ref, value_ref, output_ref, extra_ref
+):
     total = None
     for n in range(8):
-        rows = share_ref[n * 64 : n * 64 + 32, :].astype(f32)
+        rows = share_ref[n * 32 : n * 32 + 32, :].astype(f32)
         for part, ref in enumerate((query_ref, key_ref, value_ref)):
             ref[:, n * HD : n * HD + HD] = rows[:, part * HD : part * HD + HD]
         total = rows[:, 3 * HD :] if n == 0 else total + rows[:, 3 * HD :]
     extra_ref[...] = total
-    for yh in range(2):
-        start = pl.multiple_of((place_ref[0] * 2 + yh) * 64 + 32, 32)
-        rows = share_ref[pl.ds(start, 32), :].astype(f32)
-        rows = jnp.concatenate([rows, jnp.zeros((96, 512), f32)], axis=0).T
+    for ref, group in ((own_ref, place_ref[0]), (other_ref, 1 - place_ref[0])):
+        rows = jnp.concatenate([ref[...].astype(f32), jnp.zeros((96, 512), f32)], axis=0).T
         for m in range(4):
-            there = (m * 2 + yh) * HD
-            output_ref[there : there + HD, :] = rows[m * HD : m * HD + HD, :32]
+            there = pl.ds(pl.multiple_of((m * 2 + group) * HD, HD), HD)
+            output_ref[there, :] = rows[m * HD : m * HD + HD, :32]
 
 
 def attend_kernel(
@@ -428,6 +478,17 @@
     return jax.ShapeDtypeStruct((rows, columns), kind)
 
 
+def pack(*values):
+    return pl.pallas_call(
+        pack_kernel,
+        out_shape=shape(256, 4 * HD),
+        in_specs=[VMEM] * 5,
+        out_specs=VMEM,
+        compiler_params=params,
+        cost_estimate=cheap,
+    )(*values)
+
+
 def project(places, inputs, weights, cosine, sine):
     return pl.pallas_call(
         project_kernel,
@@ -450,29 +511,18 @@
     )(places, *inputs, *weights, cosine, sine)
 
 
-def back_grads(raw_grads, normed, weights, gains):
+def spread_grads(*values):
     return pl.pallas_call(
-        back_kernel,
-        out_shape=(shape(1024, D), shape(1, D, f32)),
-        in_specs=[VMEM] * 4,
+        spread_kernel,
+        out_shape=(shape(1024, D), shape(2560, 512)),
+        in_specs=[SMEM] + [VMEM] * 8,
         out_specs=(VMEM, VMEM),
         compiler_params=params,
         cost_estimate=cheap,
-    )(raw_grads, normed, weights, gains)
-
-
-def share_grads(*values):
-    return pl.pallas_call(
-        share_kernel,
-        out_shape=shape(2560, 512),
-        in_specs=[VMEM] * 6,
-        out_specs=VMEM,
-        compiler_params=params,
-        cost_estimate=dear,
     )(*values)
 
 
-def finish(place, shares):
+def finish(*values):
     return pl.pallas_call(
         finish_kernel,
         out_shape=(
@@ -482,11 +532,11 @@
             shape(8 * HD, 32, f32),
             shape(32, 128, f32),
         ),
-        in_specs=[SMEM, VMEM],
+        in_specs=[SMEM] + [VMEM] * 3,
         out_specs=(VMEM,) * 5,
         compiler_params=params,
         cost_estimate=dear,
-    )(place, shares)
+    )(*values)
 
 
 def expert_pull(side, own, other, down):
@@ -636,25 +686,9 @@
     side_place = side.reshape(1).astype(jnp.int32)
     heads_below = below(x, yh)
 
-    pad = lambda gain: jnp.pad(gain, (0, 16))[:, None]
-    small = jnp.concatenate(
-        [
-            router_weight,
-            attention_gain[:, None],
-            mixture_gain[:, None],
-            pad(query_gain),
-            pad(key_gain),
-            blocks.astype(bf16).reshape(32, 4),
-            jnp.zeros((32, 56), bf16),
-        ],
-        axis=1,
-    )
-    weights_sent = jnp.concatenate(
-        [w.reshape(32, 8, HD) for w in (query_weight, key_weight, value_weight)]
-        + [jnp.broadcast_to(small[:, None], (32, 8, 128))],
-        axis=2,
-    )
-    weights_sent = weights_sent.transpose(1, 0, 2).reshape(256, 4 * HD)
+    line = [attention_gain, mixture_gain, jnp.pad(query_gain, (0, 16)), jnp.pad(key_gain, (0, 16))]
+    line = jnp.concatenate([v.astype(f32) for v in line + [blocks]])[None]
+    weights_sent = pack(line, router_weight, query_weight, key_weight, value_weight)
     inputs_pair = swap(inputs, "yh")
     inputs_all = [ring(inputs, "x"), ring(inputs_pair, "x")]
     inputs_all = [part for i, j in OFFSETS for part in inputs_all[j][i]]
@@ -707,22 +741,23 @@
 
     kv_some, output_all = lax.optimization_barrier((kv_some, output_all))
     kv_some = lax.all_gather(kv_some, TOKENS, axis=0, tiled=True)
-    grad_rows, squares = lax.optimization_barrier((grad_rows, squares))
+    own_blocks = blocks_all.reshape(4, 4, 2, 2, 128)[:, z, :, c].reshape(1024)
+    end = jnp.sum((blocks_all[:, None] <= own_blocks[None, :]).astype(jnp.int32), axis=0)[None]
+    squares = linger(squares)
+    grad_rows, squares, end = lax.optimization_barrier((grad_rows, squares, end))
     squares = sum_over_rows(squares)
     grad_rows, squares = lax.optimization_barrier((grad_rows, squares))
     grad_other = swap(grad_rows, "ep")
     group_inverse = lax.rsqrt(squares / float(D) + epsilon)
     inverses = group_inverse[8:]
-    inverses = ring(jnp.stack([inverses, swap(inverses, "c")]), "z")
-    inverses = jnp.concatenate([part for parts in inverses for part in parts])
+    inverses = jnp.stack([inverses, swap(inverses, "c")])
+    inverses = jnp.concatenate([inverses] + [ahead(inverses, "z", i) for i in (1, 2, 3)])
     inverses = jnp.take(inverses, below(z, c), axis=0).reshape(8, 1024)
     group_inverse = group_inverse.reshape(2, 1024)
     query_inverse = group_inverse[0][:, None]
     key_inverse = group_inverse[1][:, None]
     query_factor = group_inverse[0:1] * (scale * log2e)
     query_low = (query_some.astype(f32) * query_inverse).astype(bf16)
-    own_blocks = blocks_all.reshape(4, 4, 2, 2, 128)[:, z, :, c].reshape(1024)
-    end = jnp.sum((blocks_all[:, None] <= own_blocks[None, :]).astype(jnp.int32), axis=0)[None]
     kv_some, end, query_low = lax.optimization_barrier((kv_some, end, query_low))
     attended, lse, kv = attend(
         z_place, query_some, query_factor, kv_some, inverses, end
@@ -821,34 +856,37 @@
     key_gain_part = jnp.sum(key_normed_grad * key_raw * key_inverse, axis=0)
     raw_grads = jnp.concatenate([query_raw_low, key_raw_low, value_grad_low], axis=1)
 
-    def head_part(value):
-        wide = lax.dynamic_update_slice(jnp.zeros((8 * HD,), f32), value, (head * HD,))
-        return jnp.pad(wide.reshape(64, 16), ((0, 0), (0, 16))).reshape(1, D)
-
-    extra = jnp.concatenate(
+    head_gains = jnp.concatenate(
         [
-            jnp.zeros((1, D), f32),
-            mixture_gain_part[None],
-            head_part(query_gain_part),
-            head_part(key_gain_part),
-            jnp.zeros((4, D), f32),
+            jnp.zeros((2, HD), f32),
+            query_gain_part[None],
+            key_gain_part[None],
+            jnp.zeros((4, HD), f32),
         ],
         axis=0,
     )
-    normed_part, gain_total = back_grads(raw_grads, normed_low, weights_all, gain_rows)
-    normed_back = exchange(normed_part, HEADS)
-    shares = share_grads(raw_grads, normed_low, router_part, extra, gain_total, output_part)
+    normed_part, shares = spread_grads(
+        head.reshape(1).astype(jnp.int32),
+        raw_grads,
+        normed_low,
+        weights_all,
+        router_part,
+        gain_rows,
+        mixture_gain_part[None],
+        head_gains,
+        output_part,
+    )
 
     summed = lax.psum_scatter(shares, TOKENS, scatter_dimension=0, tiled=True)
-    output_sum = jnp.broadcast_to(summed[256:].reshape(1, 2, 32, 512), (4, 2, 32, 512))
-    shares = jnp.concatenate(
-        [summed[:256].reshape(8, 32, 512), output_sum.reshape(8, 32, 512)], axis=1
-    )
-    shares, normed_back = lax.optimization_barrier((shares.reshape(512, 512), normed_back))
-    shares = exchange(shares, HEADS)
-    normed_grad = pair_sum(jnp.sum(normed_back.reshape(8, 128, D).astype(f32), axis=0))
+    output_own = lax.dynamic_slice(summed, (256 + yh * 32, 0), (32, 512))
+    output_other = swap(lax.dynamic_slice(summed, (288 - yh * 32, 0), (32, 512)), "yh")
+    shares, output_other, normed_sums = lax.optimization_barrier(
+        (exchange(summed[:256], HEADS), output_other, gather_sum(normed_part, x, yh))
+    )
+    normed_sums = [part.astype(f32) for part in normed_sums]
+    normed_grad = (normed_sums[0] + normed_sums[1]) + (normed_sums[2] + normed_sums[3])
     query_part, key_part, value_part, output_grad, extra = finish(
-        x.reshape(1).astype(jnp.int32), shares
+        yh.reshape(1).astype(jnp.int32), shares, output_own, output_other
     )
     pair = extra + swap(extra, "ep")
     router_grad = pair[:, :64]

time: 700 us -> 667 us (0.953)
  waiting for transfers between devices: 288 us -> 247 us
  starting transfers between devices: 123 us -> 136 us
  local copies, waits for them, and re-layouts: 49.1 us -> 39.3 us
    all_to_all x12 -> x11, waiting for transfers between devices: 206 us -> 155 us  [exchange(): return lax.all_to_all(value, axes, split_axis=0, concat_axis=0, tiled=True)]
    reduce_scatter x1, waiting for transfers between devices: 23 us -> 0.01 us  [local(): summed = lax.psum_scatter(shares, TOKENS, scatter_dimension=0, tiled=True)]
    ppermute x20 -> x23, waiting for transfers between devices: 28.2 us -> 48.6 us  [ahead(): return lax.ppermute(value, axis, [(a, (a + steps) % 4) for a in range(4)])]
    ppermute x5 -> x8, waiting for transfers between devices: 1.41 us -> 13.5 us  [swap(): return lax.ppermute(value, axis, [(0, 1), (1, 0)])]
    ppermute x20 -> x23, starting transfers between devices: 22.4 us -> 30.8 us  [ahead(): return lax.ppermute(value, axis, [(a, (a + steps) % 4) for a in range(4)])]
    ppermute x4 -> x3, waiting for transfers between devices: 16.9 us -> 17.7 us  [pair_sum(): other = lax.ppermute(own, 'ep', [(0, 1), (1, 0)])]
    all_to_all x12 -> x11, starting transfers between devices: 87.9 us -> 87.4 us  [exchange(): return lax.all_to_all(value, axes, split_axis=0, concat_axis=0, tiled=True)]
  transfers between devices with their start and end apart: 45 -> 50, of which waited for: 29 -> 30; matrix products, arithmetic and copies ran while one was open for 15% -> 16% of each run, Pallas kernels for 13% -> 14%
where the time goes in v4:
time: 667 us; the launch traced here: 656 us
  waiting for transfers between devices  247 us (37%)
  starting transfers between devices  136 us (20%)
  Pallas kernels  127 us (19%)
  other arithmetic  48.1 us (7%)
  matrix products  42.4 us (6%)
  local copies, waits for them, and re-layouts  39.3 us (6%)
  between operations  15.2 us (2%)
    all_to_all x11, waiting for transfers between devices, exchange(): return lax.all_to_all(value, axes, split_axis=0, concat_axis=0, tiled=True)  155 us
    all_to_all x11, starting transfers between devices, exchange(): return lax.all_to_all(value, axes, split_axis=0, concat_axis=0, tiled=True)  87.4 us
    ppermute x23, waiting for transfers between devices, ahead(): return lax.ppermute(value, axis, [(a, (a + steps) % 4) for a in range(4)])  48.6 us
    dot_general x16, matrix products, dot(): lax.dot_general(first, second, (dims, ((), ())), preferred_element_type=f32)  42.4 us
    ppermute x23, starting transfers between devices, ahead(): return lax.ppermute(value, axis, [(a, (a + steps) % 4) for a in range(4)])  30.8 us
    pallas_call x1, Pallas kernels, attend(): pl.pallas_call(attend_kernel, out_shape=(shape(1024, HD, f32), shape(1, 1...  30.8 us
    pallas_call x1, Pallas kernels, attend_back(): pl.pallas_call(attend_back_kernel, out_shape=(shape(1024, HD, f32), shape...  29.4 us
    pallas_call x1, Pallas kernels, expert_step(): pl.pallas_call(expert_kernel, grid=(2,), out_shape=(shape(1024, ROW_WIDTH...  23 us
  transfers between devices with their start and end apart: 50, of which 30 were waited for; matrix products, arithmetic and copies ran while one was open for 16% of the time, Pallas kernels for 14%

profile of v4, /device:TPU:96, one launch (start us, length us, event | category | flops | bytes accessed | tf_op | source)
XLA Modules:
  0.0 655.9 jit_solution(12493632292823943571)
XLA Ops:
  69.2 9.5 %all-to-all-start.1 = ((bf16[64,16,1280]{2,1,0:T(8,128)(2,1)}), bf16[64,16,1280]{2,1,0:T(8,128)(2,1)}, u32[]{:S(2)}, u32[]{:S(2)}) async-start(bf16[64,16,1280]{2,1,0:T(8,128)(2,1)} %bitcast.29), calls=%async_computation.1 | async-start | bytes 5242880 | tf_op jit(solution)/shard_map/all_to_all | solution.py:48
  78.7 11.3 %shard_map.264 = (bf16[1024,2048]{1,0:T(8,128)(2,1)}, f32[1024,256]{1,0:T(8,128)}, bf16[1024,128]{1,0:T(8,128)(2,1)}, bf16[1024,256]{1,0:T(8,128)(2,1)}, f32[16,...) custom-call(s32[17]{0:T(128)} %concatenate.64.place_ref, ...), custom_call_target="tpu_custom_call" | custom-call | flops 49999998976 | bytes 1 | tf_op jit(solution)/shard_map/pallas_call | solution.py:493
  97.5 15.0 %all-to-all-done.1 = bf16[64,16,1280]{2,1,0:T(8,128)(2,1)} async-done(((bf16[64,16,1280]{2,1,0:T(8,128)(2,1)}), bf16[64,16,1280]{2,1,0:T(8,128)(2,1)}, u32[]{:S(2)}, u32[]{:S(2)}) %all-to-all-start.1) | async-done | bytes 2621472 | tf_op jit(solution)/shard_map/all_to_all | solution.py:48
  120.5 7.7 %all-to-all-done.2 = f32[16,16,128]{2,1,0:T(8,128)S(1)} async-done(((f32[16,16,128]{2,1,0:T(8,128)}), f32[16,16,128]{2,1,0:T(8,128)S(1)}, u32[]{:S(2)}, u32[]{:S(2)}) %all-to-all-start.2) | async-done | bytes 131104 | tf_op jit(solution)/shard_map/all_to_all | solution.py:48
  139.2 30.8 %shard_map.266 = (f32[1024,128]{1,0:T(8,128)}, f32[1,1024]{1,0:T(1,128)}, bf16[8192,256]{1,0:T(8,128)(2,1)}) custom-call(s32[1]{0:T(128)} %bitcast.z_ref, bf16[1024,128]{1,0:T(8,128)(2,1)} %get-tuple-element.113.q_ref.raw_ref, f32[1,1024]{1,0:T(1,128)} %bitcast.227, bf16[8192,256]{1,0:T(8,128)(2,1)} %all-gather.5.cloned.1.call-done.raw_ref, ...), custom_call_target="tpu_custom_call" | custom-call | flops 1 | bytes 1 | tf_op jit(solution)/shard_map/pallas_call | solution.py:619
  194.3 7.9 %collective-permute-done.23 = bf16[128,2048]{1,0:T(8,128)(2,1)S(1)} collective-permute-done((bf16[128,2048]{1,0:T(8,128)(2,1)S(1)}, bf16[128,2048]{1,0:T(8,128)(2,1)S(1)}, u32[]{:S(2)}, u32[]{:S(2)}) %collective-permute-start.23) | collective-permute-done | bytes 524320 | tf_op jit(solution)/shard_map/ppermute | solution.py:94
  207.5 10.5 %all-to-all-start.4 = ((bf16[64,16,2560]{2,1,0:T(8,128)(2,1)}), bf16[64,16,2560]{2,1,0:T(8,128)(2,1)}, u32[]{:S(2)}, u32[]{:S(2)}) async-start(bf16[64,16,2560]{2,1,0:T(8,128)(2,1)} %bitcast.181), calls=%async_computation.4 | async-start | bytes 10485760 | tf_op jit(solution)/shard_map/all_to_all | solution.py:48
  218.6 7.4 %shard_map.267 = (bf16[1280,2048]{1,0:T(8,128)(2,1)}, f32[1280,512]{1,0:T(8,128)}) custom-call(s32[1]{0:T(128)} %bitcast.60.side_ref, bf16[1024,1280]{1,0:T(8,128)(2,1)} %bitcast.30.own_ref, bf16[1024,1280]{1,0:T(8,128)(2,1)} %collective-permute-done.22.other_ref, bf16[512,2048]{1,0:T(8,128)(2,1)} %bitcast.182), custom_call_target="tpu_custom_call" | custom-call | flops 1 | bytes 1 | tf_op jit(solution)/shard_map/pallas_call | solution.py:543
  233.2 49.9 %all-to-all-done.4 = bf16[64,16,2560]{2,1,0:T(8,128)(2,1)} async-done(((bf16[64,16,2560]{2,1,0:T(8,128)(2,1)}), bf16[64,16,2560]{2,1,0:T(8,128)(2,1)}, u32[]{:S(2)}, u32[]{:S(2)}) %all-to-all-start.4) | async-done | bytes 5242912 | tf_op jit(solution)/shard_map/all_to_all | solution.py:48
  283.1 23.0 %shard_map.268 = (bf16[1024,2560]{1,0:T(8,128)(2,1)}, bf16[1280,2048]{1,0:T(8,128)(2,1)}, bf16[1280,512]{1,0:T(8,128)(2,1)}, bf16[1280,512]{1,0:T(8,128)(2,1)}, ...) custom-call(s32[1]{0:T(128)} %bitcast.50.place_ref, bf16[1024,2560]{1,0:T(8,128)(2,1)} %bitcast.55.rows_ref, ...), custom_call_target="tpu_custom_call" | custom-call | flops 1 | bytes 1 | tf_op jit(solution)/shard_map/pallas_call | solution.py:560
  306.1 14.4 %all-to-all-start.5 = ((bf16[64,16,2560]{2,1,0:T(8,128)(2,1)}), bf16[64,16,2560]{2,1,0:T(8,128)(2,1)}, u32[]{:S(2)}, u32[]{:S(2)}) async-start(bf16[64,16,2560]{2,1,0:T(8,128)(2,1)} %bitcast.186), calls=%async_computation.5 | async-start | bytes 10485760 | tf_op jit(solution)/shard_map/all_to_all | solution.py:48
  340.6 44.9 %all-to-all-done.5 = bf16[64,16,2560]{2,1,0:T(8,128)(2,1)} async-done(((bf16[64,16,2560]{2,1,0:T(8,128)(2,1)}), bf16[64,16,2560]{2,1,0:T(8,128)(2,1)}, u32[]{:S(2)}, u32[]{:S(2)}) %all-to-all-start.5) | async-done | bytes 5242912 | tf_op jit(solution)/shard_map/all_to_all | solution.py:48
  395.7 9.8 %collective-permute-done.24 = bf16[128,2048]{1,0:T(8,128)(2,1)S(1)} collective-permute-done((bf16[128,2048]{1,0:T(8,128)(2,1)S(1)}, bf16[128,2048]{1,0:T(8,128)(2,1)S(1)}, u32[]{:S(2)}, u32[]{:S(2)}) %collective-permute-start.24) | collective-permute-done | bytes 524320 | tf_op jit(solution)/shard_map/ppermute | solution.py:94
  415.3 8.3 %shard_map.269 = bf16[1024,2560]{1,0:T(8,128)(2,1)} custom-call(bf16[1280,512]{1,0:T(8,128)(2,1)} %get-tuple-element.139.hidden_ref, bf16[512,2048]{1,0:T(8,128)(2,1)} %bitcast.183), custom_call_target="tpu_custom_call" | custom-call | flops 1 | bytes 1 | tf_op jit(solution)/shard_map/pallas_call | solution.py:593
  423.7 14.5 %all-to-all-start.7 = ((bf16[64,16,2560]{2,1,0:T(8,128)(2,1)}), bf16[64,16,2560]{2,1,0:T(8,128)(2,1)}, u32[]{:S(2)}, u32[]{:S(2)}) async-start(bf16[64,16,2560]{2,1,0:T(8,128)(2,1)} %bitcast.180), calls=%async_computation.7 | async-start | bytes 10485760 | tf_op jit(solution)/shard_map/all_to_all | solution.py:48
  441.9 29.4 %shard_map.270 = (f32[1024,128]{1,0:T(8,128)}, bf16[8192,256]{1,0:T(8,128)(2,1)}) custom-call(s32[1]{0:T(128)} %bitcast.z_ref, bf16[1024,128]{1,0:T(8,128)(2,1)} %get-tuple-element.113.q_ref.raw_ref, f32[1,1024]{1,0:T(1,128)} %bitcast.228, bf16[1024,128]{1,0:T(8,128)(2,1)} %multiply_convert_fusion.1.q_ref, bf16[1024,128]{1,0:T(8,128)(2,1)} %bitcast.195, ...), custom_call_target="tpu_custom_call" | custom-call | flops 1 | bytes 1 | tf_op jit(solution)/shard_map/pallas_call | solution.py:630
  471.3 32.2 %all-to-all-done.7 = bf16[64,16,2560]{2,1,0:T(8,128)(2,1)} async-done(((bf16[64,16,2560]{2,1,0:T(8,128)(2,1)}), bf16[64,16,2560]{2,1,0:T(8,128)(2,1)}, u32[]{:S(2)}, u32[]{:S(2)}) %all-to-all-start.7) | async-done | bytes 5242912 | tf_op jit(solution)/shard_map/all_to_all | solution.py:48
  505.1 7.1 %all-to-all-start.8 = ((bf16[8,128,512]{2,1,0:T(8,128)(2,1)}), bf16[8,128,512]{2,1,0:T(8,128)(2,1)}, u32[]{:S(2)}, u32[]{:S(2)}) async-start(bf16[8,128,512]{2,1,0:T(8,128)(2,1)} %bitcast.80), calls=%async_computation.8 | async-start | bytes 2097152 | tf_op jit(solution)/shard_map/all_to_all | solution.py:48
  514.2 10.1 %reduce-scatter.3.cloned.1.call-done = bf16[1024,256]{1,0:T(8,128)(2,1)} async-done(((bf16[8192,256]{1,0:T(8,128)(2,1)}), bf16[1024,256]{1,0:T(8,128)(2,1)}) %reduce-scatter.3.cloned.1.call-update) | async-done | bytes 524304 | tf_op jit(solution)/shard_map/reduce_scatter | solution.py:829
  546.8 9.9 %shard_map.272 = (bf16[1024,2048]{1,0:T(8,128)(2,1)}, bf16[2560,512]{1,0:T(8,128)(2,1)}) custom-call(s32[1]{0:T(128)} %bitcast.17.place_ref, bf16[1024,384]{1,0:T(8,128)(2,1)} %pad_maximum_fusion.4.raw_ref, bf16[1024,2048]{1,0:T(8,128)(2,1)} %get-tuple-element.159.normed_ref, bf16[2048,384]{1,0:T(8,128)(2,1)} %get-tuple-element.160.weight_ref, ...), custom_call_target="tpu_custom_call" | custom-call | flops 1 | bytes 1 | tf_op jit(solution)/shard_map/pallas_call | solution.py:515
  561.3 11.8 %collective-permute-done.27 = bf16[256,1024]{1,0:T(8,128)(2,1)S(1)} collective-permute-done((bf16[256,1024]{1,0:T(8,128)(2,1)S(1)}, bf16[256,1024]{1,0:T(8,128)(2,1)S(1)}, u32[]{:S(2)}, u32[]{:S(2)}) %collective-permute-start.27) | collective-permute-done | bytes 524320 | tf_op jit(solution)/shard_map/ppermute | solution.py:55
  587.4 16.4 %collective-permute-done.28 = bf16[256,2048]{1,0:T(8,128)(2,1)S(1)} collective-permute-done((bf16[256,2048]{1,0:T(8,128)(2,1)}, bf16[256,2048]{1,0:T(8,128)(2,1)S(1)}, u32[]{:S(2)}, u32[]{:S(2)}) %collective-permute-start.28) | collective-permute-done | bytes 1048608 | tf_op jit(solution)/shard_map/ppermute | solution.py:55
  612.0 7.0 %all-to-all-start.10 = ((bf16[8,32,512]{2,1,0:T(8,128)(2,1)}), bf16[8,32,512]{2,1,0:T(8,128)(2,1)S(1)}, u32[]{:S(2)}, u32[]{:S(2)}) async-start(bf16[8,32,512]{2,1,0:T(8,128)(2,1)} %bitcast.91), calls=%async_computation.12 | async-start | bytes 524288 | tf_op jit(solution)/shard_map/all_to_all | solution.py:48
  626.2 8.5 %collective-permute-done.31 = bf16[128,2048]{1,0:T(8,128)(2,1)S(1)} collective-permute-done((bf16[128,2048]{1,0:T(8,128)(2,1)S(1)}, bf16[128,2048]{1,0:T(8,128)(2,1)S(1)}, u32[]{:S(2)}, u32[]{:S(2)}) %collective-permute-start.31) | collective-permute-done | bytes 524320 | tf_op jit(solution)/shard_map/ppermute | solution.py:67
  (351 shorter events, 243.4 us)
Async XLA Ops:
  7.2 82.8 %all-gather.3.cloned.1.call-start = ((), (), s32[]{:S(2)}) async-start(), calls=%async_computation.13 | async-start | bytes 4259840 | tf_op jit(solution)/shard_map/all_gather | solution.py:698
  7.9 27.4 %collective-permute-start = (bf16[128,2048]{1,0:T(8,128)(2,1)}, bf16[128,2048]{1,0:T(8,128)(2,1)}, u32[]{:S(2)}, u32[]{:S(2)}) collective-permute-start(bf16[128,2048]{1,0:T(8,128)(2,1)} %refs_0_), channel_id=1, source_target_pairs={{0,4},{4,0},{1,5},{5,1},{2,6},{6,2},{3,7},{7,3},{8,12},{12,8},{9,1... | collective-permute-start | bytes 1572872 | tf_op jit(solution)/shard_map/ppermute | solution.py:67
  11.2 24.9 %collective-permute-start.1 = (bf16[128,2048]{1,0:T(8,128)(2,1)}, bf16[128,2048]{1,0:T(8,128)(2,1)}, u32[]{:S(2)}, u32[]{:S(2)}) collective-permute-start(bf16[128,2048]{1,0:T(8,128)(2,1)} %refs_0_), channel_id=1, source_target_pairs={{0,32},{32,64},{64,96},{96,0},{1,33},{33,65},{65,97},{97,1},{2,34}... | collective-permute-start | bytes 1572872 | tf_op jit(solution)/shard_map/ppermute | solution.py:55
  12.7 28.3 %collective-permute-start.4 = (bf16[128,2048]{1,0:T(8,128)(2,1)}, bf16[128,2048]{1,0:T(8,128)(2,1)}, u32[]{:S(2)}, u32[]{:S(2)}) collective-permute-start(bf16[128,2048]{1,0:T(8,128)(2,1)} %refs_0_), channel_id=1, source_target_pairs={{0,96},{32,0},{64,32},{96,64},{1,97},{33,1},{65,33},{97,65},{2,98}... | collective-permute-start | bytes 1572872 | tf_op jit(solution)/shard_map/ppermute | solution.py:55
  35.3 17.9 %collective-permute-start.2 = (bf16[128,2048]{1,0:T(8,128)(2,1)}, bf16[128,2048]{1,0:T(8,128)(2,1)S(1)}, u32[]{:S(2)}, u32[]{:S(2)}) collective-permute-start(bf16[128,2048]{1,0:T(8,128)(2,1)} %collective-permute-done.refs_1_), channel_id=1, source_target_pairs={{0,32},{32,64},{64,96},{96,0},{1,33},{33,65},{65,97},{97,1},{2,34}... | collective-permute-start | bytes 1572872 | tf_op jit(solution)/shard_map/ppermute | solution.py:55
  36.1 17.2 %collective-permute-start.7 = (bf16[128,2048]{1,0:T(8,128)(2,1)}, bf16[128,2048]{1,0:T(8,128)(2,1)}, u32[]{:S(2)}, u32[]{:S(2)}) collective-permute-start(bf16[128,2048]{1,0:T(8,128)(2,1)} %collective-permute-done.refs_1_), channel_id=1, source_target_pairs={{0,96},{32,0},{64,32},{96,64},{1,97},{33,1},{65,33},{97,65},{2,98}... | collective-permute-start | bytes 1572872 | tf_op jit(solution)/shard_map/ppermute | solution.py:55
  41.0 18.9 %collective-permute-start.3 = (bf16[64,2048]{1,0:T(8,128)(2,1)S(1)}, bf16[64,2048]{1,0:T(8,128)(2,1)S(1)}, u32[]{:S(2)}, u32[]{:S(2)}) collective-permute-start(bf16[64,2048]{1,0:T(8,128)(2,1)S(1)} %slice.190), channel_id=1, source_target_pairs={{0,32},{32,64},{64,96},{96,0},{1,33},{33,65},{65,97},{97,1},{2,34}... | collective-permute-start | bytes 786440 | tf_op jit(solution)/shard_map/ppermute | solution.py:55
  69.2 43.3 %all-to-all-start.1 = ((bf16[64,16,1280]{2,1,0:T(8,128)(2,1)}), bf16[64,16,1280]{2,1,0:T(8,128)(2,1)}, u32[]{:S(2)}, u32[]{:S(2)}) async-start(bf16[64,16,1280]{2,1,0:T(8,128)(2,1)} %bitcast.29), calls=%async_computation.1 | async-start | bytes 5242880 | tf_op jit(solution)/shard_map/all_to_all | solution.py:48
  78.7 60.6 %all-gather.5.cloned.1.call-start = ((), (), s32[]{:S(2)}) async-start(), calls=%async_computation.14 | async-start | bytes 4718592 | tf_op jit(solution)/shard_map/all_gather | solution.py:743
  128.3 59.0 %collective-permute-start.22 = (bf16[1024,1280]{1,0:T(8,128)(2,1)}, bf16[1024,1280]{1,0:T(8,128)(2,1)}, u32[]{:S(2)}, u32[]{:S(2)}) collective-permute-start(bf16[1024,1280]{1,0:T(8,128)(2,1)} %bitcast.30.own_ref), channel_id=1, source_target_pairs={{0,1},{1,0},{2,3},{3,2},{4,5},{5,4},{6,7},{7,6},{8,9},{9,8},{10,11... | collective-permute-start | bytes 7864328 | tf_op jit(solution)/shard_map/ppermute | solution.py:67
  207.5 75.6 %all-to-all-start.4 = ((bf16[64,16,2560]{2,1,0:T(8,128)(2,1)}), bf16[64,16,2560]{2,1,0:T(8,128)(2,1)}, u32[]{:S(2)}, u32[]{:S(2)}) async-start(bf16[64,16,2560]{2,1,0:T(8,128)(2,1)} %bitcast.181), calls=%async_computation.4 | async-start | bytes 10485760 | tf_op jit(solution)/shard_map/all_to_all | solution.py:48
  306.1 79.4 %all-to-all-start.5 = ((bf16[64,16,2560]{2,1,0:T(8,128)(2,1)}), bf16[64,16,2560]{2,1,0:T(8,128)(2,1)}, u32[]{:S(2)}, u32[]{:S(2)}) async-start(bf16[64,16,2560]{2,1,0:T(8,128)(2,1)} %bitcast.186), calls=%async_computation.5 | async-start | bytes 10485760 | tf_op jit(solution)/shard_map/all_to_all | solution.py:48
  423.7 79.8 %all-to-all-start.7 = ((bf16[64,16,2560]{2,1,0:T(8,128)(2,1)}), bf16[64,16,2560]{2,1,0:T(8,128)(2,1)}, u32[]{:S(2)}, u32[]{:S(2)}) async-start(bf16[64,16,2560]{2,1,0:T(8,128)(2,1)} %bitcast.180), calls=%async_computation.7 | async-start | bytes 10485760 | tf_op jit(solution)/shard_map/all_to_all | solution.py:48
  438.2 86.1 %reduce-scatter.3.cloned.1.call-start = ((), (), s32[]{:S(2)}) async-start(), calls=%async_computation.15 | async-start | bytes 4718592 | tf_op jit(solution)/shard_map/reduce_scatter | solution.py:829
  505.1 25.2 %all-to-all-start.8 = ((bf16[8,128,512]{2,1,0:T(8,128)(2,1)}), bf16[8,128,512]{2,1,0:T(8,128)(2,1)}, u32[]{:S(2)}, u32[]{:S(2)}) async-start(bf16[8,128,512]{2,1,0:T(8,128)(2,1)} %bitcast.80), calls=%async_computation.8 | async-start | bytes 2097152 | tf_op jit(solution)/shard_map/all_to_all | solution.py:48
  536.1 74.2 %reduce-scatter.5.cloned.1.call-start = ((), (), s32[]{:S(2)}) async-start(), calls=%async_computation.16 | async-start | bytes 2949120 | tf_op jit(solution)/shard_map/reduce_scatter | solution.py:880
  576.2 27.6 %collective-permute-start.28 = (bf16[256,2048]{1,0:T(8,128)(2,1)}, bf16[256,2048]{1,0:T(8,128)(2,1)S(1)}, u32[]{:S(2)}, u32[]{:S(2)}) collective-permute-start(bf16[256,2048]{1,0:T(8,128)(2,1)} %pad_maximum_fusion.2), channel_id=1, source_target_pairs={{0,32},{32,64},{64,96},{96,0},{1,33},{33,65},{65,97},{97,1},{2,34}... | collective-permute-start | bytes 3145736 | tf_op jit(solution)/shard_map/ppermute | solution.py:55
  577.5 26.7 %collective-permute-start.30 = (bf16[256,2048]{1,0:T(8,128)(2,1)}, bf16[256,2048]{1,0:T(8,128)(2,1)S(1)}, u32[]{:S(2)}, u32[]{:S(2)}) collective-permute-start(bf16[256,2048]{1,0:T(8,128)(2,1)} %pad_maximum_fusion.3), channel_id=1, source_target_pairs={{0,96},{32,0},{64,32},{96,64},{1,97},{33,1},{65,33},{97,65},{2,98}... | collective-permute-start | bytes 3145736 | tf_op jit(solution)/shard_map/ppermute | solution.py:55
  587.0 36.9 %collective-permute-start.25 = (bf16[128,2048]{1,0:T(8,128)(2,1)}, bf16[128,2048]{1,0:T(8,128)(2,1)}, u32[]{:S(2)}, u32[]{:S(2)}) collective-permute-start(bf16[128,2048]{1,0:T(8,128)(2,1)} %fusion.10), channel_id=1, source_target_pairs={{0,1},{1,0},{2,3},{3,2},{4,5},{5,4},{6,7},{7,6},{8,9},{9,8},{10,11... | collective-permute-start | bytes 1572872 | tf_op jit(solution)/shard_map/ppermute | solution.py:94
  606.8 27.9 %collective-permute-start.32 = (bf16[128,2048]{1,0:T(8,128)(2,1)}, bf16[128,2048]{1,0:T(8,128)(2,1)S(1)}, u32[]{:S(2)}, u32[]{:S(2)}) collective-permute-start(bf16[128,2048]{1,0:T(8,128)(2,1)} %get-tuple-element.167), channel_id=1, source_target_pairs={{0,4},{4,0},{1,5},{5,1},{2,6},{6,2},{3,7},{7,3},{8,12},{12,8},{9,1... | collective-permute-start | bytes 1572872 | tf_op jit(solution)/shard_map/ppermute | solution.py:67
  608.3 27.8 %collective-permute-start.33 = (bf16[128,2048]{1,0:T(8,128)(2,1)}, bf16[128,2048]{1,0:T(8,128)(2,1)S(1)}, u32[]{:S(2)}, u32[]{:S(2)}) collective-permute-start(bf16[128,2048]{1,0:T(8,128)(2,1)} %get-tuple-element.167), channel_id=1, source_target_pairs={{0,5},{1,4},{4,1},{5,0},{2,7},{3,6},{6,3},{7,2},{8,13},{9,12},{12,... | collective-permute-start | bytes 1572872 | tf_op jit(solution)/shard_map/ppermute | solution.py:84
  610.0 24.8 %collective-permute-start.31 = (bf16[128,2048]{1,0:T(8,128)(2,1)S(1)}, bf16[128,2048]{1,0:T(8,128)(2,1)S(1)}, u32[]{:S(2)}, u32[]{:S(2)}) collective-permute-start(bf16[128,2048]{1,0:T(8,128)(2,1)S(1)} %get-tuple-element.168), channel_id=1, source_target_pairs={{0,1},{1,0},{2,3},{3,2},{4,5},{5,4},{6,7},{7,6},{8,9},{9,8},{10,11... | collective-permute-start | bytes 1572872 | tf_op jit(solution)/shard_map/ppermute | solution.py:67
  612.0 24.9 %all-to-all-start.10 = ((bf16[8,32,512]{2,1,0:T(8,128)(2,1)}), bf16[8,32,512]{2,1,0:T(8,128)(2,1)S(1)}, u32[]{:S(2)}, u32[]{:S(2)}) async-start(bf16[8,32,512]{2,1,0:T(8,128)(2,1)} %bitcast.91), calls=%async_computation.12 | async-start | bytes 524288 | tf_op jit(solution)/shard_map/all_to_all | solution.py:48
  620.4 16.5 %collective-permute-start.26 = (bf16[32,512]{1,0:T(8,128)(2,1)S(1)}, bf16[32,512]{1,0:T(8,128)(2,1)S(1)}, u32[]{:S(2)}, u32[]{:S(2)}) collective-permute-start(bf16[32,512]{1,0:T(8,128)(2,1)S(1)} %get-tuple-element.269), channel_id=1, source_target_pairs={{0,4},{4,0},{1,5},{5,1},{2,6},{6,2},{3,7},{7,3},{8,12},{12,8},{9,1... | collective-permute-start | bytes 98312 | tf_op jit(solution)/shard_map/ppermute | solution.py:67
  (86 other events, 1099.1 us)
Sparse Core Ops, SparseCore 0:
  11.2 77.2 all-gather.2
  90.2 39.6 all-gather.4
  471.5 52.7 reduce-scatter.2
  556.8 32.6 reduce-scatter.4

commit v5 on v4

--- a/solution.py
+++ b/solution.py
@@ -121,9 +121,18 @@
     return pl.multiple_of((index % 4) * 2048 + (index // 4) * 256, 256)
 
 
-def window_mask(index, end):
-    row = lax.broadcasted_iota(jnp.int32, (WINDOW, 1), 0)
-    place = (row & 127) + ((row >> 7) & 1) * 256 + (row >> 8) * 128 + index * WINDOW
+def window(ref, index, count):
+    parts = []
+    for n in range(count):
+        base = window_rows(index + n)
+        parts += [ref[pl.ds(base, 256), :], ref[pl.ds(base + 1024, 256), :]]
+    return jnp.concatenate(parts, axis=0)
+
+
+def window_mask(index, end, count):
+    row = lax.broadcasted_iota(jnp.int32, (WINDOW * count, 1), 0)
+    place = (row & 127) + ((row >> 7) & 1) * 256 + ((row >> 8) & 1) * 128
+    place = place + ((row >> 9) + index) * WINDOW
     return place < end
 
 
@@ -272,16 +281,13 @@
         end = end_ref[:, span]
         factor = factor_ref[:, span]
 
-        def tile(index, state, masked):
+        def tile(index, state, count, masked=False):
             peak, mass, total = state
-            base = window_rows(index)
-            part = jnp.concatenate(
-                [kv_ref[pl.ds(base, 256), :], kv_ref[pl.ds(base + 1024, 256), :]], axis=0
-            )
+            part = window(kv_ref, index, count)
             keys, values = part[:, :HD], part[:, HD:]
             scores = dot(keys, queries, ((1,), (1,)))
             if masked:
-                scores = jnp.where(window_mask(index, end), scores, masked_score)
+                scores = jnp.where(window_mask(index, end, count), scores, masked_score)
             new_peak = jnp.maximum(peak, jnp.max(scores, axis=0, keepdims=True))
             weights = jnp.exp2((scores - new_peak) * factor)
             shrink = jnp.exp2((peak - new_peak) * factor)
@@ -295,10 +301,10 @@
             jnp.zeros((HD, 256), f32),
         )
         last = 4 * x + z
-        state = lax.fori_loop(0, last, lambda i, s: tile(i, s, False), state)
-        state = lax.fori_loop(
-            last, jnp.minimum(last + 2, 16), lambda i, s: tile(i, s, True), state
-        )
+        state = lax.fori_loop(0, last // 4, lambda i, s: tile(4 * i, s, 4), state)
+        state = lax.fori_loop(last // 4 * 2, last // 2, lambda i, s: tile(2 * i, s, 2), state)
+        state = lax.fori_loop(last // 2 * 2, last, lambda i, s: tile(i, s, 1), state)
+        state = tile(last, state, 2, True)
         peak, mass, total = state
         out_ref[span, :] = (total / mass).T
         lse_ref[:, span] = peak * factor + jnp.log(mass) * log2e
@@ -330,32 +336,29 @@
         lse = lse_ref[:, span]
         delta = delta_ref[:, span]
 
-        def tile(index, total, masked):
-            base = window_rows(index)
-            part = jnp.concatenate(
-                [kv_ref[pl.ds(base, 256), :], kv_ref[pl.ds(base + 1024, 256), :]], axis=0
-            )
+        def tile(index, total, count, masked=False):
+            part = window(kv_ref, index, count)
             keys, values = part[:, :HD], part[:, HD:]
             scores = dot(keys, raw, ((1,), (1,))) * factor - lse
             if masked:
-                scores = jnp.where(window_mask(index, end), scores, masked_score)
+                scores = jnp.where(window_mask(index, end, count), scores, masked_score)
             chances = jnp.exp2(scores)
             value_dot = dot(values, grads, ((1,), (1,)))
             score_grad = (chances * (value_dot - delta)).astype(bf16)
             key_term = dot(score_grad, queries)
             value_term = dot(chances.astype(bf16), grads)
-            sums[pl.ds(base, 256), :HD] += key_term[:256]
-            sums[pl.ds(base + 1024, 256), :HD] += key_term[256:]
-            sums[pl.ds(base, 256), HD:] += value_term[:256]
-            sums[pl.ds(base + 1024, 256), HD:] += value_term[256:]
+            for n in range(2 * count):
+                here = pl.ds(window_rows(index + n // 2) + n % 2 * 1024, 256)
+                sums[here, :HD] += key_term[n * 256 : n * 256 + 256]
+                sums[here, HD:] += value_term[n * 256 : n * 256 + 256]
             return total + dot(keys, score_grad, ((0,), (0,)))
 
         total = jnp.zeros((HD, 256), f32)
         last = 4 * x + z
-        total = lax.fori_loop(0, last, lambda i, s: tile(i, s, False), total)
-        total = lax.fori_loop(
-            last, jnp.minimum(last + 2, 16), lambda i, s: tile(i, s, True), total
-        )
+        total = lax.fori_loop(0, last // 4, lambda i, s: tile(4 * i, s, 4), total)
+        total = lax.fori_loop(last // 4 * 2, last // 2, lambda i, s: tile(2 * i, s, 2), total)
+        total = lax.fori_loop(last // 2 * 2, last, lambda i, s: tile(i, s, 1), total)
+        total = tile(last, total, 2, True)
         dq_ref[span, :] = total.T * scale
     dkv_ref[:, :HD] = (sums[:, :HD] * scale).astype(bf16)
     dkv_ref[:, HD:] = sums[:, HD:].astype(bf16)

time: 667 us -> 667 us (level)
  waiting for transfers between devices: 247 us -> 261 us
  Pallas kernels: 127 us -> 114 us
    pallas_call x1, Pallas kernels: 30.8 us -> 22.6 us  [attend(): pl.pallas_call(attend_kernel, out_shape=(shape(1024, HD, f32), shape(1, 1...]
    ppermute x8, waiting for transfers between devices: 13.5 us -> 21.7 us  [swap(): return lax.ppermute(value, axis, [(0, 1), (1, 0)])]
  transfers between devices with their start and end apart: 50 -> 50, of which waited for: 30 -> 30; matrix products, arithmetic and copies ran while one was open for 16% -> 16% of each run, Pallas kernels for 14% -> 12%
where the time goes in v5:
time: 667 us; the launch traced here: 655 us
  waiting for transfers between devices  261 us (39%)
  starting transfers between devices  135 us (20%)
  Pallas kernels  114 us (17%)
  other arithmetic  48.1 us (7%)
  matrix products  42.3 us (6%)
  local copies, waits for them, and re-layouts  39.3 us (6%)
  between operations  15.5 us (2%)
    all_to_all x11, waiting for transfers between devices, exchange(): return lax.all_to_all(value, axes, split_axis=0, concat_axis=0, tiled=True)  161 us
    all_to_all x11, starting transfers between devices, exchange(): return lax.all_to_all(value, axes, split_axis=0, concat_axis=0, tiled=True)  86.8 us
    ppermute x23, waiting for transfers between devices, ahead(): return lax.ppermute(value, axis, [(a, (a + steps) % 4) for a in range(4)])  49 us
    dot_general x16, matrix products, dot(): lax.dot_general(first, second, (dims, ((), ())), preferred_element_type=f32)  42.3 us
    ppermute x23, starting transfers between devices, ahead(): return lax.ppermute(value, axis, [(a, (a + steps) % 4) for a in range(4)])  30.5 us
    pallas_call x1, Pallas kernels, attend_back(): pl.pallas_call(attend_back_kernel, out_shape=(shape(1024, HD, f32), shape...  24 us
    pallas_call x1, Pallas kernels, expert_step(): pl.pallas_call(expert_kernel, grid=(2,), out_shape=(shape(1024, ROW_WIDTH...  23 us
    pallas_call x1, Pallas kernels, attend(): pl.pallas_call(attend_kernel, out_shape=(shape(1024, HD, f32), shape(1, 1...  22.6 us
  transfers between devices with their start and end apart: 50, of which 30 were waited for; matrix products, arithmetic and copies ran while one was open for 16% of the time, Pallas kernels for 12%

profile of v5, /device:TPU:96, one launch (start us, length us, event | category | flops | bytes accessed | tf_op | source)
XLA Modules:
  0.0 655.3 jit_solution(15123839237827070238)
XLA Ops:
  69.2 9.5 %all-to-all-start.1 = ((bf16[64,16,1280]{2,1,0:T(8,128)(2,1)}), bf16[64,16,1280]{2,1,0:T(8,128)(2,1)}, u32[]{:S(2)}, u32[]{:S(2)}) async-start(bf16[64,16,1280]{2,1,0:T(8,128)(2,1)} %bitcast.29), calls=%async_computation.1 | async-start | bytes 5242880 | tf_op jit(solution)/shard_map/all_to_all | solution.py:48
  78.7 11.3 %shard_map.264 = (bf16[1024,2048]{1,0:T(8,128)(2,1)}, f32[1024,256]{1,0:T(8,128)}, bf16[1024,128]{1,0:T(8,128)(2,1)}, bf16[1024,256]{1,0:T(8,128)(2,1)}, f32[16,...) custom-call(s32[17]{0:T(128)} %concatenate.64.place_ref, ...), custom_call_target="tpu_custom_call" | custom-call | flops 49999998976 | bytes 1 | tf_op jit(solution)/shard_map/pallas_call | solution.py:496
  97.5 15.0 %all-to-all-done.1 = bf16[64,16,1280]{2,1,0:T(8,128)(2,1)} async-done(((bf16[64,16,1280]{2,1,0:T(8,128)(2,1)}), bf16[64,16,1280]{2,1,0:T(8,128)(2,1)}, u32[]{:S(2)}, u32[]{:S(2)}) %all-to-all-start.1) | async-done | bytes 2621472 | tf_op jit(solution)/shard_map/all_to_all | solution.py:48
  120.5 7.7 %all-to-all-done.2 = f32[16,16,128]{2,1,0:T(8,128)S(1)} async-done(((f32[16,16,128]{2,1,0:T(8,128)}), f32[16,16,128]{2,1,0:T(8,128)S(1)}, u32[]{:S(2)}, u32[]{:S(2)}) %all-to-all-start.2) | async-done | bytes 131104 | tf_op jit(solution)/shard_map/all_to_all | solution.py:48
  139.2 22.6 %shard_map.266 = (f32[1024,128]{1,0:T(8,128)}, f32[1,1024]{1,0:T(1,128)}, bf16[8192,256]{1,0:T(8,128)(2,1)}) custom-call(s32[1]{0:T(128)} %bitcast.z_ref, bf16[1024,128]{1,0:T(8,128)(2,1)} %get-tuple-element.113.q_ref.raw_ref, f32[1,1024]{1,0:T(1,128)} %bitcast.227, bf16[8192,256]{1,0:T(8,128)(2,1)} %all-gather.5.cloned.1.call-done.raw_ref, ...), custom_call_target="tpu_custom_call" | custom-call | flops 1 | bytes 1 | tf_op jit(solution)/shard_map/pallas_call | solution.py:622
  175.1 12.1 %collective-permute-done.22.other_ref = bf16[1024,1280]{1,0:T(8,128)(2,1)} collective-permute-done((bf16[1024,1280]{1,0:T(8,128)(2,1)}, bf16[1024,1280]{1,0:T(8,128)(2,1)}, u32[]{:S(2)}, u32[]{:S(2)}) %collective-permute-start.22) | collective-permute-done | bytes 2621472 | tf_op jit(solution)/shard_map/ppermute | solution.py:67
  194.0 8.2 %collective-permute-done.23 = bf16[128,2048]{1,0:T(8,128)(2,1)S(1)} collective-permute-done((bf16[128,2048]{1,0:T(8,128)(2,1)S(1)}, bf16[128,2048]{1,0:T(8,128)(2,1)S(1)}, u32[]{:S(2)}, u32[]{:S(2)}) %collective-permute-start.23) | collective-permute-done | bytes 524320 | tf_op jit(solution)/shard_map/ppermute | solution.py:94
  207.6 10.3 %all-to-all-start.4 = ((bf16[64,16,2560]{2,1,0:T(8,128)(2,1)}), bf16[64,16,2560]{2,1,0:T(8,128)(2,1)}, u32[]{:S(2)}, u32[]{:S(2)}) async-start(bf16[64,16,2560]{2,1,0:T(8,128)(2,1)} %bitcast.181), calls=%async_computation.4 | async-start | bytes 10485760 | tf_op jit(solution)/shard_map/all_to_all | solution.py:48
  218.4 7.4 %shard_map.267 = (bf16[1280,2048]{1,0:T(8,128)(2,1)}, f32[1280,512]{1,0:T(8,128)}) custom-call(s32[1]{0:T(128)} %bitcast.60.side_ref, bf16[1024,1280]{1,0:T(8,128)(2,1)} %bitcast.30.own_ref, bf16[1024,1280]{1,0:T(8,128)(2,1)} %collective-permute-done.22.other_ref, bf16[512,2048]{1,0:T(8,128)(2,1)} %bitcast.182), custom_call_target="tpu_custom_call" | custom-call | flops 1 | bytes 1 | tf_op jit(solution)/shard_map/pallas_call | solution.py:546
  233.0 50.0 %all-to-all-done.4 = bf16[64,16,2560]{2,1,0:T(8,128)(2,1)} async-done(((bf16[64,16,2560]{2,1,0:T(8,128)(2,1)}), bf16[64,16,2560]{2,1,0:T(8,128)(2,1)}, u32[]{:S(2)}, u32[]{:S(2)}) %all-to-all-start.4) | async-done | bytes 5242912 | tf_op jit(solution)/shard_map/all_to_all | solution.py:48
  283.0 23.0 %shard_map.268 = (bf16[1024,2560]{1,0:T(8,128)(2,1)}, bf16[1280,2048]{1,0:T(8,128)(2,1)}, bf16[1280,512]{1,0:T(8,128)(2,1)}, bf16[1280,512]{1,0:T(8,128)(2,1)}, ...) custom-call(s32[1]{0:T(128)} %bitcast.50.place_ref, bf16[1024,2560]{1,0:T(8,128)(2,1)} %bitcast.55.rows_ref, ...), custom_call_target="tpu_custom_call" | custom-call | flops 1 | bytes 1 | tf_op jit(solution)/shard_map/pallas_call | solution.py:563
  306.0 14.7 %all-to-all-start.5 = ((bf16[64,16,2560]{2,1,0:T(8,128)(2,1)}), bf16[64,16,2560]{2,1,0:T(8,128)(2,1)}, u32[]{:S(2)}, u32[]{:S(2)}) async-start(bf16[64,16,2560]{2,1,0:T(8,128)(2,1)} %bitcast.186), calls=%async_computation.5 | async-start | bytes 10485760 | tf_op jit(solution)/shard_map/all_to_all | solution.py:48
  340.9 44.9 %all-to-all-done.5 = bf16[64,16,2560]{2,1,0:T(8,128)(2,1)} async-done(((bf16[64,16,2560]{2,1,0:T(8,128)(2,1)}), bf16[64,16,2560]{2,1,0:T(8,128)(2,1)}, u32[]{:S(2)}, u32[]{:S(2)}) %all-to-all-start.5) | async-done | bytes 5242912 | tf_op jit(solution)/shard_map/all_to_all | solution.py:48
  396.3 9.7 %collective-permute-done.24 = bf16[128,2048]{1,0:T(8,128)(2,1)S(1)} collective-permute-done((bf16[128,2048]{1,0:T(8,128)(2,1)S(1)}, bf16[128,2048]{1,0:T(8,128)(2,1)S(1)}, u32[]{:S(2)}, u32[]{:S(2)}) %collective-permute-start.24) | collective-permute-done | bytes 524320 | tf_op jit(solution)/shard_map/ppermute | solution.py:94
  415.5 8.3 %shard_map.269 = bf16[1024,2560]{1,0:T(8,128)(2,1)} custom-call(bf16[1280,512]{1,0:T(8,128)(2,1)} %get-tuple-element.139.hidden_ref, bf16[512,2048]{1,0:T(8,128)(2,1)} %bitcast.183), custom_call_target="tpu_custom_call" | custom-call | flops 1 | bytes 1 | tf_op jit(solution)/shard_map/pallas_call | solution.py:596
  424.0 14.5 %all-to-all-start.7 = ((bf16[64,16,2560]{2,1,0:T(8,128)(2,1)}), bf16[64,16,2560]{2,1,0:T(8,128)(2,1)}, u32[]{:S(2)}, u32[]{:S(2)}) async-start(bf16[64,16,2560]{2,1,0:T(8,128)(2,1)} %bitcast.180), calls=%async_computation.7 | async-start | bytes 10485760 | tf_op jit(solution)/shard_map/all_to_all | solution.py:48
  441.9 24.0 %shard_map.270 = (f32[1024,128]{1,0:T(8,128)}, bf16[8192,256]{1,0:T(8,128)(2,1)}) custom-call(s32[1]{0:T(128)} %bitcast.z_ref, bf16[1024,128]{1,0:T(8,128)(2,1)} %get-tuple-element.113.q_ref.raw_ref, f32[1,1024]{1,0:T(1,128)} %bitcast.228, bf16[1024,128]{1,0:T(8,128)(2,1)} %multiply_convert_fusion.1.q_ref, bf16[1024,128]{1,0:T(8,128)(2,1)} %bitcast.195, ...), custom_call_target="tpu_custom_call" | custom-call | flops 1 | bytes 1 | tf_op jit(solution)/shard_map/pallas_call | solution.py:633
  465.9 37.8 %all-to-all-done.7 = bf16[64,16,2560]{2,1,0:T(8,128)(2,1)} async-done(((bf16[64,16,2560]{2,1,0:T(8,128)(2,1)}), bf16[64,16,2560]{2,1,0:T(8,128)(2,1)}, u32[]{:S(2)}, u32[]{:S(2)}) %all-to-all-start.7) | async-done | bytes 5242912 | tf_op jit(solution)/shard_map/all_to_all | solution.py:48
  505.3 7.1 %all-to-all-start.8 = ((bf16[8,128,512]{2,1,0:T(8,128)(2,1)}), bf16[8,128,512]{2,1,0:T(8,128)(2,1)}, u32[]{:S(2)}, u32[]{:S(2)}) async-start(bf16[8,128,512]{2,1,0:T(8,128)(2,1)} %bitcast.80), calls=%async_computation.8 | async-start | bytes 2097152 | tf_op jit(solution)/shard_map/all_to_all | solution.py:48
  514.4 10.0 %reduce-scatter.3.cloned.1.call-done = bf16[1024,256]{1,0:T(8,128)(2,1)} async-done(((bf16[8192,256]{1,0:T(8,128)(2,1)}), bf16[1024,256]{1,0:T(8,128)(2,1)}) %reduce-scatter.3.cloned.1.call-update) | async-done | bytes 524304 | tf_op jit(solution)/shard_map/reduce_scatter | solution.py:832
  546.8 9.9 %shard_map.272 = (bf16[1024,2048]{1,0:T(8,128)(2,1)}, bf16[2560,512]{1,0:T(8,128)(2,1)}) custom-call(s32[1]{0:T(128)} %bitcast.17.place_ref, bf16[1024,384]{1,0:T(8,128)(2,1)} %pad_maximum_fusion.4.raw_ref, bf16[1024,2048]{1,0:T(8,128)(2,1)} %get-tuple-element.159.normed_ref, bf16[2048,384]{1,0:T(8,128)(2,1)} %get-tuple-element.160.weight_ref, ...), custom_call_target="tpu_custom_call" | custom-call | flops 1 | bytes 1 | tf_op jit(solution)/shard_map/pallas_call | solution.py:518
  561.3 12.8 %collective-permute-done.27 = bf16[256,1024]{1,0:T(8,128)(2,1)S(1)} collective-permute-done((bf16[256,1024]{1,0:T(8,128)(2,1)S(1)}, bf16[256,1024]{1,0:T(8,128)(2,1)S(1)}, u32[]{:S(2)}, u32[]{:S(2)}) %collective-permute-start.27) | collective-permute-done | bytes 524320 | tf_op jit(solution)/shard_map/ppermute | solution.py:55
  587.9 15.8 %collective-permute-done.28 = bf16[256,2048]{1,0:T(8,128)(2,1)S(1)} collective-permute-done((bf16[256,2048]{1,0:T(8,128)(2,1)}, bf16[256,2048]{1,0:T(8,128)(2,1)S(1)}, u32[]{:S(2)}, u32[]{:S(2)}) %collective-permute-start.28) | collective-permute-done | bytes 1048608 | tf_op jit(solution)/shard_map/ppermute | solution.py:55
  626.1 8.5 %collective-permute-done.31 = bf16[128,2048]{1,0:T(8,128)(2,1)S(1)} collective-permute-done((bf16[128,2048]{1,0:T(8,128)(2,1)S(1)}, bf16[128,2048]{1,0:T(8,128)(2,1)S(1)}, u32[]{:S(2)}, u32[]{:S(2)}) %collective-permute-start.31) | collective-permute-done | bytes 524320 | tf_op jit(solution)/shard_map/ppermute | solution.py:67
  (351 shorter events, 244.8 us)
Async XLA Ops:
  7.2 82.8 %all-gather.3.cloned.1.call-start = ((), (), s32[]{:S(2)}) async-start(), calls=%async_computation.13 | async-start | bytes 4259840 | tf_op jit(solution)/shard_map/all_gather | solution.py:701
  7.9 27.4 %collective-permute-start = (bf16[128,2048]{1,0:T(8,128)(2,1)}, bf16[128,2048]{1,0:T(8,128)(2,1)}, u32[]{:S(2)}, u32[]{:S(2)}) collective-permute-start(bf16[128,2048]{1,0:T(8,128)(2,1)} %refs_0_), channel_id=1, source_target_pairs={{0,4},{4,0},{1,5},{5,1},{2,6},{6,2},{3,7},{7,3},{8,12},{12,8},{9,1... | collective-permute-start | bytes 1572872 | tf_op jit(solution)/shard_map/ppermute | solution.py:67
  11.2 24.9 %collective-permute-start.1 = (bf16[128,2048]{1,0:T(8,128)(2,1)}, bf16[128,2048]{1,0:T(8,128)(2,1)}, u32[]{:S(2)}, u32[]{:S(2)}) collective-permute-start(bf16[128,2048]{1,0:T(8,128)(2,1)} %refs_0_), channel_id=1, source_target_pairs={{0,32},{32,64},{64,96},{96,0},{1,33},{33,65},{65,97},{97,1},{2,34}... | collective-permute-start | bytes 1572872 | tf_op jit(solution)/shard_map/ppermute | solution.py:55
  12.7 28.3 %collective-permute-start.4 = (bf16[128,2048]{1,0:T(8,128)(2,1)}, bf16[128,2048]{1,0:T(8,128)(2,1)}, u32[]{:S(2)}, u32[]{:S(2)}) collective-permute-start(bf16[128,2048]{1,0:T(8,128)(2,1)} %refs_0_), channel_id=1, source_target_pairs={{0,96},{32,0},{64,32},{96,64},{1,97},{33,1},{65,33},{97,65},{2,98}... | collective-permute-start | bytes 1572872 | tf_op jit(solution)/shard_map/ppermute | solution.py:55
  35.3 17.9 %collective-permute-start.2 = (bf16[128,2048]{1,0:T(8,128)(2,1)}, bf16[128,2048]{1,0:T(8,128)(2,1)S(1)}, u32[]{:S(2)}, u32[]{:S(2)}) collective-permute-start(bf16[128,2048]{1,0:T(8,128)(2,1)} %collective-permute-done.refs_1_), channel_id=1, source_target_pairs={{0,32},{32,64},{64,96},{96,0},{1,33},{33,65},{65,97},{97,1},{2,34}... | collective-permute-start | bytes 1572872 | tf_op jit(solution)/shard_map/ppermute | solution.py:55
  36.1 17.2 %collective-permute-start.7 = (bf16[128,2048]{1,0:T(8,128)(2,1)}, bf16[128,2048]{1,0:T(8,128)(2,1)}, u32[]{:S(2)}, u32[]{:S(2)}) collective-permute-start(bf16[128,2048]{1,0:T(8,128)(2,1)} %collective-permute-done.refs_1_), channel_id=1, source_target_pairs={{0,96},{32,0},{64,32},{96,64},{1,97},{33,1},{65,33},{97,65},{2,98}... | collective-permute-start | bytes 1572872 | tf_op jit(solution)/shard_map/ppermute | solution.py:55
  41.0 18.9 %collective-permute-start.3 = (bf16[64,2048]{1,0:T(8,128)(2,1)S(1)}, bf16[64,2048]{1,0:T(8,128)(2,1)S(1)}, u32[]{:S(2)}, u32[]{:S(2)}) collective-permute-start(bf16[64,2048]{1,0:T(8,128)(2,1)S(1)} %slice.190), channel_id=1, source_target_pairs={{0,32},{32,64},{64,96},{96,0},{1,33},{33,65},{65,97},{97,1},{2,34}... | collective-permute-start | bytes 786440 | tf_op jit(solution)/shard_map/ppermute | solution.py:55
  69.2 43.3 %all-to-all-start.1 = ((bf16[64,16,1280]{2,1,0:T(8,128)(2,1)}), bf16[64,16,1280]{2,1,0:T(8,128)(2,1)}, u32[]{:S(2)}, u32[]{:S(2)}) async-start(bf16[64,16,1280]{2,1,0:T(8,128)(2,1)} %bitcast.29), calls=%async_computation.1 | async-start | bytes 5242880 | tf_op jit(solution)/shard_map/all_to_all | solution.py:48
  78.7 60.6 %all-gather.5.cloned.1.call-start = ((), (), s32[]{:S(2)}) async-start(), calls=%async_computation.14 | async-start | bytes 4718592 | tf_op jit(solution)/shard_map/all_gather | solution.py:746
  128.3 59.0 %collective-permute-start.22 = (bf16[1024,1280]{1,0:T(8,128)(2,1)}, bf16[1024,1280]{1,0:T(8,128)(2,1)}, u32[]{:S(2)}, u32[]{:S(2)}) collective-permute-start(bf16[1024,1280]{1,0:T(8,128)(2,1)} %bitcast.30.own_ref), channel_id=1, source_target_pairs={{0,1},{1,0},{2,3},{3,2},{4,5},{5,4},{6,7},{7,6},{8,9},{9,8},{10,11... | collective-permute-start | bytes 7864328 | tf_op jit(solution)/shard_map/ppermute | solution.py:67
  167.1 21.0 %all-to-all-start.3 = ((bf16[8,128,128]{1,2,0:T(8,128)(2,1)}), bf16[8,128,128]{1,2,0:T(8,128)(2,1)S(1)}, u32[]{:S(2)}, u32[]{:S(2)}) async-start(bf16[8,128,128]{1,2,0:T(8,128)(2,1)} %copy.72), calls=%async_computation.3 | async-start | bytes 524288 | tf_op jit(solution)/shard_map/all_to_all | solution.py:48
  207.6 75.5 %all-to-all-start.4 = ((bf16[64,16,2560]{2,1,0:T(8,128)(2,1)}), bf16[64,16,2560]{2,1,0:T(8,128)(2,1)}, u32[]{:S(2)}, u32[]{:S(2)}) async-start(bf16[64,16,2560]{2,1,0:T(8,128)(2,1)} %bitcast.181), calls=%async_computation.4 | async-start | bytes 10485760 | tf_op jit(solution)/shard_map/all_to_all | solution.py:48
  306.0 79.7 %all-to-all-start.5 = ((bf16[64,16,2560]{2,1,0:T(8,128)(2,1)}), bf16[64,16,2560]{2,1,0:T(8,128)(2,1)}, u32[]{:S(2)}, u32[]{:S(2)}) async-start(bf16[64,16,2560]{2,1,0:T(8,128)(2,1)} %bitcast.186), calls=%async_computation.5 | async-start | bytes 10485760 | tf_op jit(solution)/shard_map/all_to_all | solution.py:48
  424.0 79.8 %all-to-all-start.7 = ((bf16[64,16,2560]{2,1,0:T(8,128)(2,1)}), bf16[64,16,2560]{2,1,0:T(8,128)(2,1)}, u32[]{:S(2)}, u32[]{:S(2)}) async-start(bf16[64,16,2560]{2,1,0:T(8,128)(2,1)} %bitcast.180), calls=%async_computation.7 | async-start | bytes 10485760 | tf_op jit(solution)/shard_map/all_to_all | solution.py:48
  438.5 85.9 %reduce-scatter.3.cloned.1.call-start = ((), (), s32[]{:S(2)}) async-start(), calls=%async_computation.15 | async-start | bytes 4718592 | tf_op jit(solution)/shard_map/reduce_scatter | solution.py:832
  505.3 25.1 %all-to-all-start.8 = ((bf16[8,128,512]{2,1,0:T(8,128)(2,1)}), bf16[8,128,512]{2,1,0:T(8,128)(2,1)}, u32[]{:S(2)}, u32[]{:S(2)}) async-start(bf16[8,128,512]{2,1,0:T(8,128)(2,1)} %bitcast.80), calls=%async_computation.8 | async-start | bytes 2097152 | tf_op jit(solution)/shard_map/all_to_all | solution.py:48
  536.0 74.3 %reduce-scatter.5.cloned.1.call-start = ((), (), s32[]{:S(2)}) async-start(), calls=%async_computation.16 | async-start | bytes 2949120 | tf_op jit(solution)/shard_map/reduce_scatter | solution.py:883
  577.2 26.6 %collective-permute-start.28 = (bf16[256,2048]{1,0:T(8,128)(2,1)}, bf16[256,2048]{1,0:T(8,128)(2,1)S(1)}, u32[]{:S(2)}, u32[]{:S(2)}) collective-permute-start(bf16[256,2048]{1,0:T(8,128)(2,1)} %pad_maximum_fusion.2), channel_id=1, source_target_pairs={{0,32},{32,64},{64,96},{96,0},{1,33},{33,65},{65,97},{97,1},{2,34}... | collective-permute-start | bytes 3145736 | tf_op jit(solution)/shard_map/ppermute | solution.py:55
  578.2 26.0 %collective-permute-start.30 = (bf16[256,2048]{1,0:T(8,128)(2,1)}, bf16[256,2048]{1,0:T(8,128)(2,1)S(1)}, u32[]{:S(2)}, u32[]{:S(2)}) collective-permute-start(bf16[256,2048]{1,0:T(8,128)(2,1)} %pad_maximum_fusion.3), channel_id=1, source_target_pairs={{0,96},{32,0},{64,32},{96,64},{1,97},{33,1},{65,33},{97,65},{2,98}... | collective-permute-start | bytes 3145736 | tf_op jit(solution)/shard_map/ppermute | solution.py:55
  587.6 36.2 %collective-permute-start.25 = (bf16[128,2048]{1,0:T(8,128)(2,1)}, bf16[128,2048]{1,0:T(8,128)(2,1)}, u32[]{:S(2)}, u32[]{:S(2)}) collective-permute-start(bf16[128,2048]{1,0:T(8,128)(2,1)} %fusion.10), channel_id=1, source_target_pairs={{0,1},{1,0},{2,3},{3,2},{4,5},{5,4},{6,7},{7,6},{8,9},{9,8},{10,11... | collective-permute-start | bytes 1572872 | tf_op jit(solution)/shard_map/ppermute | solution.py:94
  606.8 27.8 %collective-permute-start.32 = (bf16[128,2048]{1,0:T(8,128)(2,1)}, bf16[128,2048]{1,0:T(8,128)(2,1)S(1)}, u32[]{:S(2)}, u32[]{:S(2)}) collective-permute-start(bf16[128,2048]{1,0:T(8,128)(2,1)} %get-tuple-element.167), channel_id=1, source_target_pairs={{0,4},{4,0},{1,5},{5,1},{2,6},{6,2},{3,7},{7,3},{8,12},{12,8},{9,1... | collective-permute-start | bytes 1572872 | tf_op jit(solution)/shard_map/ppermute | solution.py:67
  608.2 27.1 %collective-permute-start.33 = (bf16[128,2048]{1,0:T(8,128)(2,1)}, bf16[128,2048]{1,0:T(8,128)(2,1)S(1)}, u32[]{:S(2)}, u32[]{:S(2)}) collective-permute-start(bf16[128,2048]{1,0:T(8,128)(2,1)} %get-tuple-element.167), channel_id=1, source_target_pairs={{0,5},{1,4},{4,1},{5,0},{2,7},{3,6},{6,3},{7,2},{8,13},{9,12},{12,... | collective-permute-start | bytes 1572872 | tf_op jit(solution)/shard_map/ppermute | solution.py:84
  609.8 24.8 %collective-permute-start.31 = (bf16[128,2048]{1,0:T(8,128)(2,1)S(1)}, bf16[128,2048]{1,0:T(8,128)(2,1)S(1)}, u32[]{:S(2)}, u32[]{:S(2)}) collective-permute-start(bf16[128,2048]{1,0:T(8,128)(2,1)S(1)} %get-tuple-element.168), channel_id=1, source_target_pairs={{0,1},{1,0},{2,3},{3,2},{4,5},{5,4},{6,7},{7,6},{8,9},{9,8},{10,11... | collective-permute-start | bytes 1572872 | tf_op jit(solution)/shard_map/ppermute | solution.py:67
  612.0 24.1 %all-to-all-start.10 = ((bf16[8,32,512]{2,1,0:T(8,128)(2,1)}), bf16[8,32,512]{2,1,0:T(8,128)(2,1)S(1)}, u32[]{:S(2)}, u32[]{:S(2)}) async-start(bf16[8,32,512]{2,1,0:T(8,128)(2,1)} %bitcast.91), calls=%async_computation.12 | async-start | bytes 524288 | tf_op jit(solution)/shard_map/all_to_all | solution.py:48
  (86 other events, 1124.5 us)
Sparse Core Ops, SparseCore 0:
  11.2 77.2 all-gather.2
  90.2 39.6 all-gather.4
  466.1 58.2 reduce-scatter.2
  556.8 32.0 reduce-scatter.4

commit v6 on v5

--- a/solution.py
+++ b/solution.py
@@ -694,9 +694,12 @@
     weights_sent = pack(line, router_weight, query_weight, key_weight, value_weight)
     inputs_pair = swap(inputs, "yh")
     inputs_all = [ring(inputs, "x"), ring(inputs_pair, "x")]
+    near = [inputs_all[0][1], inputs_all[0][3], inputs_all[0][2]]
+    near += [inputs_all[1][1], inputs_all[1][3]]
     inputs_all = [part for i, j in OFFSETS for part in inputs_all[j][i]]
     weights_come = exchange(weights_sent, HEADS)
     weights_all = ring(jnp.stack([weights_come, swap(weights_come, "c")]), "z")
+    near += [weights_all[1], weights_all[3]]
     weights_all = [part for parts in weights_all for part in parts]
     output_all = lax.all_gather(output_weight.T, CTX, axis=0, tiled=True)
 
@@ -715,9 +718,7 @@
 
     cotangent_side = lax.dynamic_slice(cotangent, (0, side * SIDE), (128, SIDE))
     grad_sent = dispatch(main_table, rest_table, cotangent_side)
-    inputs_all, weights_all, grad_sent = lax.optimization_barrier(
-        (inputs_all, weights_all, grad_sent)
-    )
+    near, grad_sent = lax.optimization_barrier((near, grad_sent))
     grad_rows = exchange(grad_sent, CTX)
     chunk = jnp.arange(8, dtype=jnp.int32)
     chunk_start = ((chunk // 2) * 16 + z * 4 + (chunk % 2) * 2 + c) * 128

time: 667 us -> 670 us (level)
    all_gather x1, waiting for transfers between devices: 0.02 us -> 19.7 us  [local(): output_all = lax.all_gather(output_weight.T, CTX, axis=0, tiled=True)]
    all_to_all x11, waiting for transfers between devices: 161 us -> 146 us  [exchange(): return lax.all_to_all(value, axes, split_axis=0, concat_axis=0, tiled=True)]
  transfers between devices with their start and end apart: 50 -> 50, of which waited for: 30 -> 27; matrix products, arithmetic and copies ran while one was open for 16% -> 16% of each run, Pallas kernels for 12% -> 12%
where the time goes in v6:
time: 670 us; the launch traced here: 658 us
  waiting for transfers between devices  261 us (39%)
  starting transfers between devices  136 us (20%)
  Pallas kernels  114 us (17%)
  other arithmetic  48.1 us (7%)
  matrix products  42.3 us (6%)
  local copies, waits for them, and re-layouts  41.5 us (6%)
  between operations  15.4 us (2%)
    all_to_all x11, waiting for transfers between devices, exchange(): return lax.all_to_all(value, axes, split_axis=0, concat_axis=0, tiled=True)  146 us
    all_to_all x11, starting transfers between devices, exchange(): return lax.all_to_all(value, axes, split_axis=0, concat_axis=0, tiled=True)  86.1 us
    ppermute x23, waiting for transfers between devices, ahead(): return lax.ppermute(value, axis, [(a, (a + steps) % 4) for a in range(4)])  43.4 us
    dot_general x16, matrix products, dot(): lax.dot_general(first, second, (dims, ((), ())), preferred_element_type=f32)  42.3 us
    ppermute x23, starting transfers between devices, ahead(): return lax.ppermute(value, axis, [(a, (a + steps) % 4) for a in range(4)])  32 us
    pallas_call x1, Pallas kernels, attend_back(): pl.pallas_call(attend_back_kernel, out_shape=(shape(1024, HD, f32), shape...  24 us
    pallas_call x1, Pallas kernels, expert_step(): pl.pallas_call(expert_kernel, grid=(2,), out_shape=(shape(1024, ROW_WIDTH...  23 us
    pallas_call x1, Pallas kernels, attend(): pl.pallas_call(attend_kernel, out_shape=(shape(1024, HD, f32), shape(1, 1...  22.6 us
  transfers between devices with their start and end apart: 50, of which 27 were waited for; matrix products, arithmetic and copies ran while one was open for 16% of the time, Pallas kernels for 12%

profile of v6, /device:TPU:96, one launch (start us, length us, event | category | flops | bytes accessed | tf_op | source)
XLA Modules:
  0.0 658.3 jit_solution(8790843223956179742)
XLA Ops:
  65.8 7.9 %all-to-all-start.1 = ((bf16[64,16,1280]{2,1,0:T(8,128)(2,1)}), bf16[64,16,1280]{2,1,0:T(8,128)(2,1)}, u32[]{:S(2)}, u32[]{:S(2)}) async-start(bf16[64,16,1280]{2,1,0:T(8,128)(2,1)} %bitcast.29), calls=%async_computation.1 | async-start | bytes 5242880 | tf_op jit(solution)/shard_map/all_to_all | solution.py:48
  73.9 11.4 %shard_map.264 = (bf16[1024,2048]{1,0:T(8,128)(2,1)}, f32[1024,256]{1,0:T(8,128)}, bf16[1024,128]{1,0:T(8,128)(2,1)}, bf16[1024,256]{1,0:T(8,128)(2,1)}, f32[16,...) custom-call(s32[17]{0:T(128)} %concatenate.64.place_ref, ...), custom_call_target="tpu_custom_call" | custom-call | flops 49999998976 | bytes 1 | tf_op jit(solution)/shard_map/pallas_call | solution.py:496
  85.2 19.7 %all-gather.3.cloned.1.call-done = bf16[2048,1024]{1,0:T(8,128)(2,1)} async-done(((bf16[32,1024]{1,0:T(8,128)(2,1)}), bf16[2048,1024]{1,0:T(8,128)(2,1)}) %all-gather.3.cloned.1.call-update) | async-done | bytes 4194320 | tf_op jit(solution)/shard_map/all_gather | solution.py:704
  120.8 7.7 %all-to-all-done.2 = f32[16,16,128]{2,1,0:T(8,128)S(1)} async-done(((f32[16,16,128]{2,1,0:T(8,128)}), f32[16,16,128]{2,1,0:T(8,128)S(1)}, u32[]{:S(2)}, u32[]{:S(2)}) %all-to-all-start.2) | async-done | bytes 131104 | tf_op jit(solution)/shard_map/all_to_all | solution.py:48
  141.9 22.6 %shard_map.266 = (f32[1024,128]{1,0:T(8,128)}, f32[1,1024]{1,0:T(1,128)}, bf16[8192,256]{1,0:T(8,128)(2,1)}) custom-call(s32[1]{0:T(128)} %bitcast.z_ref, bf16[1024,128]{1,0:T(8,128)(2,1)} %get-tuple-element.83.q_ref.raw_ref, f32[1,1024]{1,0:T(1,128)} %bitcast.227, bf16[8192,256]{1,0:T(8,128)(2,1)} %all-gather.5.cloned.1.call-done.raw_ref, ...), custom_call_target="tpu_custom_call" | custom-call | flops 1 | bytes 1 | tf_op jit(solution)/shard_map/pallas_call | solution.py:622
  177.5 11.5 %collective-permute-done.22.other_ref = bf16[1024,1280]{1,0:T(8,128)(2,1)} collective-permute-done((bf16[1024,1280]{1,0:T(8,128)(2,1)}, bf16[1024,1280]{1,0:T(8,128)(2,1)}, u32[]{:S(2)}, u32[]{:S(2)}) %collective-permute-start.22) | collective-permute-done | bytes 2621472 | tf_op jit(solution)/shard_map/ppermute | solution.py:67
  196.1 9.4 %collective-permute-done.23 = bf16[128,2048]{1,0:T(8,128)(2,1)S(1)} collective-permute-done((bf16[128,2048]{1,0:T(8,128)(2,1)S(1)}, bf16[128,2048]{1,0:T(8,128)(2,1)S(1)}, u32[]{:S(2)}, u32[]{:S(2)}) %collective-permute-start.23) | collective-permute-done | bytes 524320 | tf_op jit(solution)/shard_map/ppermute | solution.py:94
  210.9 9.8 %all-to-all-start.4 = ((bf16[64,16,2560]{2,1,0:T(8,128)(2,1)}), bf16[64,16,2560]{2,1,0:T(8,128)(2,1)}, u32[]{:S(2)}, u32[]{:S(2)}) async-start(bf16[64,16,2560]{2,1,0:T(8,128)(2,1)} %bitcast.181), calls=%async_computation.4 | async-start | bytes 10485760 | tf_op jit(solution)/shard_map/all_to_all | solution.py:48
  221.3 7.4 %shard_map.267 = (bf16[1280,2048]{1,0:T(8,128)(2,1)}, f32[1280,512]{1,0:T(8,128)}) custom-call(s32[1]{0:T(128)} %bitcast.60.side_ref, bf16[1024,1280]{1,0:T(8,128)(2,1)} %bitcast.30.own_ref, bf16[1024,1280]{1,0:T(8,128)(2,1)} %collective-permute-done.22.other_ref, bf16[512,2048]{1,0:T(8,128)(2,1)} %bitcast.182), custom_call_target="tpu_custom_call" | custom-call | flops 1 | bytes 1 | tf_op jit(solution)/shard_map/pallas_call | solution.py:546
  235.9 50.0 %all-to-all-done.4 = bf16[64,16,2560]{2,1,0:T(8,128)(2,1)} async-done(((bf16[64,16,2560]{2,1,0:T(8,128)(2,1)}), bf16[64,16,2560]{2,1,0:T(8,128)(2,1)}, u32[]{:S(2)}, u32[]{:S(2)}) %all-to-all-start.4) | async-done | bytes 5242912 | tf_op jit(solution)/shard_map/all_to_all | solution.py:48
  285.9 23.0 %shard_map.268 = (bf16[1024,2560]{1,0:T(8,128)(2,1)}, bf16[1280,2048]{1,0:T(8,128)(2,1)}, bf16[1280,512]{1,0:T(8,128)(2,1)}, bf16[1280,512]{1,0:T(8,128)(2,1)}, ...) custom-call(s32[1]{0:T(128)} %bitcast.50.place_ref, bf16[1024,2560]{1,0:T(8,128)(2,1)} %bitcast.55.rows_ref, ...), custom_call_target="tpu_custom_call" | custom-call | flops 1 | bytes 1 | tf_op jit(solution)/shard_map/pallas_call | solution.py:563
  308.9 14.8 %all-to-all-start.5 = ((bf16[64,16,2560]{2,1,0:T(8,128)(2,1)}), bf16[64,16,2560]{2,1,0:T(8,128)(2,1)}, u32[]{:S(2)}, u32[]{:S(2)}) async-start(bf16[64,16,2560]{2,1,0:T(8,128)(2,1)} %bitcast.186), calls=%async_computation.5 | async-start | bytes 10485760 | tf_op jit(solution)/shard_map/all_to_all | solution.py:48
  343.8 44.9 %all-to-all-done.5 = bf16[64,16,2560]{2,1,0:T(8,128)(2,1)} async-done(((bf16[64,16,2560]{2,1,0:T(8,128)(2,1)}), bf16[64,16,2560]{2,1,0:T(8,128)(2,1)}, u32[]{:S(2)}, u32[]{:S(2)}) %all-to-all-start.5) | async-done | bytes 5242912 | tf_op jit(solution)/shard_map/all_to_all | solution.py:48
  399.3 9.7 %collective-permute-done.24 = bf16[128,2048]{1,0:T(8,128)(2,1)S(1)} collective-permute-done((bf16[128,2048]{1,0:T(8,128)(2,1)S(1)}, bf16[128,2048]{1,0:T(8,128)(2,1)S(1)}, u32[]{:S(2)}, u32[]{:S(2)}) %collective-permute-start.24) | collective-permute-done | bytes 524320 | tf_op jit(solution)/shard_map/ppermute | solution.py:94
  418.5 8.3 %shard_map.269 = bf16[1024,2560]{1,0:T(8,128)(2,1)} custom-call(bf16[1280,512]{1,0:T(8,128)(2,1)} %get-tuple-element.109.hidden_ref, bf16[512,2048]{1,0:T(8,128)(2,1)} %bitcast.183), custom_call_target="tpu_custom_call" | custom-call | flops 1 | bytes 1 | tf_op jit(solution)/shard_map/pallas_call | solution.py:596
  426.9 14.5 %all-to-all-start.7 = ((bf16[64,16,2560]{2,1,0:T(8,128)(2,1)}), bf16[64,16,2560]{2,1,0:T(8,128)(2,1)}, u32[]{:S(2)}, u32[]{:S(2)}) async-start(bf16[64,16,2560]{2,1,0:T(8,128)(2,1)} %bitcast.180), calls=%async_computation.7 | async-start | bytes 10485760 | tf_op jit(solution)/shard_map/all_to_all | solution.py:48
  444.9 24.0 %shard_map.270 = (f32[1024,128]{1,0:T(8,128)}, bf16[8192,256]{1,0:T(8,128)(2,1)}) custom-call(s32[1]{0:T(128)} %bitcast.z_ref, bf16[1024,128]{1,0:T(8,128)(2,1)} %get-tuple-element.83.q_ref.raw_ref, f32[1,1024]{1,0:T(1,128)} %bitcast.228, bf16[1024,128]{1,0:T(8,128)(2,1)} %multiply_convert_fusion.1.q_ref, bf16[1024,128]{1,0:T(8,128)(2,1)} %bitcast.195, ...), custom_call_target="tpu_custom_call" | custom-call | flops 1 | bytes 1 | tf_op jit(solution)/shard_map/pallas_call | solution.py:633
  468.9 37.8 %all-to-all-done.7 = bf16[64,16,2560]{2,1,0:T(8,128)(2,1)} async-done(((bf16[64,16,2560]{2,1,0:T(8,128)(2,1)}), bf16[64,16,2560]{2,1,0:T(8,128)(2,1)}, u32[]{:S(2)}, u32[]{:S(2)}) %all-to-all-start.7) | async-done | bytes 5242912 | tf_op jit(solution)/shard_map/all_to_all | solution.py:48
  508.3 7.1 %all-to-all-start.8 = ((bf16[8,128,512]{2,1,0:T(8,128)(2,1)}), bf16[8,128,512]{2,1,0:T(8,128)(2,1)}, u32[]{:S(2)}, u32[]{:S(2)}) async-start(bf16[8,128,512]{2,1,0:T(8,128)(2,1)} %bitcast.80), calls=%async_computation.8 | async-start | bytes 2097152 | tf_op jit(solution)/shard_map/all_to_all | solution.py:48
  517.4 10.0 %reduce-scatter.3.cloned.1.call-done = bf16[1024,256]{1,0:T(8,128)(2,1)} async-done(((bf16[8192,256]{1,0:T(8,128)(2,1)}), bf16[1024,256]{1,0:T(8,128)(2,1)}) %reduce-scatter.3.cloned.1.call-update) | async-done | bytes 524304 | tf_op jit(solution)/shard_map/reduce_scatter | solution.py:833
  549.8 9.9 %shard_map.272 = (bf16[1024,2048]{1,0:T(8,128)(2,1)}, bf16[2560,512]{1,0:T(8,128)(2,1)}) custom-call(s32[1]{0:T(128)} %bitcast.17.place_ref, bf16[1024,384]{1,0:T(8,128)(2,1)} %pad_maximum_fusion.4.raw_ref, bf16[1024,2048]{1,0:T(8,128)(2,1)} %get-tuple-element.129.normed_ref, bf16[2048,384]{1,0:T(8,128)(2,1)} %get-tuple-element.130.weight_ref, ...), custom_call_target="tpu_custom_call" | custom-call | flops 1 | bytes 1 | tf_op jit(solution)/shard_map/pallas_call | solution.py:518
  564.3 12.8 %collective-permute-done.27 = bf16[256,1024]{1,0:T(8,128)(2,1)S(1)} collective-permute-done((bf16[256,1024]{1,0:T(8,128)(2,1)S(1)}, bf16[256,1024]{1,0:T(8,128)(2,1)S(1)}, u32[]{:S(2)}, u32[]{:S(2)}) %collective-permute-start.27) | collective-permute-done | bytes 524320 | tf_op jit(solution)/shard_map/ppermute | solution.py:55
  591.0 15.7 %collective-permute-done.28 = bf16[256,2048]{1,0:T(8,128)(2,1)S(1)} collective-permute-done((bf16[256,2048]{1,0:T(8,128)(2,1)}, bf16[256,2048]{1,0:T(8,128)(2,1)S(1)}, u32[]{:S(2)}, u32[]{:S(2)}) %collective-permute-start.28) | collective-permute-done | bytes 1048608 | tf_op jit(solution)/shard_map/ppermute | solution.py:55
  629.1 8.4 %collective-permute-done.31 = bf16[128,2048]{1,0:T(8,128)(2,1)S(1)} collective-permute-done((bf16[128,2048]{1,0:T(8,128)(2,1)S(1)}, bf16[128,2048]{1,0:T(8,128)(2,1)S(1)}, u32[]{:S(2)}, u32[]{:S(2)}) %collective-permute-start.31) | collective-permute-done | bytes 524320 | tf_op jit(solution)/shard_map/ppermute | solution.py:67
  (343 shorter events, 244.5 us)
Async XLA Ops:
  7.2 97.7 %all-gather.3.cloned.1.call-start = ((), (), s32[]{:S(2)}) async-start(), calls=%async_computation.13 | async-start | bytes 4259840 | tf_op jit(solution)/shard_map/all_gather | solution.py:704
  7.9 27.2 %collective-permute-start = (bf16[128,2048]{1,0:T(8,128)(2,1)}, bf16[128,2048]{1,0:T(8,128)(2,1)}, u32[]{:S(2)}, u32[]{:S(2)}) collective-permute-start(bf16[128,2048]{1,0:T(8,128)(2,1)} %refs_0_.1), channel_id=1, source_target_pairs={{0,4},{4,0},{1,5},{5,1},{2,6},{6,2},{3,7},{7,3},{8,12},{12,8},{9,1... | collective-permute-start | bytes 1572872 | tf_op jit(solution)/shard_map/ppermute | solution.py:67
  11.2 24.9 %collective-permute-start.1 = (bf16[128,2048]{1,0:T(8,128)(2,1)}, bf16[128,2048]{1,0:T(8,128)(2,1)}, u32[]{:S(2)}, u32[]{:S(2)}) collective-permute-start(bf16[128,2048]{1,0:T(8,128)(2,1)} %refs_0_.1), channel_id=1, source_target_pairs={{0,32},{32,64},{64,96},{96,0},{1,33},{33,65},{65,97},{97,1},{2,34}... | collective-permute-start | bytes 1572872 | tf_op jit(solution)/shard_map/ppermute | solution.py:55
  12.7 28.4 %collective-permute-start.4 = (bf16[128,2048]{1,0:T(8,128)(2,1)}, bf16[128,2048]{1,0:T(8,128)(2,1)}, u32[]{:S(2)}, u32[]{:S(2)}) collective-permute-start(bf16[128,2048]{1,0:T(8,128)(2,1)} %refs_0_.1), channel_id=1, source_target_pairs={{0,96},{32,0},{64,32},{96,64},{1,97},{33,1},{65,33},{97,65},{2,98}... | collective-permute-start | bytes 1572872 | tf_op jit(solution)/shard_map/ppermute | solution.py:55
  49.5 24.3 %collective-permute-start.11 = (bf16[1,256,512]{2,1,0:T(8,128)(2,1)S(1)}, bf16[1,256,512]{2,1,0:T(8,128)(2,1)}, u32[]{:S(2)}, u32[]{:S(2)}) collective-permute-start(bf16[1,256,512]{2,1,0:T(8,128)(2,1)S(1)} %slice.194), channel_id=1, source_target_pairs={{0,8},{8,16},{16,24},{24,0},{1,9},{9,17},{17,25},{25,1},{2,10},{10... | collective-permute-start | bytes 786440 | tf_op jit(solution)/shard_map/ppermute | solution.py:55
  52.7 21.1 %collective-permute-start.13 = (bf16[1,256,512]{2,1,0:T(8,128)(2,1)}, bf16[1,256,512]{2,1,0:T(8,128)(2,1)}, u32[]{:S(2)}, u32[]{:S(2)}) collective-permute-start(bf16[1,256,512]{2,1,0:T(8,128)(2,1)} %slice.195), channel_id=1, source_target_pairs={{0,24},{8,0},{16,8},{24,16},{1,25},{9,1},{17,9},{25,17},{2,26},{10... | collective-permute-start | bytes 786440 | tf_op jit(solution)/shard_map/ppermute | solution.py:55
  53.6 20.3 %collective-permute-start.6 = (bf16[64,2048]{1,0:T(8,128)(2,1)}, bf16[64,2048]{1,0:T(8,128)(2,1)}, u32[]{:S(2)}, u32[]{:S(2)}) collective-permute-start(bf16[64,2048]{1,0:T(8,128)(2,1)} %slice.192), channel_id=1, source_target_pairs={{0,32},{32,64},{64,96},{96,0},{1,33},{33,65},{65,97},{97,1},{2,34}... | collective-permute-start | bytes 786440 | tf_op jit(solution)/shard_map/ppermute | solution.py:55
  65.8 46.5 %all-to-all-start.1 = ((bf16[64,16,1280]{2,1,0:T(8,128)(2,1)}), bf16[64,16,1280]{2,1,0:T(8,128)(2,1)}, u32[]{:S(2)}, u32[]{:S(2)}) async-start(bf16[64,16,1280]{2,1,0:T(8,128)(2,1)} %bitcast.29), calls=%async_computation.1 | async-start | bytes 5242880 | tf_op jit(solution)/shard_map/all_to_all | solution.py:48
  73.8 68.2 %all-gather.5.cloned.1.call-start = ((), (), s32[]{:S(2)}) async-start(), calls=%async_computation.14 | async-start | bytes 4718592 | tf_op jit(solution)/shard_map/all_gather | solution.py:747
  128.6 60.5 %collective-permute-start.22 = (bf16[1024,1280]{1,0:T(8,128)(2,1)}, bf16[1024,1280]{1,0:T(8,128)(2,1)}, u32[]{:S(2)}, u32[]{:S(2)}) collective-permute-start(bf16[1024,1280]{1,0:T(8,128)(2,1)} %bitcast.30.own_ref), channel_id=1, source_target_pairs={{0,1},{1,0},{2,3},{3,2},{4,5},{5,4},{6,7},{7,6},{8,9},{9,8},{10,11... | collective-permute-start | bytes 7864328 | tf_op jit(solution)/shard_map/ppermute | solution.py:67
  169.9 20.1 %all-to-all-start.3 = ((bf16[8,128,128]{1,2,0:T(8,128)(2,1)}), bf16[8,128,128]{1,2,0:T(8,128)(2,1)S(1)}, u32[]{:S(2)}, u32[]{:S(2)}) async-start(bf16[8,128,128]{1,2,0:T(8,128)(2,1)} %copy.72), calls=%async_computation.3 | async-start | bytes 524288 | tf_op jit(solution)/shard_map/all_to_all | solution.py:48
  210.9 75.0 %all-to-all-start.4 = ((bf16[64,16,2560]{2,1,0:T(8,128)(2,1)}), bf16[64,16,2560]{2,1,0:T(8,128)(2,1)}, u32[]{:S(2)}, u32[]{:S(2)}) async-start(bf16[64,16,2560]{2,1,0:T(8,128)(2,1)} %bitcast.181), calls=%async_computation.4 | async-start | bytes 10485760 | tf_op jit(solution)/shard_map/all_to_all | solution.py:48
  308.9 79.8 %all-to-all-start.5 = ((bf16[64,16,2560]{2,1,0:T(8,128)(2,1)}), bf16[64,16,2560]{2,1,0:T(8,128)(2,1)}, u32[]{:S(2)}, u32[]{:S(2)}) async-start(bf16[64,16,2560]{2,1,0:T(8,128)(2,1)} %bitcast.186), calls=%async_computation.5 | async-start | bytes 10485760 | tf_op jit(solution)/shard_map/all_to_all | solution.py:48
  426.9 79.8 %all-to-all-start.7 = ((bf16[64,16,2560]{2,1,0:T(8,128)(2,1)}), bf16[64,16,2560]{2,1,0:T(8,128)(2,1)}, u32[]{:S(2)}, u32[]{:S(2)}) async-start(bf16[64,16,2560]{2,1,0:T(8,128)(2,1)} %bitcast.180), calls=%async_computation.7 | async-start | bytes 10485760 | tf_op jit(solution)/shard_map/all_to_all | solution.py:48
  441.4 85.9 %reduce-scatter.3.cloned.1.call-start = ((), (), s32[]{:S(2)}) async-start(), calls=%async_computation.15 | async-start | bytes 4718592 | tf_op jit(solution)/shard_map/reduce_scatter | solution.py:833
  508.3 25.1 %all-to-all-start.8 = ((bf16[8,128,512]{2,1,0:T(8,128)(2,1)}), bf16[8,128,512]{2,1,0:T(8,128)(2,1)}, u32[]{:S(2)}, u32[]{:S(2)}) async-start(bf16[8,128,512]{2,1,0:T(8,128)(2,1)} %bitcast.80), calls=%async_computation.8 | async-start | bytes 2097152 | tf_op jit(solution)/shard_map/all_to_all | solution.py:48
  539.0 74.3 %reduce-scatter.5.cloned.1.call-start = ((), (), s32[]{:S(2)}) async-start(), calls=%async_computation.16 | async-start | bytes 2949120 | tf_op jit(solution)/shard_map/reduce_scatter | solution.py:884
  580.2 26.6 %collective-permute-start.28 = (bf16[256,2048]{1,0:T(8,128)(2,1)}, bf16[256,2048]{1,0:T(8,128)(2,1)S(1)}, u32[]{:S(2)}, u32[]{:S(2)}) collective-permute-start(bf16[256,2048]{1,0:T(8,128)(2,1)} %pad_maximum_fusion.2), channel_id=1, source_target_pairs={{0,32},{32,64},{64,96},{96,0},{1,33},{33,65},{65,97},{97,1},{2,34}... | collective-permute-start | bytes 3145736 | tf_op jit(solution)/shard_map/ppermute | solution.py:55
  581.2 25.9 %collective-permute-start.30 = (bf16[256,2048]{1,0:T(8,128)(2,1)}, bf16[256,2048]{1,0:T(8,128)(2,1)S(1)}, u32[]{:S(2)}, u32[]{:S(2)}) collective-permute-start(bf16[256,2048]{1,0:T(8,128)(2,1)} %pad_maximum_fusion.3), channel_id=1, source_target_pairs={{0,96},{32,0},{64,32},{96,64},{1,97},{33,1},{65,33},{97,65},{2,98}... | collective-permute-start | bytes 3145736 | tf_op jit(solution)/shard_map/ppermute | solution.py:55
  590.6 36.2 %collective-permute-start.25 = (bf16[128,2048]{1,0:T(8,128)(2,1)}, bf16[128,2048]{1,0:T(8,128)(2,1)}, u32[]{:S(2)}, u32[]{:S(2)}) collective-permute-start(bf16[128,2048]{1,0:T(8,128)(2,1)} %fusion.10), channel_id=1, source_target_pairs={{0,1},{1,0},{2,3},{3,2},{4,5},{5,4},{6,7},{7,6},{8,9},{9,8},{10,11... | collective-permute-start | bytes 1572872 | tf_op jit(solution)/shard_map/ppermute | solution.py:94
  609.8 27.7 %collective-permute-start.32 = (bf16[128,2048]{1,0:T(8,128)(2,1)}, bf16[128,2048]{1,0:T(8,128)(2,1)S(1)}, u32[]{:S(2)}, u32[]{:S(2)}) collective-permute-start(bf16[128,2048]{1,0:T(8,128)(2,1)} %get-tuple-element.137), channel_id=1, source_target_pairs={{0,4},{4,0},{1,5},{5,1},{2,6},{6,2},{3,7},{7,3},{8,12},{12,8},{9,1... | collective-permute-start | bytes 1572872 | tf_op jit(solution)/shard_map/ppermute | solution.py:67
  611.1 27.1 %collective-permute-start.33 = (bf16[128,2048]{1,0:T(8,128)(2,1)}, bf16[128,2048]{1,0:T(8,128)(2,1)S(1)}, u32[]{:S(2)}, u32[]{:S(2)}) collective-permute-start(bf16[128,2048]{1,0:T(8,128)(2,1)} %get-tuple-element.137), channel_id=1, source_target_pairs={{0,5},{1,4},{4,1},{5,0},{2,7},{3,6},{6,3},{7,2},{8,13},{9,12},{12,... | collective-permute-start | bytes 1572872 | tf_op jit(solution)/shard_map/ppermute | solution.py:84
  612.8 24.6 %collective-permute-start.31 = (bf16[128,2048]{1,0:T(8,128)(2,1)S(1)}, bf16[128,2048]{1,0:T(8,128)(2,1)S(1)}, u32[]{:S(2)}, u32[]{:S(2)}) collective-permute-start(bf16[128,2048]{1,0:T(8,128)(2,1)S(1)} %get-tuple-element.138), channel_id=1, source_target_pairs={{0,1},{1,0},{2,3},{3,2},{4,5},{5,4},{6,7},{7,6},{8,9},{9,8},{10,11... | collective-permute-start | bytes 1572872 | tf_op jit(solution)/shard_map/ppermute | solution.py:67
  614.9 24.1 %all-to-all-start.10 = ((bf16[8,32,512]{2,1,0:T(8,128)(2,1)}), bf16[8,32,512]{2,1,0:T(8,128)(2,1)S(1)}, u32[]{:S(2)}, u32[]{:S(2)}) async-start(bf16[8,32,512]{2,1,0:T(8,128)(2,1)} %bitcast.91), calls=%async_computation.12 | async-start | bytes 524288 | tf_op jit(solution)/shard_map/all_to_all | solution.py:48
  (82 other events, 1116.1 us)
Sparse Core Ops, SparseCore 0:
  11.2 93.6 all-gather.2
  106.6 33.9 all-gather.4
  469.1 58.2 reduce-scatter.2
  559.8 31.9 reduce-scatter.4
